TPU v7x, 256 devices: a whole 4x4x8 slice. The times are simulated.
256 devices in a mesh: orb: 32 (over y, z), slab: 8 (over x, core).
Axes of the slice: x: 4, y: 4, z: 8, core: 2. Of those that a mesh axis runs over, the one named last changes fastest.
Arguments:
- orbitals: bfloat16 [256, 64, 4096], P('orb', 'slab'), may hold values from -6 to 6
- pair_first: int32 [512], P('orb'), may hold values from 0 to 7
- second_owner: int32 [512, 1], replicated, may hold values from 0 to 31; in each aligned block of 16 rows (0 to 15, 16 to 31, ...) at most 2 rows name the same one
- second_local: int32 [512], replicated, may hold values from 0 to 7
- pair_shift: int32 [512, 2], P('orb'), may hold values from -32 to 32
- pair_count: int32 [32], replicated, may hold values from 1 to 16, 256 in all
Outputs:
- exchange_applied: bfloat16 [256, 64, 4096], P('orb', 'slab')
Inputs may be any that keep to these rules, and one draw needn't show every extreme that they name: `second_owner`: in each aligned block of 16 pair slots (those of one orb index) no owner is named by more than 2 slots; some owner is named by exactly 2. `pair_count`: the counts sum to 16 * 32 // 2 and the largest equals 16.
All inputs are finite; a program needn't handle non-finite values.
Results may differ from a plain program's by a relative error of at most 0.0033.
Values may be sent and summed in bfloat16 or wider, within the bound.
No kernel may reach another device: no remote copies, remote signals or barrier semaphores. Data moves between devices by JAX's collectives and lax.ppermute only.
A program may use at most 128 MiB of HBM per device.

v0:
```python
import math

import jax
import jax.numpy as jnp
from jax import lax
from jax.sharding import PartitionSpec as P

BOX = 64


screening = 0.02


def hartley(length):
    line = jnp.arange(length, dtype=jnp.int32)
    product = line[:, None] * line[None, :] % length
    angle = product.astype(jnp.float32) * (2.0 * math.pi / length)
    return jnp.cos(angle) + jnp.sin(angle)


def eigen(length, line):
    angle = (line % length).astype(jnp.float32) * (2.0 * math.pi / length)
    return 2.0 - 2.0 * jnp.cos(angle)


def move_flat(field, shift_x, shift_y):
    flat = jnp.arange(BOX * BOX, dtype=jnp.int32)
    cell_x = flat // BOX
    cell_y = flat % BOX
    rolled = jnp.roll(field, shift_x * BOX + shift_y, axis=1)
    keep = (
        (cell_x - shift_x >= 0)
        & (cell_x - shift_x < BOX)
        & (cell_y - shift_y >= 0)
        & (cell_y - shift_y < BOX)
    )
    return rolled * keep.astype(field.dtype)[None, :]


def plane_forward(field, table, high):
    shaped = field.reshape(field.shape[:-1] + (BOX, BOX))
    shaped = jnp.einsum("pzxy,yb->pzxb", shaped, table, precision=high)
    shaped = jnp.einsum("pzxb,xa->pzab", shaped, table, precision=high)
    return shaped.reshape(field.shape)


def solve_boxes(density):
    parts = lax.axis_size("slab")
    column_count = BOX // parts
    table = hartley(BOX)
    high = lax.Precision.HIGHEST
    spectrum = plane_forward(density, table, high)
    columns = lax.all_to_all(spectrum, "slab", split_axis=2, concat_axis=1, tiled=True)
    columns = jnp.einsum("pzk,zc->pck", columns, table, precision=high)
    line = jnp.arange(BOX, dtype=jnp.int32)
    mine = lax.axis_index("slab") * column_count + jnp.arange(column_count, dtype=jnp.int32)
    lam_full = eigen(BOX, line)
    lam_mine = eigen(BOX, mine)
    plane_lam = (lam_mine[:, None] + lam_full[None, :]).reshape(column_count * BOX)
    kernel = 1.0 / (lam_full[:, None] + plane_lam[None, :] + screening)
    columns = columns * kernel[None]
    columns = jnp.einsum("pck,cz->pzk", columns, table, precision=high) / BOX
    field = lax.all_to_all(columns, "slab", split_axis=1, concat_axis=2, tiled=True)
    field = plane_forward(field, table, high) / (BOX * BOX)
    return field


def pair_terms(first_boxes, second_boxes, shifts, live):
    moved = jax.vmap(move_flat)(second_boxes, shifts[:, 0], shifts[:, 1])
    density = first_boxes.astype(jnp.float32) * moved.astype(jnp.float32)
    potential = solve_boxes(density)
    alive = live.astype(jnp.float32)[:, None, None]
    own_term = alive * potential * moved.astype(jnp.float32)
    carried = potential * first_boxes.astype(jnp.float32)
    other_term = alive * jax.vmap(move_flat)(carried, -shifts[:, 0], -shifts[:, 1])
    return (own_term, other_term.astype(jnp.bfloat16))


def body(orbitals, pair_first, second_owner, second_local, pair_shift, pair_count):
    owners_count = lax.axis_size("orb")
    position = lax.axis_index("orb")
    orb_local = orbitals.shape[0]
    slot_count = pair_first.shape[0]
    capacity = max(2, slot_count // owners_count)
    owners = second_owner[:, 0].reshape(owners_count, slot_count)
    locals_all = second_local.reshape(owners_count, slot_count)
    same = (owners[:, :, None] == owners[:, None, :]).astype(jnp.int32)
    slot_line = jnp.arange(slot_count, dtype=jnp.int32)
    earlier = (slot_line[None, :] < slot_line[:, None]).astype(jnp.int32)
    ranks = jnp.sum(same * earlier[None], axis=2)
    cap_line = jnp.arange(capacity, dtype=jnp.int32)
    hits = (
        (owners == position)[:, :, None] & (ranks[:, :, None] == cap_line[None, None, :])
    ).astype(jnp.int32)
    chosen = jnp.sum(hits * locals_all[:, :, None], axis=1).reshape(owners_count * capacity)
    used = jnp.sum(hits, axis=1).reshape(owners_count * capacity)
    outgoing = orbitals[chosen] * used.astype(jnp.bfloat16)[:, None, None]
    outgoing = outgoing.reshape((owners_count, capacity) + orbitals.shape[1:])
    incoming = lax.all_to_all(outgoing, "orb", split_axis=0, concat_axis=0, tiled=True)
    incoming = incoming.reshape((owners_count * capacity,) + orbitals.shape[1:])
    my_owners = lax.dynamic_index_in_dim(owners, position, 0, keepdims=False)
    my_ranks = lax.dynamic_index_in_dim(ranks, position, 0, keepdims=False)
    slots = my_owners * capacity + my_ranks
    live_count = lax.dynamic_index_in_dim(pair_count, position, 0, keepdims=False)
    live = slot_line < live_count
    first_boxes = orbitals[pair_first]
    second_boxes = incoming[slots]
    returning = jnp.zeros(incoming.shape, jnp.bfloat16)
    orb_line = jnp.arange(orb_local, dtype=jnp.int32)
    high = lax.Precision.HIGHEST
    ret_acc = returning
    own_term, other_term = pair_terms(first_boxes, second_boxes, pair_shift, live)
    picker = (pair_first[:, None] == orb_line[None, :]).astype(jnp.float32)
    own_acc = jnp.einsum("po,pzk->ozk", picker, own_term, precision=high)
    ret_acc = ret_acc.at[slots].add(other_term)
    own_total = own_acc
    returning = ret_acc
    returning = returning.reshape((owners_count, capacity) + orbitals.shape[1:])
    arrived = lax.all_to_all(returning, "orb", split_axis=0, concat_axis=0, tiled=True)
    arrived = arrived.reshape((owners_count * capacity,) + orbitals.shape[1:])
    placer = ((chosen[:, None] == orb_line[None, :]) & (used[:, None] > 0)).astype(jnp.bfloat16)
    own_total = own_total + jnp.einsum(
        "so,szk->ozk", placer, arrived, preferred_element_type=jnp.float32
    )
    return own_total.astype(jnp.bfloat16)


def solution(mesh):
    in_specs = (P("orb", "slab", None), P("orb"), P(), P(), P("orb", None), P())
    out_specs = P("orb", "slab", None)
    return jax.shard_map(body, mesh=mesh, in_specs=in_specs, out_specs=out_specs, check_vma=False)
```

profile of v0, /device:TPU:2, one launch (start us, length us, event | category | flops | bytes accessed | tf_op | source)
XLA Modules:
  0.0 559.1 jit_solution(12351385183274970054)
XLA Ops:
  6.2 4.5 broadcast_multiply_fusion
  10.6 11.7 %all-to-all-start = ((bf16[32,2,8,4096]{3,2,1,0:T(8,128)(2,1)}), bf16[32,2,8,4096]{3,2,1,0:T(8,128)(2,1)}, u32[]{:S(2)}, u32[]{:S(2)}) async-start(bf16[32,2,8,4096]{3,2,1,0:T(8,128)(2,1)} %broadcast_multiply_fusion), calls=%async_computation | async-start | bytes 8388608 | tf_op jit(solution)/shard_map/all_to_all | solution.py:99
  23.3 3.2 reshape.430
  27.0 92.6 %all-to-all-done = bf16[32,2,8,4096]{3,2,1,0:T(8,128)(2,1)} async-done(((bf16[32,2,8,4096]{3,2,1,0:T(8,128)(2,1)}), bf16[32,2,8,4096]{3,2,1,0:T(8,128)(2,1)}, u32[]{:S(2)}, u32[]{:S(2)}) %all-to-all-start) | async-done | bytes 4194336 | tf_op jit(solution)/shard_map/all_to_all | solution.py:99
  119.6 3.8 gather_fusion.2
  126.6 47.6 %while.2 = (s32[]{:T(128)}, bf16[16,8,8192]{2,1,0:T(8,128)(2,1)}, s32[16,3]{0,1:T(4,128)S(1)}, bf16[16,8,4096]{2,1,0:T(8,128)(2,1)S(1)}, s32[]{:T(128)}) while((s32[]{:T(128)}, bf16[16,8,8192]{2,1,0:T(8,128)(2,1)}, s32[16,3]{0,1:T(4,128)S(1)}, bf16[16,8,4096]{2,1,0:T(8,128)(2,1)S(1)}, s32[]{:T(128)}) %tuple.43), condition=%wide.while_cond, body=%wide.while_body.sunk | while | flops 2 | bytes 131189 | solution.py:30
  174.2 3.3 gather.26
  177.5 7.2 %fusion.1 = f32[16,8,64,64]{3,2,1,0:T(8,128)S(1)} fusion(f32[16,8,64,64]{3,2,1,0:T(8,128)} %reshape.430, bf16[16,8,64,64]{3,2,1,0:T(8,128)(2,1)} %gather.26, bf16[16,64,64]{2,1,0:T(8,128)(2,1)S(1)} %fusion.19), kind=kOutput, calls=%fused_computation.11 | convolution fusion | flops 404287488 | bytes 5373952 | tf_op jit(solution)/shard_map/pzxy,yb->pzxb/dot_general | solution.py:42
  184.7 5.5 convolution_bitcast_fusion.1
  190.2 10.6 %copy.87 = f32[16,8,64,64]{0,1,3,2:T(8,128)} copy(f32[16,8,64,64]{3,2,1,0:T(8,128)} %convolution_bitcast_fusion.1) | data formatting | bytes 4194304 | tf_op jit(solution)/shard_map/reshape | solution.py:44
  200.7 11.6 %reshape.480 = f32[8,1,65536]{2,1,0:T(1,128)} reshape(f32[4096,8,16]{2,1,0:T(8,128)} %bitcast.89) | data formatting | bytes 4194304
  212.3 5.1 all-to-all-start.1
  217.9 25.4 %all-to-all-done.1 = f32[8,1,65536]{2,1,0:T(1,128)} async-done(((f32[8,1,65536]{2,1,0:T(1,128)}), f32[8,1,65536]{2,1,0:T(1,128)}, u32[]{:S(2)}, u32[]{:S(2)}) %all-to-all-start.1) | async-done | bytes 2097184 | tf_op jit(solution)/shard_map/all_to_all | solution.py:53
  243.8 8.5 %reduce.6 = f32[8,65536]{1,0:T(8,128)} reduce(f32[8,1,65536]{2,1,0:T(1,128)} %all-to-all-done.1, f32[]{:T(128)} %broadcast.569), dimensions={1}, to_apply=%all_to_all.31.reduce_sub_computation | reduce | bytes 4194308 | tf_op jit(solution)/shard_map/all_to_all | solution.py:53
  252.3 12.8 %reshape.481 = f32[4096,8,16]{2,1,0:T(8,128)} reshape(f32[8,65536]{1,0:T(8,128)} %reduce.6) | data formatting | bytes 4194304
  265.2 22.4 %copy.73 = f32[16,8,8,512]{3,1,2,0:T(8,128)} copy(f32[16,8,8,512]{0,1,3,2:T(8,128)} %bitcast.90) | data formatting | bytes 4194304 | tf_op jit(solution)/shard_map/all_to_all | solution.py:53
  287.6 3.6 fusion.4
  295.9 5.8 %all-to-all-start.2 = ((f32[16,64,512]{2,0,1:T(8,128)}), f32[16,64,512]{2,0,1:T(8,128)}, u32[]{:S(2)}, u32[]{:S(2)}) async-start(f32[16,64,512]{2,0,1:T(8,128)} %copy.74), calls=%async_computation.2 | async-start | bytes 4194304 | tf_op jit(solution)/shard_map/all_to_all | solution.py:63
  304.0 23.5 %all-to-all-done.2 = f32[16,64,512]{2,0,1:T(8,128)} async-done(((f32[16,64,512]{2,0,1:T(8,128)}), f32[16,64,512]{2,0,1:T(8,128)}, u32[]{:S(2)}, u32[]{:S(2)}) %all-to-all-start.2) | async-done | bytes 2097184 | tf_op jit(solution)/shard_map/all_to_all | solution.py:63
  327.6 4.1 copy.92
  331.7 4.4 reshape.380
  336.1 6.7 %fusion.31 = f32[16,8,64,64]{3,2,1,0:T(8,128)S(1)} fusion(f32[16,8,64,64]{3,2,1,0:T(8,128)} %reshape.380), kind=kOutput, calls=%fused_computation.67 | convolution fusion | flops 402714624 | bytes 4194304 | tf_op jit(solution)/shard_map/pzxy,yb->pzxb/dot_general | solution.py:42
  342.9 5.5 convolution_bitcast_fusion
  348.4 4.7 reshape.381
  353.1 3.5 multiply_multiply_fusion
  359.0 58.4 %while.3 = (s32[]{:T(128)}, f32[16,8,8192]{2,1,0:T(8,128)}, s32[16,3]{0,1:T(4,128)S(1)}, f32[16,8,4096]{2,1,0:T(8,128)}, s32[]{:T(128)}) while((s32[]{:T(128)}, f32[16,8,8192]{2,1,0:T(8,128)}, s32[16,3]{0,1:T(4,128)S(1)}, f32[16,8,4096]{2,1,0:T(8,128)}, s32[]{:T(128)}) %tuple.46), condition=%wide.while_cond.1, body=%wide.while_body.1.sunk | while | flops 2 | bytes 263785 | solution.py:30
  421.7 5.1 scatter_fusion
  426.8 8.5 %copy.80 = bf16[32,2,8,4096]{3,1,2,0:T(2,128)(2,1)} copy(bf16[32,2,8,4096]{3,2,1,0:T(8,128)(2,1)} %bitcast.91) | data formatting | bytes 8388608 | tf_op jit(solution)/shard_map/reshape | solution.py:118
  435.3 5.2 all-to-all-start.3
  444.0 93.5 %all-to-all-done.3 = bf16[32,2,8,4096]{3,1,2,0:T(2,128)(2,1)} async-done(((bf16[32,2,8,4096]{3,1,2,0:T(2,128)(2,1)}), bf16[32,2,8,4096]{3,1,2,0:T(2,128)(2,1)}, u32[]{:S(2)}, u32[]{:S(2)}) %all-to-all-start.3) | async-done | bytes 4194336 | tf_op jit(solution)/shard_map/all_to_all | solution.py:119
  537.5 9.9 %copy.81 = bf16[32,2,8,4096]{3,1,0,2:T(2,128)(2,1)} copy(bf16[32,2,8,4096]{3,1,2,0:T(2,128)(2,1)} %all-to-all-done.3) | data formatting | bytes 8388608 | tf_op jit(solution)/shard_map/all_to_all | solution.py:119
  547.4 7.3 %reshape.383 = bf16[64,8,4096]{2,0,1:T(8,128)(2,1)} reshape(bf16[32,2,8,4096]{3,1,0,2:T(2,128)(2,1)} %copy.81) | data formatting | bytes 8388608 | tf_op jit(solution)/shard_map/reshape | solution.py:120
  (168 shorter events, 138.1 us)
Async XLA Ops:
  0.0 3.4 copy-start
  10.6 12.0 %copy-start.5 = (s32[16]{0:T(128)S(1)}, s32[16]{0:T(128)}, u32[]{:S(2)}) copy-start(s32[16]{0:T(128)} %param.7) | copy-start | bytes 196
  10.6 108.9 %all-to-all-start = ((bf16[32,2,8,4096]{3,2,1,0:T(8,128)(2,1)}), bf16[32,2,8,4096]{3,2,1,0:T(8,128)(2,1)}, u32[]{:S(2)}, u32[]{:S(2)}) async-start(bf16[32,2,8,4096]{3,2,1,0:T(8,128)(2,1)} %broadcast_multiply_fusion), calls=%async_computation | async-start | bytes 8388608 | tf_op jit(solution)/shard_map/all_to_all | solution.py:99
  23.3 3.4 copy-start.4
  212.3 30.9 %all-to-all-start.1 = ((f32[8,1,65536]{2,1,0:T(1,128)}), f32[8,1,65536]{2,1,0:T(1,128)}, u32[]{:S(2)}, u32[]{:S(2)}) async-start(f32[8,1,65536]{2,1,0:T(1,128)} %reshape.480), calls=%async_computation.1 | async-start | bytes 4194304 | tf_op jit(solution)/shard_map/all_to_all | solution.py:53
  295.9 5.8 %copy-start.6 = (s32[32]{0:T(128)S(1)}, s32[32]{0:T(128)}, u32[]{:S(2)}) copy-start(s32[32]{0:T(128)} %param.11) | copy-start | bytes 388
  295.9 31.7 %all-to-all-start.2 = ((f32[16,64,512]{2,0,1:T(8,128)}), f32[16,64,512]{2,0,1:T(8,128)}, u32[]{:S(2)}, u32[]{:S(2)}) async-start(f32[16,64,512]{2,0,1:T(8,128)} %copy.74), calls=%async_computation.2 | async-start | bytes 4194304 | tf_op jit(solution)/shard_map/all_to_all | solution.py:63
  435.3 5.6 copy-start.2
  435.3 102.2 %all-to-all-start.3 = ((bf16[32,2,8,4096]{3,1,2,0:T(2,128)(2,1)}), bf16[32,2,8,4096]{3,1,2,0:T(2,128)(2,1)}, u32[]{:S(2)}, u32[]{:S(2)}) async-start(bf16[32,2,8,4096]{3,1,2,0:T(2,128)(2,1)} %copy.80), calls=%async_computation.3 | async-start | bytes 8388608 | tf_op jit(solution)/shard_map/all_to_all | solution.py:119
  547.4 7.3 %copy-start.3 = (f32[8,8,4096]{2,0,1:T(8,128)S(1)}, f32[8,8,4096]{2,0,1:T(8,128)}, u32[]{:S(2)}) copy-start(f32[8,8,4096]{2,0,1:T(8,128)} %fusion.8) | copy-start | bytes 3145732
  547.4 11.2 %copy-start.1 = (bf16[8,8,4096]{2,1,0:T(8,128)(2,1)S(1)}, bf16[8,8,4096]{2,1,0:T(8,128)(2,1)}, u32[]{:S(2)}) copy-start(bf16[8,8,4096]{2,1,0:T(8,128)(2,1)} %param.6) | copy-start | bytes 1572868
where the time goes:
time: 570 us; the launch traced here: 559 us
  waiting for transfers between devices  235 us (41%)
  local copies, waits for them, and re-layouts  226 us (40%)
  matrix products  36.6 us (6%)
  other arithmetic  32.8 us (6%)
  starting transfers between devices  27.9 us (5%)
    gather x96, local copies, waits for them, and re-layouts  106 us
    all_to_all x1, waiting for transfers between devices, body(): lax.all_to_all(returning, 'orb', split_axis=0, concat_axis=0, tiled=True)  93.5 us
    all_to_all x1, waiting for transfers between devices, body(): lax.all_to_all(outgoing, 'orb', split_axis=0, concat_axis=0, tiled=True)  92.6 us
    all_to_all x1, waiting for transfers between devices, solve_boxes(): lax.all_to_all(spectrum, 'slab', split_axis=2, concat_axis=1, tiled=True)  25.4 us
    unnamed x18, local copies, waits for them, and re-layouts  25 us
    all_to_all x1, waiting for transfers between devices, solve_boxes(): lax.all_to_all(columns, 'slab', split_axis=1, concat_axis=2, tiled=True)  23.5 us
    all_to_all x2, local copies, waits for them, and re-layouts, solve_boxes(): lax.all_to_all(spectrum, 'slab', split_axis=2, concat_axis=1, tiled=True)  22.9 us
    reshape x2, local copies, waits for them, and re-layouts, plane_forward(): return shaped.reshape(field.shape)  15.3 us
  transfers between devices with their start and end apart: 4, of which 4 were waited for; matrix products, arithmetic and copies ran while one was open for 2% of the time, Pallas kernels for 0%

commit v1 on v0

v1 whole, which is shorter than its diff:
```python
import math

import jax
import jax.numpy as jnp
import numpy as np
from jax import lax
from jax.experimental import pallas as pl
from jax.experimental.pallas import tpu as pltpu
from jax.sharding import PartitionSpec as P

BOX = 64
ORB_DEV = 8
PAIR_DEV = 16
N_ORB = 32
N_DEV = 256
TILES = 32
LANES = 128
SCREENING = 0.02
PARAMS = pltpu.CompilerParams(vmem_limit_bytes=48 * 1024 * 1024)
WHOLE_V = pl.BlockSpec(memory_space=pltpu.VMEM)
WHOLE_S = pl.BlockSpec(memory_space=pltpu.SMEM)


def hartley_table():
    line = np.arange(BOX)
    angle = (line[:, None] * line[None, :] % BOX) * (2.0 * math.pi / BOX)
    return np.cos(angle) + np.sin(angle)


def halves(table):
    high = table.astype(np.float32).astype(jnp.bfloat16)
    low = (table - high.astype(np.float64)).astype(np.float32).astype(jnp.bfloat16)
    return high, low


def tables():
    high, low = halves(hartley_table())
    zero = np.zeros((BOX, BOX), high.dtype)

    def twice(table):
        return np.block([[table, zero], [zero, table]])

    right = np.block([[twice(high), twice(low)], [twice(high), np.zeros((128, 128), high.dtype)]])
    left = np.concatenate([high, high, low], axis=1)
    lam = 2.0 - 2.0 * np.cos(np.arange(BOX) * (2.0 * math.pi / BOX))
    base = lam[:, None] + np.tile(lam, 2)[None, :] + SCREENING
    lam_a = np.repeat(lam.reshape(2, TILES).T, BOX, axis=1)
    return right, left, base.astype(np.float32), lam_a.astype(np.float32)


def split(field):
    high = field.astype(jnp.bfloat16)
    low = (field - high.astype(jnp.float32)).astype(jnp.bfloat16)
    return high, low


def fast_hartley(parts):
    n = len(parts)
    if n == 1:
        return parts
    if n == 2:
        return [parts[0] + parts[1], parts[0] - parts[1]]
    even, odd = fast_hartley(parts[0::2]), fast_hartley(parts[1::2])
    m = n // 2
    out = [None] * n
    for k in range(m):
        if k == 0 or 4 * k == n:
            turned = odd[k]
        else:
            angle = 2.0 * math.pi * k / n
            turned = odd[k] * math.cos(angle) + odd[m - k] * math.sin(angle)
        out[k] = even[k] + turned
        out[k + m] = even[k] - turned
    return out


def twist(parts, first):
    out = []
    for k in range(TILES):
        mirror = parts[(TILES - k) % TILES]
        angle = 2.0 * math.pi * k / BOX
        if k == 0 or 2 * k == TILES:
            out.append(parts[k])
        else:
            out.append(jnp.where(first, parts[k], parts[k] * math.cos(angle) + mirror * math.sin(angle)))
    return out


def untwist(parts, first):
    out = []
    for k in range(TILES):
        mirror = parts[(TILES - k) % TILES]
        angle = 2.0 * math.pi * k / BOX
        back = 2.0 * math.pi * ((TILES - k) % TILES) / BOX
        if k == 0 or 2 * k == TILES:
            out.append(parts[k])
        else:
            out.append(jnp.where(first, parts[k], parts[k] * math.cos(angle) + mirror * math.sin(back)))
    return out


def spread_kernel(orbitals, pieces):
    for pair in range(ORB_DEV // 2):
        one = orbitals[2 * pair].astype(jnp.float32)
        two = orbitals[2 * pair + 1].astype(jnp.float32)
        for tile in range(TILES):
            at = slice(tile * LANES, (tile + 1) * LANES)
            pieces[tile, 16 * pair : 16 * pair + 16, :] = jnp.concatenate(
                [one[:, at], two[:, at]], axis=0
            ).astype(jnp.bfloat16)


def pick_kernel(count, owner, local, about, pieces, picked, index, held):
    def widen(e, carry):
        block = pieces[e].astype(jnp.float32).reshape(ORB_DEV, 8, LANES)
        held[pl.ds(e * ORB_DEV, ORB_DEV)] = block
        return carry

    lax.fori_loop(0, N_ORB, widen, 0)

    def of_orb(e, base):
        live = count[e]

        def of_slot(k, carry):
            slot = e * PAIR_DEV + k
            first = e * ORB_DEV + about[e * 3 * PAIR_DEV + k]
            second = owner[slot] * ORB_DEV + local[slot]
            picked[base + k] = jnp.concatenate([held[first], held[second]], axis=0).astype(jnp.bfloat16)
            index[base + k] = first
            index[N_DEV + base + k] = second
            index[2 * N_DEV + base + k] = e * 3 * PAIR_DEV + PAIR_DEV + k
            return carry

        lax.fori_loop(0, live, of_slot, 0)
        return base + live

    lax.fori_loop(0, N_ORB, of_orb, 0)


def shifted(source, tile, flat, shift_x, shift_y, lane):
    whole, rest = flat // LANES, flat % LANES
    here = source[(tile - whole + 2 * TILES) % TILES]
    before = source[(tile - whole - 1 + 2 * TILES) % TILES]
    both = jnp.where(lane >= rest, pltpu.roll(here, rest, 1), pltpu.roll(before, rest, 1))
    x = 2 * tile + lane // BOX - shift_x
    y = lane % BOX - shift_y
    keep = (x >= 0) & (x < BOX) & (y >= 0) & (y < BOX)
    return jnp.where(keep, both, 0.0)


def solve_kernel(me, index, about, right, left, base, lam_a, boxes, terms, first_box, moved, field, other):
    at = index[2 * N_DEV + me[0]]
    shift_x, shift_y = about[at], about[at + PAIR_DEV]
    full = BOX * BOX
    ahead = (shift_x * BOX + shift_y + full) % full
    back = (full - ahead) % full
    lane = lax.broadcasted_iota(jnp.int32, (BOX, LANES), 1)
    lane_small = lax.broadcasted_iota(jnp.int32, (8, LANES), 1)
    early = lane_small < BOX
    sign = jnp.where(early, 1.0, -1.0)

    def unpack(tile, carry):
        block = boxes[pl.ds(tile * 8, 8)].astype(jnp.float32)
        first_box[tile] = block[:, :8].reshape(BOX, LANES)
        other[tile] = block[:, 8:].reshape(BOX, LANES)
        return carry

    lax.fori_loop(0, TILES, unpack, 0)

    def along_y(blocks):
        high, low = split(jnp.concatenate(blocks, axis=0))
        product = jnp.dot(
            jnp.concatenate([high, low], axis=1), right[...], preferred_element_type=jnp.float32
        )
        return product[:, :LANES] + product[:, LANES:]

    def forward_y(step, carry):
        blocks = []
        for k in range(4):
            tile = step * 4 + k
            box = shifted(other, tile, ahead, shift_x, shift_y, lane)
            moved[tile] = box
            blocks.append(first_box[tile] * box)
        field[pl.ds(step * 4, 4)] = along_y(blocks).reshape(4, BOX, LANES)
        return carry

    lax.fori_loop(0, TILES // 4, forward_y, 0)

    def forward_x(step, carry):
        rows = pl.ds(pl.multiple_of(step * 8, 8), 8)
        parts = twist(fast_hartley([field[k, rows, :] for k in range(TILES)]), early)
        for k in range(TILES):
            field[k, rows, :] = sign * parts[k] + pltpu.roll(parts[k], BOX, 1)
        return carry

    lax.fori_loop(0, 8, forward_x, 0)

    def along_z(block):
        high, low = split(block)
        return jnp.dot(
            left[...], jnp.concatenate([high, low, high], axis=0), preferred_element_type=jnp.float32
        )

    def screened_z(step, carry):
        block = jnp.concatenate([field[2 * step], field[2 * step + 1]], axis=1)
        under = jnp.concatenate(
            [base[...] + lam_a[pl.ds(2 * step + k, 1), :] for k in range(2)], axis=1
        )
        block = along_z(block) * ((1.0 / BOX**3) / under)
        block = along_z(block)
        field[2 * step] = block[:, :LANES]
        field[2 * step + 1] = block[:, LANES:]
        return carry

    lax.fori_loop(0, TILES // 2, screened_z, 0)

    def inverse_x(step, carry):
        rows = pl.ds(pl.multiple_of(step * 8, 8), 8)
        parts = [field[k, rows, :] for k in range(TILES)]
        parts = [sign * part + pltpu.roll(part, BOX, 1) for part in parts]
        parts = fast_hartley(untwist(parts, early))
        for k in range(TILES):
            field[k, rows, :] = parts[k]
        return carry

    lax.fori_loop(0, 8, inverse_x, 0)

    def inverse_y(step, carry):
        tiles = pl.ds(step * 4, 4)
        potential = along_y([field[step * 4 + k] for k in range(4)]).reshape(4, BOX, LANES)
        other[tiles] = potential * first_box[tiles]
        moved[tiles] = potential * moved[tiles]
        return carry

    lax.fori_loop(0, TILES // 4, inverse_y, 0)

    def pack(tile, carry):
        own = moved[tile].reshape(8, 8, LANES)
        carried = shifted(other, tile, back, -shift_x, -shift_y, lane).reshape(8, 8, LANES)
        terms[pl.ds(tile * 8, 8)] = jnp.concatenate([own, carried], axis=1).astype(jnp.bfloat16)
        return carry

    lax.fori_loop(0, TILES, pack, 0)


def sum_kernel(index, terms, pieces, own, carried):
    own[...] = jnp.zeros_like(own)
    carried[...] = jnp.zeros_like(carried)

    def of_pair(d, carry):
        both = terms[d].astype(jnp.float32)
        first, second = index[d], index[N_DEV + d]
        own[first] = own[first] + both[:8]
        carried[second] = carried[second] + both[8:]
        return carry

    lax.fori_loop(0, N_DEV, of_pair, 0)

    def narrow(e, carry):
        at = pl.ds(e * ORB_DEV, ORB_DEV)
        pieces[e] = (own[at] + carried[at]).reshape(ORB_DEV * 8, LANES).astype(jnp.bfloat16)
        return carry

    lax.fori_loop(0, N_ORB, narrow, 0)


def join_kernel(pieces, result):
    for pair in range(ORB_DEV // 2):
        tiles = [pieces[tile, 16 * pair : 16 * pair + 16, :].astype(jnp.float32) for tile in range(TILES)]
        for side in range(2):
            rows = [tile[8 * side : 8 * side + 8] for tile in tiles]
            result[2 * pair + side] = jnp.concatenate(rows, axis=1).astype(jnp.bfloat16)


def body(orbitals, pair_first, second_owner, second_local, pair_shift, pair_count):
    f32, bf16 = jnp.float32, jnp.bfloat16
    about = jnp.concatenate([pair_first, pair_shift[:, 0], pair_shift[:, 1]])
    about = lax.all_gather(about, "orb", axis=0, tiled=True)
    me = (lax.axis_index("orb") * 8 + lax.axis_index("slab")).reshape(1)
    piece_shape = jax.ShapeDtypeStruct((N_ORB, ORB_DEV * 8, LANES), bf16)
    pair_shape = jax.ShapeDtypeStruct((N_DEV, 16, LANES), bf16)
    pieces = pl.pallas_call(
        spread_kernel, out_shape=piece_shape, in_specs=[WHOLE_V], out_specs=WHOLE_V,
        compiler_params=PARAMS, name="spread",
    )(orbitals)
    pieces = lax.all_to_all(pieces, "orb", split_axis=0, concat_axis=0, tiled=True)
    picked, index = pl.pallas_call(
        pick_kernel,
        out_shape=(pair_shape, jax.ShapeDtypeStruct((3 * N_DEV,), jnp.int32)),
        in_specs=[WHOLE_S] * 4 + [WHOLE_V],
        out_specs=(WHOLE_V, WHOLE_S),
        scratch_shapes=[pltpu.VMEM((N_DEV, 8, LANES), f32)],
        compiler_params=PARAMS, name="pick",
    )(pair_count, second_owner[:, 0], second_local, about, pieces)
    boxes = lax.all_to_all(picked, ("orb", "slab"), split_axis=0, concat_axis=0, tiled=True)
    right, left, base, lam_a = (jnp.asarray(table) for table in tables())
    terms = pl.pallas_call(
        solve_kernel, out_shape=pair_shape,
        in_specs=[WHOLE_S] * 3 + [WHOLE_V] * 5,
        out_specs=WHOLE_V,
        scratch_shapes=[pltpu.VMEM((TILES, BOX, LANES), f32)] * 4,
        compiler_params=PARAMS, name="solve",
    )(me, index, about, right, left, base, lam_a, boxes)
    terms = lax.all_to_all(terms, ("orb", "slab"), split_axis=0, concat_axis=0, tiled=True)
    pieces = pl.pallas_call(
        sum_kernel, out_shape=piece_shape,
        in_specs=[WHOLE_S, WHOLE_V], out_specs=WHOLE_V,
        scratch_shapes=[pltpu.VMEM((N_DEV, 8, LANES), f32)] * 2,
        compiler_params=PARAMS, name="sum",
    )(index, terms)
    pieces = lax.all_to_all(pieces, "orb", split_axis=0, concat_axis=0, tiled=True)
    return pl.pallas_call(
        join_kernel, out_shape=jax.ShapeDtypeStruct((ORB_DEV, 8, BOX * BOX), bf16),
        in_specs=[WHOLE_V], out_specs=WHOLE_V,
        compiler_params=PARAMS, name="join",
    )(pieces)


def solution(mesh):
    in_specs = (P("orb", "slab", None), P("orb"), P(), P(), P("orb", None), P())
    out_specs = P("orb", "slab", None)
    return jax.shard_map(body, mesh=mesh, in_specs=in_specs, out_specs=out_specs, check_vma=False)
```

time: 570 us -> 166 us (0.29); the launches traced: 559 us -> 164 us
  local copies, waits for them, and re-layouts: 226 us -> 3.66 us
  waiting for transfers between devices: 235 us -> 31.2 us
  blocking collectives: 0 us -> 83.8 us
  matrix products: 36.6 us -> 0 us
  other arithmetic: 32.8 us -> 0.16 us
  Pallas kernels: 0 us -> 24.4 us
  starting transfers between devices: 27.9 us -> 20.3 us
    all_to_all x4 -> x2, waiting for transfers between devices: 235 us -> 31.2 us  [the longest x1 31.2 us: body(): lax.all_to_all(picked, ('orb', 'slab'), split_axis=0, concat_axis=0, tile...]
    gather x100 -> x0, local copies, waits for them, and re-layouts: 116 us -> none
    all_to_all x0 -> x2, blocking collectives: none -> 57.9 us  [the longest x1 37.2 us: body(): lax.all_to_all(terms, ('orb', 'slab'), split_axis=0, concat_axis=0, tiled...]
    all_to_all x4 -> x0, local copies, waits for them, and re-layouts: 37 us -> none  [the longest x2 22.9 us: solve_boxes(): lax.all_to_all(spectrum, 'slab', split_axis=2, concat_axis=1, tiled=True)]
    dot_general x8 -> x0, matrix products: 36.6 us -> none  [the longest x2 13.9 us: plane_forward(): shaped = jnp.einsum('pzxy,yb->pzxb', shaped, table, precision=high)]
    reshape x6 -> x0, local copies, waits for them, and re-layouts: 35.6 us -> none  [the longest x2 15.3 us: plane_forward(): return shaped.reshape(field.shape)]
    unnamed x0 -> x1, blocking collectives: none -> 25.9 us
    pallas_call x0 -> x5, Pallas kernels: none -> 24.4 us  [the longest x1 14.7 us: body(): pl.pallas_call(solve_kernel, out_shape=pair_shape, in_specs=[WHOLE_S] * 3...]
  transfers between devices with their start and end apart: 4 -> 2, of which waited for: 4 -> 1; matrix products, arithmetic and copies ran while one was open for 2% -> 0% of each run, Pallas kernels for 0% -> 0%
where the time goes in v1:
time: 166 us; the launch traced here: 164 us
  blocking collectives  83.8 us (50%)
  waiting for transfers between devices  31.2 us (19%)
  Pallas kernels  24.4 us (15%)
  starting transfers between devices  20.3 us (12%)
  local copies, waits for them, and re-layouts  3.66 us (2%)
    all_to_all x1, blocking collectives, body(): lax.all_to_all(terms, ('orb', 'slab'), split_axis=0, concat_axis=0, tiled...  37.2 us
    all_to_all x1, waiting for transfers between devices, body(): lax.all_to_all(picked, ('orb', 'slab'), split_axis=0, concat_axis=0, tile...  31.2 us
    unnamed x1, blocking collectives  25.9 us
    all_to_all x1, blocking collectives, body(): lax.all_to_all(pieces, 'orb', split_axis=0, concat_axis=0, tiled=True)  20.7 us
    pallas_call x1, Pallas kernels, body(): pl.pallas_call(solve_kernel, out_shape=pair_shape, in_specs=[WHOLE_S] * 3...  14.7 us
    all_to_all x1, starting transfers between devices, body(): lax.all_to_all(pieces, 'orb', split_axis=0, concat_axis=0, tiled=True)  11.5 us
    all_to_all x1, starting transfers between devices, body(): lax.all_to_all(picked, ('orb', 'slab'), split_axis=0, concat_axis=0, tile...  8.85 us
    pallas_call x1, Pallas kernels, body(): pl.pallas_call(pick_kernel, out_shape=(pair_shape, jax.ShapeDtypeStruct((...  5.18 us
  transfers between devices with their start and end apart: 2, of which 1 were waited for; matrix products, arithmetic and copies ran while one was open for 0% of the time, Pallas kernels for 0%

profile of v1, /device:TPU:2, one launch (start us, length us, event | category | flops | bytes accessed | tf_op | source)
XLA Modules:
  0.0 164.3 jit_solution(12611869851687507525)
XLA Ops:
  0.0 0.0 copy-start
  0.0 1.0 copy-done
  1.0 0.9 spread.1
  1.9 11.5 %all-to-all-start = ((bf16[32,64,128]{2,1,0:T(8,128)(2,1)}), bf16[32,64,128]{2,1,0:T(8,128)(2,1)S(1)}, u32[]{:S(2)}, u32[]{:S(2)}) async-start(bf16[32,64,128]{2,1,0:T(8,128)(2,1)} %spread.1), calls=%async_computation | async-start | bytes 1048576 | tf_op jit(solution)/shard_map/all_to_all | solution.py:286
  13.4 0.0 copy-start.10
  13.4 0.7 copy-done.10
  14.1 0.6 dynamic-slice
  14.7 0.0 copy-start.8
  15.4 0.0 copy-done.8
  15.4 0.6 copy-done.9
  16.0 0.2 add_dynamic-update-slice_fusion
  16.2 25.9 %all-reduce.about = s32[1536]{0:T(1024)S(1)} all-reduce(s32[1536]{0:T(1024)S(1)} %add_dynamic-update-slice_fusion), channel_id=1, replica_groups=mesh['orb'=32,'slab'=8] {'orb'}, use_global_device_ids=true, to_apply=%add | all-reduce | flops 1536 | bytes 12288
  42.1 0.0 all-to-all-done.pieces
  42.1 0.0 copy-done.5
  42.1 0.0 copy-done.6
  42.1 0.6 copy-done.7
  42.7 5.2 %pick.1 = (bf16[256,16,128]{2,1,0:T(8,128)(2,1)}, s32[768]{0:T(1024)S(1)}) custom-call(s32[32]{0:T(128)S(1)} %copy-done.7, s32[512]{0:T(512)S(1)} %bitcast.7, s32[512]{0:T(512)S(1)} %copy-done.6, s32[1536]{0:T(1024)S(1)} %all-reduce.about, bf16[32,64,128]{2,1,0:T(8,128)(2,1)S(1)} %all-to-all-done.pieces), custom_call_target="tpu_custom_call" | custom-call | tf_op jit(solution)/shard_map/pick/pallas_call | solution.py:287
  47.9 0.0 copy-start.1
  47.9 0.0 copy-start.2
  47.9 0.0 copy-start.3
  47.9 8.8 %all-to-all-start.1 = ((bf16[256,16,128]{2,1,0:T(8,128)(2,1)}), bf16[256,16,128]{2,1,0:T(8,128)(2,1)S(1)}, u32[]{:S(2)}, u32[]{:S(2)}) async-start(bf16[256,16,128]{2,1,0:T(8,128)(2,1)} %get-tuple-element.8), calls=%async_computation.1 | async-start | bytes 2097152 | tf_op jit(solution)/shard_map/all_to_all | solution.py:295
  56.8 0.0 copy-start.4
  56.8 31.2 %all-to-all-done.1.boxes = bf16[256,16,128]{2,1,0:T(8,128)(2,1)S(1)} async-done(((bf16[256,16,128]{2,1,0:T(8,128)(2,1)}), bf16[256,16,128]{2,1,0:T(8,128)(2,1)S(1)}, u32[]{:S(2)}, u32[]{:S(2)}) %all-to-all-start.1) | async-done | bytes 1048608 | tf_op jit(solution)/shard_map/all_to_all | solution.py:295
  88.0 0.0 copy-done.1
  88.0 0.0 copy-done.2
  88.0 0.0 copy-done.3
  88.0 0.0 copy-done.4
  88.0 14.7 %solve.1 = bf16[256,16,128]{2,1,0:T(8,128)(2,1)S(1)} custom-call(s32[1]{0:T(128)} %bitcast.4.me, s32[768]{0:T(1024)S(1)} %get-tuple-element.7.index, s32[1536]{0:T(1024)S(1)} %all-reduce.about, bf16[256,256]{1,0:T(8,128)(2,1)S(1)} %copy-done.1, bf16[64,192]{1,0:T(8,128)(2,1)S(1)} %copy-done.3, f32[64,128]{1,0:T(8,128)S(1)} %copy-done.2, ...), custom_call_target="tpu_custom_call" | custom-call | tf_op jit(solution)/shard_map/solve/pallas_call | solution.py:297
  102.7 37.2 %all_to_all.20.terms = bf16[256,16,128]{2,1,0:T(8,128)(2,1)S(1)} all-to-all(bf16[256,16,128]{2,1,0:T(8,128)(2,1)S(1)} %solve.1), channel_id=1, replica_groups=mesh['orb'=32,'slab'=8] {'orb','slab'}, dimensions={0} | all-to-all | bytes 2097152 | tf_op jit(solution)/shard_map/all_to_all | solution.py:304
  139.9 2.9 %sum.1 = bf16[32,64,128]{2,1,0:T(8,128)(2,1)S(1)} custom-call(s32[768]{0:T(1024)S(1)} %get-tuple-element.7.index, bf16[256,16,128]{2,1,0:T(8,128)(2,1)S(1)} %all_to_all.20.terms), custom_call_target="tpu_custom_call" | custom-call | tf_op jit(solution)/shard_map/sum/pallas_call | solution.py:305
  142.8 20.7 %all_to_all.21.pieces = bf16[32,64,128]{2,1,0:T(8,128)(2,1)S(1)} all-to-all(bf16[32,64,128]{2,1,0:T(8,128)(2,1)S(1)} %sum.1), channel_id=1, replica_groups=mesh['orb'=32,'slab'=8] {'orb'}, dimensions={0} | all-to-all | bytes 1048576 | tf_op jit(solution)/shard_map/all_to_all | solution.py:311
  163.5 0.9 join.1
  (6 shorter events, 0.0 us)
Async XLA Ops:
  0.0 1.0 copy-start
  1.9 40.2 %all-to-all-start = ((bf16[32,64,128]{2,1,0:T(8,128)(2,1)}), bf16[32,64,128]{2,1,0:T(8,128)(2,1)S(1)}, u32[]{:S(2)}, u32[]{:S(2)}) async-start(bf16[32,64,128]{2,1,0:T(8,128)(2,1)} %spread.1), calls=%async_computation | async-start | bytes 1048576 | tf_op jit(solution)/shard_map/all_to_all | solution.py:286
  13.4 0.7 copy-start.10
  14.7 0.7 copy-start.8
  15.4 0.7 copy-start.9
  16.2 25.9 %copy-start.5 = (s32[512,1]{0,1:T(1,128)S(1)}, s32[512,1]{0,1:T(1,128)}, u32[]{:S(2)}) copy-start(s32[512,1]{0,1:T(1,128)} %param.12) | copy-start | bytes 6148
  16.2 25.9 %copy-start.6 = (s32[512]{0:T(512)S(1)}, s32[512]{0:T(512)}, u32[]{:S(2)}) copy-start(s32[512]{0:T(512)} %local.1) | copy-start | bytes 6148
  42.1 0.7 copy-start.7
  47.9 40.1 %copy-start.1 = (bf16[256,256]{1,0:T(8,128)(2,1)S(1)}, bf16[256,256]{1,0:T(8,128)(2,1)}, u32[]{:S(2)}) copy-start(bf16[256,256]{1,0:T(8,128)(2,1)} %constant.19.clone.right) | copy-start | bytes 393220
  47.9 40.1 %copy-start.2 = (f32[64,128]{1,0:T(8,128)S(1)}, f32[64,128]{1,0:T(8,128)}, u32[]{:S(2)}) copy-start(f32[64,128]{1,0:T(8,128)} %constant.21.clone.base) | copy-start | bytes 98308
  47.9 40.1 %copy-start.3 = (bf16[64,192]{1,0:T(8,128)(2,1)S(1)}, bf16[64,192]{1,0:T(8,128)(2,1)}, u32[]{:S(2)}) copy-start(bf16[64,192]{1,0:T(8,128)(2,1)} %constant.20.clone.left) | copy-start | bytes 73732
  47.9 40.1 %all-to-all-start.1 = ((bf16[256,16,128]{2,1,0:T(8,128)(2,1)}), bf16[256,16,128]{2,1,0:T(8,128)(2,1)S(1)}, u32[]{:S(2)}, u32[]{:S(2)}) async-start(bf16[256,16,128]{2,1,0:T(8,128)(2,1)} %get-tuple-element.8), calls=%async_computation.1 | async-start | bytes 2097152 | tf_op jit(solution)/shard_map/all_to_all | solution.py:295
  56.8 31.2 %copy-start.4 = (f32[32,128]{1,0:T(8,128)S(1)}, f32[32,128]{1,0:T(8,128)}, u32[]{:S(2)}) copy-start(f32[32,128]{1,0:T(8,128)} %constant.22.clone.lam_a) | copy-start | bytes 49156

commit v2 on v1

v2 whole, which is shorter than its diff:
```python
import math

import jax
import jax.numpy as jnp
import numpy as np
from jax import lax
from jax.experimental import pallas as pl
from jax.experimental.pallas import tpu as pltpu
from jax.sharding import PartitionSpec as P

BOX = 64
ORB_DEV = 8
PAIR_DEV = 16
N_ORB = 32
N_DEV = 256
TILES = 32
LANES = 128
SCREENING = 0.02
PARAMS = pltpu.CompilerParams(vmem_limit_bytes=48 * 1024 * 1024)
WHOLE_V = pl.BlockSpec(memory_space=pltpu.VMEM)
WHOLE_S = pl.BlockSpec(memory_space=pltpu.SMEM)


def hartley_table():
    line = np.arange(BOX)
    angle = (line[:, None] * line[None, :] % BOX) * (2.0 * math.pi / BOX)
    return np.cos(angle) + np.sin(angle)


def halves(table):
    high = table.astype(np.float32).astype(jnp.bfloat16)
    low = (table - high.astype(np.float64)).astype(np.float32).astype(jnp.bfloat16)
    return high, low


def tables():
    high, low = halves(hartley_table())
    zero = np.zeros((BOX, BOX), high.dtype)

    def twice(table):
        return np.block([[table, zero], [zero, table]])

    right = np.block([[twice(high), twice(low)], [twice(high), np.zeros((128, 128), high.dtype)]])
    left = np.concatenate([high, high, low], axis=1)
    lam = 2.0 - 2.0 * np.cos(np.arange(BOX) * (2.0 * math.pi / BOX))
    lam_a = np.repeat(lam.reshape(2, TILES).T, BOX, axis=1)
    under = lam_a[:, None, :] + lam[None, :, None] + np.tile(lam, 2)[None, None, :] + SCREENING
    return right, left, (1.0 / BOX**3 / under).astype(np.float32)


def split(field):
    high = field.astype(jnp.bfloat16)
    low = (field - high.astype(jnp.float32)).astype(jnp.bfloat16)
    return high, low


def fast_hartley(parts):
    n = len(parts)
    if n == 1:
        return parts
    if n == 2:
        return [parts[0] + parts[1], parts[0] - parts[1]]
    even, odd = fast_hartley(parts[0::2]), fast_hartley(parts[1::2])
    m = n // 2
    out = [None] * n
    for k in range(m):
        if k == 0 or 4 * k == n:
            turned = odd[k]
        else:
            angle = 2.0 * math.pi * k / n
            turned = odd[k] * math.cos(angle) + odd[m - k] * math.sin(angle)
        out[k] = even[k] + turned
        out[k + m] = even[k] - turned
    return out


def twist(parts, first):
    out = []
    for k in range(TILES):
        mirror = parts[(TILES - k) % TILES]
        angle = 2.0 * math.pi * k / BOX
        if k == 0 or 2 * k == TILES:
            out.append(parts[k])
        else:
            out.append(jnp.where(first, parts[k], parts[k] * math.cos(angle) + mirror * math.sin(angle)))
    return out


def untwist(parts, first):
    out = []
    for k in range(TILES):
        mirror = parts[(TILES - k) % TILES]
        angle = 2.0 * math.pi * k / BOX
        back = 2.0 * math.pi * ((TILES - k) % TILES) / BOX
        if k == 0 or 2 * k == TILES:
            out.append(parts[k])
        else:
            out.append(jnp.where(first, parts[k], parts[k] * math.cos(angle) + mirror * math.sin(back)))
    return out


def spread_kernel(first, shift, orbitals, pieces):
    for pair in range(ORB_DEV // 2):
        one = orbitals[2 * pair].astype(jnp.float32)
        two = orbitals[2 * pair + 1].astype(jnp.float32)
        for tile in range(TILES):
            at = slice(tile * LANES, (tile + 1) * LANES)
            pieces[tile, 16 * pair : 16 * pair + 16, :] = jnp.concatenate(
                [one[:, at], two[:, at]], axis=0
            ).astype(jnp.bfloat16)
    lane = lax.broadcasted_iota(jnp.int32, (8, LANES), 1)
    about = jnp.zeros((8, LANES), jnp.int32)
    for k in range(PAIR_DEV):
        about = jnp.where(lane == k, first[k], about)
        about = jnp.where(lane == PAIR_DEV + k, shift[k, 0], about)
        about = jnp.where(lane == 2 * PAIR_DEV + k, shift[k, 1], about)
    about = about.astype(jnp.float32).astype(jnp.bfloat16)
    for tile in range(TILES):
        pieces[tile, ORB_DEV * 8 :, :] = about


def list_kernel(count, owner, local, listed):
    def of_orb(e, base):
        live = count[e]

        def of_slot(k, carry):
            slot = e * PAIR_DEV + k
            listed[base + k] = e * LANES + k
            listed[N_DEV + base + k] = owner[slot] * ORB_DEV + local[slot]
            return carry

        lax.fori_loop(0, live, of_slot, 0)
        return base + live

    lax.fori_loop(0, N_ORB, of_orb, 0)


def pick_kernel(me, listed, pieces, picked, firsts, mine, held, whole, about, done):
    whole[...] = pieces[:, ORB_DEV * 8, :].astype(jnp.float32).astype(jnp.int32)
    copy = pltpu.make_async_copy(whole, about, done)
    copy.start()
    for e in range(N_ORB):
        block = pieces[e, : ORB_DEV * 8, :].astype(jnp.float32)
        held[e * ORB_DEV : (e + 1) * ORB_DEV] = block.reshape(ORB_DEV, 8, LANES)
    copy.wait()

    def step(at, carry):
        for k in range(8):
            d = at * 8 + k
            e, lane = listed[d] // LANES, listed[d] % LANES
            first = e * ORB_DEV + about[e, lane]
            firsts[d] = first
            both = jnp.concatenate([held[first], held[listed[N_DEV + d]]], axis=0)
            picked[d] = both.astype(jnp.bfloat16)
        return carry

    lax.fori_loop(0, N_DEV // 8, step, 0)
    e, lane = listed[me[0]] // LANES, listed[me[0]] % LANES
    mine[0] = about[e, lane + PAIR_DEV]
    mine[1] = about[e, lane + 2 * PAIR_DEV]


def shifted(tiles, start, count, flat, shift_x, shift_y):
    lane = lax.broadcasted_iota(jnp.int32, (8, LANES), 1)
    whole, rest = flat // LANES, flat % LANES
    later = (lane >= rest)[None]
    y = lane % BOX - shift_y
    keep_y = (y >= 0) & (y < BOX)
    turned = [
        pltpu.roll(tiles((start + k - whole - 1 + 2 * TILES) % TILES), rest, 2) for k in range(count + 1)
    ]
    out = []
    for k in range(count):
        x = 2 * (start + k) + lane // BOX - shift_x
        keep = jnp.where(keep_y & (x >= 0) & (x < BOX), 1.0, 0.0)
        out.append(jnp.where(later, turned[k + 1], turned[k]) * keep[None])
    return out


def solve_kernel(shift, right, left, screen, boxes, terms, moved, field, other):
    shift_x, shift_y = shift[0], shift[1]
    full = BOX * BOX
    ahead = (shift_x * BOX + shift_y + full) % full
    back = (full - ahead) % full
    early = lax.broadcasted_iota(jnp.int32, (8, LANES), 1) < BOX
    sign = jnp.where(early, 1.0, -1.0)

    def first_tile(tile):
        return boxes[pl.ds(tile * 8, 8), :8, :].astype(jnp.float32)

    def second_tile(tile):
        return boxes[pl.ds(tile * 8, 8), 8:, :].astype(jnp.float32)

    def along_y(block):
        high, low = split(block)
        product = jnp.dot(
            jnp.concatenate([high, low], axis=1), right[...], preferred_element_type=jnp.float32
        )
        return product[:, :LANES] + product[:, LANES:]

    def forward_y(step, carry):
        for k, box in enumerate(shifted(second_tile, step * 4, 4, ahead, shift_x, shift_y)):
            tile = step * 4 + k
            moved[tile] = box
            other[tile] = first_tile(tile) * box
        tiles = pl.ds(step * 4, 4)
        field[tiles] = along_y(other[tiles].reshape(4 * BOX, LANES)).reshape(4, BOX, LANES)
        return carry

    lax.fori_loop(0, TILES // 4, forward_y, 0)

    def forward_x(step, carry):
        rows = pl.ds(pl.multiple_of(step * 8, 8), 8)
        parts = twist(fast_hartley([field[k, rows, :] for k in range(TILES)]), early)
        for k in range(TILES):
            field[k, rows, :] = sign * parts[k] + pltpu.roll(parts[k], BOX, 1)
        return carry

    lax.fori_loop(0, 8, forward_x, 0)

    def along_z(block):
        high, low = split(block)
        return jnp.dot(
            left[...], jnp.concatenate([high, low, high], axis=0), preferred_element_type=jnp.float32
        )

    def screened_z(step, carry):
        tiles = [step * 8 + k for k in range(8)]
        blocks = [jnp.concatenate([field[tiles[k]], field[tiles[k + 1]]], axis=1) for k in range(0, 8, 2)]
        blocks = [along_z(block) for block in blocks]
        for k in range(8):
            half = slice(k % 2 * LANES, (k % 2 + 1) * LANES)
            field[tiles[k]] = blocks[k // 2][:, half] * screen[tiles[k]]
        blocks = [jnp.concatenate([field[tiles[k]], field[tiles[k + 1]]], axis=1) for k in range(0, 8, 2)]
        blocks = [along_z(block) for block in blocks]
        for k in range(8):
            half = slice(k % 2 * LANES, (k % 2 + 1) * LANES)
            field[tiles[k]] = blocks[k // 2][:, half]
        return carry

    lax.fori_loop(0, TILES // 8, screened_z, 0)

    def inverse_x(step, carry):
        rows = pl.ds(pl.multiple_of(step * 8, 8), 8)
        parts = [field[k, rows, :] for k in range(TILES)]
        parts = [sign * part + pltpu.roll(part, BOX, 1) for part in parts]
        parts = fast_hartley(untwist(parts, early))
        for k in range(TILES):
            field[k, rows, :] = parts[k]
        return carry

    lax.fori_loop(0, 8, inverse_x, 0)

    def inverse_y(step, carry):
        tiles = pl.ds(step * 4, 4)
        potential = along_y(field[tiles].reshape(4 * BOX, LANES)).reshape(4, 8, 8, LANES)
        for k in range(4):
            other[step * 4 + k] = potential[k] * first_tile(step * 4 + k)
            moved[step * 4 + k] = potential[k] * moved[step * 4 + k]
        return carry

    lax.fori_loop(0, TILES // 4, inverse_y, 0)

    def pack(step, carry):
        carried = shifted(lambda tile: other[tile], step * 4, 4, back, -shift_x, -shift_y)
        for k in range(4):
            both = jnp.concatenate([moved[step * 4 + k], carried[k]], axis=1)
            terms[pl.ds((step * 4 + k) * 8, 8)] = both.astype(jnp.bfloat16)
        return carry

    lax.fori_loop(0, TILES // 4, pack, 0)


def sum_kernel(firsts, listed, terms, pieces, own, carried):
    own[...] = jnp.zeros_like(own)
    carried[...] = jnp.zeros_like(carried)

    def step(at, carry):
        for k in range(8):
            d = at * 8 + k
            both = terms[d].astype(jnp.float32)
            first, second = firsts[d], listed[N_DEV + d]
            own[first] = own[first] + both[:8]
            carried[second] = carried[second] + both[8:]
        return carry

    lax.fori_loop(0, N_DEV // 8, step, 0)
    for e in range(N_ORB):
        at = slice(e * ORB_DEV, (e + 1) * ORB_DEV)
        pieces[e] = (own[at] + carried[at]).reshape(ORB_DEV * 8, LANES).astype(jnp.bfloat16)


def join_kernel(pieces, result):
    for pair in range(ORB_DEV // 2):
        tiles = [pieces[tile, 16 * pair : 16 * pair + 16, :].astype(jnp.float32) for tile in range(TILES)]
        for side in range(2):
            rows = [tile[8 * side : 8 * side + 8] for tile in tiles]
            result[2 * pair + side] = jnp.concatenate(rows, axis=1).astype(jnp.bfloat16)


def body(orbitals, pair_first, second_owner, second_local, pair_shift, pair_count):
    f32, bf16, i32 = jnp.float32, jnp.bfloat16, jnp.int32
    shape = jax.ShapeDtypeStruct
    me = (lax.axis_index("orb") * 8 + lax.axis_index("slab")).reshape(1)
    rows = ORB_DEV * 8
    pair_shape = shape((N_DEV, 16, LANES), bf16)
    pieces = pl.pallas_call(
        spread_kernel, out_shape=shape((N_ORB, rows + 8, LANES), bf16),
        in_specs=[WHOLE_S, WHOLE_S, WHOLE_V], out_specs=WHOLE_V,
        compiler_params=PARAMS, name="spread",
    )(pair_first, pair_shift, orbitals)
    pieces = lax.all_to_all(pieces, "orb", split_axis=0, concat_axis=0, tiled=True)
    listed = pl.pallas_call(
        list_kernel, out_shape=shape((2 * N_DEV,), i32),
        in_specs=[WHOLE_S] * 3, out_specs=WHOLE_S,
        compiler_params=PARAMS, name="list",
    )(pair_count, second_owner[:, 0], second_local)
    picked, firsts, mine = pl.pallas_call(
        pick_kernel,
        out_shape=(pair_shape, shape((N_DEV,), i32), shape((2,), i32)),
        in_specs=[WHOLE_S, WHOLE_S, WHOLE_V],
        out_specs=(WHOLE_V, WHOLE_S, WHOLE_S),
        scratch_shapes=[
            pltpu.VMEM((N_DEV, 8, LANES), f32),
            pltpu.VMEM((N_ORB, LANES), i32),
            pltpu.SMEM((N_ORB, LANES), i32),
            pltpu.SemaphoreType.DMA,
        ],
        compiler_params=PARAMS, name="pick",
    )(me, listed, pieces)
    boxes = lax.all_to_all(picked, ("orb", "slab"), split_axis=0, concat_axis=0, tiled=True)
    right, left, screen = (jnp.asarray(table) for table in tables())
    terms = pl.pallas_call(
        solve_kernel, out_shape=pair_shape,
        in_specs=[WHOLE_S] + [WHOLE_V] * 4,
        out_specs=WHOLE_V,
        scratch_shapes=[
            pltpu.VMEM((TILES, 8, 8, LANES), f32),
            pltpu.VMEM((TILES, BOX, LANES), f32),
            pltpu.VMEM((TILES, 8, 8, LANES), f32),
        ],
        compiler_params=PARAMS, name="solve",
    )(mine, right, left, screen, boxes)
    terms = lax.all_to_all(terms, ("orb", "slab"), split_axis=0, concat_axis=0, tiled=True)
    pieces = pl.pallas_call(
        sum_kernel, out_shape=shape((N_ORB, rows, LANES), bf16),
        in_specs=[WHOLE_S, WHOLE_S, WHOLE_V], out_specs=WHOLE_V,
        scratch_shapes=[pltpu.VMEM((N_DEV, 8, LANES), f32)] * 2,
        compiler_params=PARAMS, name="sum",
    )(firsts, listed, terms)
    pieces = lax.all_to_all(pieces, "orb", split_axis=0, concat_axis=0, tiled=True)
    return pl.pallas_call(
        join_kernel, out_shape=shape((ORB_DEV, 8, BOX * BOX), bf16),
        in_specs=[WHOLE_V], out_specs=WHOLE_V,
        compiler_params=PARAMS, name="join",
    )(pieces)


def solution(mesh):
    in_specs = (P("orb", "slab", None), P("orb"), P(), P(), P("orb", None), P())
    out_specs = P("orb", "slab", None)
    return jax.shard_map(body, mesh=mesh, in_specs=in_specs, out_specs=out_specs, check_vma=False)
```

time: 166 us -> 149 us (0.90)
  waiting for transfers between devices: 31.2 us -> 14.2 us
  blocking collectives: 83.8 us -> 97.6 us
  starting transfers between devices: 20.3 us -> 11.5 us
  Pallas kernels: 24.4 us -> 21.5 us
    all_to_all x0 -> x1, blocking collectives: none -> 39.7 us  [body(): lax.all_to_all(picked, ('orb', 'slab'), split_axis=0, concat_axis=0, tile...]
    all_to_all x1 -> x0, waiting for transfers between devices: 31.2 us -> none  [body(): lax.all_to_all(picked, ('orb', 'slab'), split_axis=0, concat_axis=0, tile...]
    unnamed x1 -> x0, blocking collectives: 25.9 us -> none
    all_to_all x1, waiting for transfers between devices: 0.01 us -> 14.2 us  [body(): lax.all_to_all(pieces, 'orb', split_axis=0, concat_axis=0, tiled=True)]
    all_to_all x1 -> x0, starting transfers between devices: 8.85 us -> none  [body(): lax.all_to_all(picked, ('orb', 'slab'), split_axis=0, concat_axis=0, tile...]
    pallas_call x5 -> x6, Pallas kernels: 24.4 us -> 21.5 us  [the longest x1 8.87 us: body(): pl.pallas_call(solve_kernel, out_shape=pair_shape, in_specs=[WHOLE_S] + [...]
    unnamed x24 -> x17, local copies, waits for them, and re-layouts: 3.66 us -> 2.51 us
  transfers between devices with their start and end apart: 2 -> 1, of which waited for: 1 -> 1; matrix products, arithmetic and copies ran while one was open for 0% -> 0% of each run, Pallas kernels for 0% -> 2%
where the time goes in v2:
time: 149 us; the launch traced here: 147 us
  blocking collectives  97.6 us (66%)
  Pallas kernels  21.5 us (14%)
  waiting for transfers between devices  14.2 us (10%)
  starting transfers between devices  11.5 us (8%)
  local copies, waits for them, and re-layouts  2.51 us (2%)
    all_to_all x1, blocking collectives, body(): lax.all_to_all(picked, ('orb', 'slab'), split_axis=0, concat_axis=0, tile...  39.7 us
    all_to_all x1, blocking collectives, body(): lax.all_to_all(terms, ('orb', 'slab'), split_axis=0, concat_axis=0, tiled...  37.2 us
    all_to_all x1, blocking collectives, body(): lax.all_to_all(pieces, 'orb', split_axis=0, concat_axis=0, tiled=True)  20.7 us
    all_to_all x1, waiting for transfers between devices, body(): lax.all_to_all(pieces, 'orb', split_axis=0, concat_axis=0, tiled=True)  14.2 us
    all_to_all x1, starting transfers between devices, body(): lax.all_to_all(pieces, 'orb', split_axis=0, concat_axis=0, tiled=True)  11.5 us
    pallas_call x1, Pallas kernels, body(): pl.pallas_call(solve_kernel, out_shape=pair_shape, in_specs=[WHOLE_S] + [...  8.87 us
    pallas_call x1, Pallas kernels, body(): pl.pallas_call(pick_kernel, out_shape=(pair_shape, shape((N_DEV,), i32),...  4.7 us
    pallas_call x1, Pallas kernels, body(): pl.pallas_call(list_kernel, out_shape=shape((2 * N_DEV,), i32), in_specs=...  3.56 us
  transfers between devices with their start and end apart: 1, of which 1 were waited for; matrix products, arithmetic and copies ran while one was open for 0% of the time, Pallas kernels for 2%

profile of v2, /device:TPU:2, one launch (start us, length us, event | category | flops | bytes accessed | tf_op | source)
XLA Modules:
  0.0 147.3 jit_solution(8207926319091756202)
XLA Ops:
  0.0 0.0 copy-start.6
  0.0 0.8 copy.10.shift
  0.8 0.0 copy-done.6
  0.8 0.0 copy-start.1
  0.8 1.0 copy-done.1
  1.8 1.6 %spread.1 = bf16[32,72,128]{2,1,0:T(8,128)(2,1)} custom-call(s32[16]{0:T(128)S(1)} %copy-done.6, s32[16,2]{1,0:T(8,128)S(1)} %copy.10.shift, bf16[8,8,4096]{2,1,0:T(8,128)(2,1)S(1)} %copy-done.1), custom_call_target="tpu_custom_call" | custom-call | tf_op jit(solution)/shard_map/spread/pallas_call | solution.py:307
  3.4 11.5 %all-to-all-start = ((bf16[32,72,128]{2,1,0:T(8,128)(2,1)}), bf16[32,72,128]{2,1,0:T(8,128)(2,1)S(1)}, u32[]{:S(2)}, u32[]{:S(2)}) async-start(bf16[32,72,128]{2,1,0:T(8,128)(2,1)} %spread.1), calls=%async_computation | async-start | bytes 1179648 | tf_op jit(solution)/shard_map/all_to_all | solution.py:312
  14.9 0.0 copy-start.5
  14.9 0.0 copy-start.4
  14.9 0.0 copy-start.7
  14.9 0.6 copy-done.5
  15.6 0.0 copy-done.4
  15.6 0.0 copy-done.7
  15.6 3.6 %list.1.listed = s32[512]{0:T(512)S(1)} custom-call(s32[32]{0:T(128)S(1)} %copy-done.7, s32[512]{0:T(512)S(1)} %bitcast.2, s32[512]{0:T(512)S(1)} %copy-done.5), custom_call_target="tpu_custom_call" | custom-call | tf_op jit(solution)/shard_map/list/pallas_call | solution.py:313
  19.2 14.2 %all-to-all-done.pieces = bf16[32,72,128]{2,1,0:T(8,128)(2,1)S(1)} async-done(((bf16[32,72,128]{2,1,0:T(8,128)(2,1)}), bf16[32,72,128]{2,1,0:T(8,128)(2,1)S(1)}, u32[]{:S(2)}, u32[]{:S(2)}) %all-to-all-start) | async-done | bytes 589856 | tf_op jit(solution)/shard_map/all_to_all | solution.py:312
  33.3 4.7 %pick.1 = (bf16[256,16,128]{2,1,0:T(8,128)(2,1)S(1)}, s32[256]{0:T(256)S(1)}, s32[2]{0:T(128)S(1)}) custom-call(s32[1]{0:T(128)} %bitcast.me, s32[512]{0:T(512)S(1)} %list.1.listed, bf16[32,72,128]{2,1,0:T(8,128)(2,1)S(1)} %all-to-all-done.pieces), custom_call_target="tpu_custom_call" | custom-call | tf_op jit(solution)/shard_map/pick/pallas_call | solution.py:318
  38.1 0.0 copy-start
  38.1 0.0 copy-start.2
  38.1 0.0 copy-start.3
  38.1 39.7 %all_to_all.20.boxes = bf16[256,16,128]{2,1,0:T(8,128)(2,1)S(1)} all-to-all(bf16[256,16,128]{2,1,0:T(8,128)(2,1)S(1)} %get-tuple-element.10), channel_id=1, replica_groups=mesh['orb'=32,'slab'=8] {'orb','slab'}, dimensions={0} | all-to-all | bytes 2097152 | tf_op jit(solution)/shard_map/all_to_all | solution.py:331
  77.7 0.0 copy-done
  77.8 0.0 copy-done.2
  77.8 0.0 copy-done.3
  77.8 8.9 %solve.1 = bf16[256,16,128]{2,1,0:T(8,128)(2,1)S(1)} custom-call(s32[2]{0:T(128)S(1)} %get-tuple-element.9.shift, bf16[256,256]{1,0:T(8,128)(2,1)S(1)} %copy-done.2, bf16[64,192]{1,0:T(8,128)(2,1)S(1)} %copy-done.3, f32[32,64,128]{2,1,0:T(8,128)S(1)} %copy-done, bf16[256,16,128]{2,1,0:T(8,128)(2,1)S(1)} %all_to_all.20.boxes), custom_call_target="tpu_custom_call" | custom-call | tf_op jit(solution)/shard_map/solve/pallas_call | solution.py:333
  86.6 37.2 %all_to_all.21.terms = bf16[256,16,128]{2,1,0:T(8,128)(2,1)S(1)} all-to-all(bf16[256,16,128]{2,1,0:T(8,128)(2,1)S(1)} %solve.1), channel_id=1, replica_groups=mesh['orb'=32,'slab'=8] {'orb','slab'}, dimensions={0} | all-to-all | bytes 2097152 | tf_op jit(solution)/shard_map/all_to_all | solution.py:344
  123.8 1.9 %sum.1 = bf16[32,64,128]{2,1,0:T(8,128)(2,1)S(1)} custom-call(s32[256]{0:T(256)S(1)} %get-tuple-element.8.firsts, s32[512]{0:T(512)S(1)} %list.1.listed, bf16[256,16,128]{2,1,0:T(8,128)(2,1)S(1)} %all_to_all.21.terms), custom_call_target="tpu_custom_call" | custom-call | tf_op jit(solution)/shard_map/sum/pallas_call | solution.py:345
  125.7 20.7 %all_to_all.22.pieces = bf16[32,64,128]{2,1,0:T(8,128)(2,1)S(1)} all-to-all(bf16[32,64,128]{2,1,0:T(8,128)(2,1)S(1)} %sum.1), channel_id=1, replica_groups=mesh['orb'=32,'slab'=8] {'orb'}, dimensions={0} | all-to-all | bytes 1048576 | tf_op jit(solution)/shard_map/all_to_all | solution.py:351
  146.4 0.9 join.1
Async XLA Ops:
  0.0 0.8 copy-start.6
  0.8 1.0 copy-start.1
  3.4 30.0 %all-to-all-start = ((bf16[32,72,128]{2,1,0:T(8,128)(2,1)}), bf16[32,72,128]{2,1,0:T(8,128)(2,1)S(1)}, u32[]{:S(2)}, u32[]{:S(2)}) async-start(bf16[32,72,128]{2,1,0:T(8,128)(2,1)} %spread.1), calls=%async_computation | async-start | bytes 1179648 | tf_op jit(solution)/shard_map/all_to_all | solution.py:312
  14.9 0.7 copy-start.5
  14.9 0.7 copy-start.4
  14.9 0.7 copy-start.7
  38.1 39.7 %copy-start = (f32[32,64,128]{2,1,0:T(8,128)S(1)}, f32[32,64,128]{2,1,0:T(8,128)}, u32[]{:S(2)}) copy-start(f32[32,64,128]{2,1,0:T(8,128)} %constant.19.clone.screen) | copy-start | bytes 3145732
  38.1 39.7 %copy-start.2 = (bf16[256,256]{1,0:T(8,128)(2,1)S(1)}, bf16[256,256]{1,0:T(8,128)(2,1)}, u32[]{:S(2)}) copy-start(bf16[256,256]{1,0:T(8,128)(2,1)} %constant.17.clone.right) | copy-start | bytes 393220
  38.1 39.7 %copy-start.3 = (bf16[64,192]{1,0:T(8,128)(2,1)S(1)}, bf16[64,192]{1,0:T(8,128)(2,1)}, u32[]{:S(2)}) copy-start(bf16[64,192]{1,0:T(8,128)(2,1)} %constant.18.clone.left) | copy-start | bytes 73732

commit v3 on v2

--- a/solution.py
+++ b/solution.py
@@ -99,65 +99,82 @@
     return out
 
 
-def spread_kernel(first, shift, orbitals, pieces):
-    for pair in range(ORB_DEV // 2):
-        one = orbitals[2 * pair].astype(jnp.float32)
-        two = orbitals[2 * pair + 1].astype(jnp.float32)
+def spread_kernel(first, shift, orbitals, pieces, tall, about):
+    for orbital in range(ORB_DEV):
+        box = orbitals[orbital].astype(jnp.float32)
         for tile in range(TILES):
-            at = slice(tile * LANES, (tile + 1) * LANES)
-            pieces[tile, 16 * pair : 16 * pair + 16, :] = jnp.concatenate(
-                [one[:, at], two[:, at]], axis=0
-            ).astype(jnp.bfloat16)
-    lane = lax.broadcasted_iota(jnp.int32, (8, LANES), 1)
-    about = jnp.zeros((8, LANES), jnp.int32)
-    for k in range(PAIR_DEV):
-        about = jnp.where(lane == k, first[k], about)
-        about = jnp.where(lane == PAIR_DEV + k, shift[k, 0], about)
-        about = jnp.where(lane == 2 * PAIR_DEV + k, shift[k, 1], about)
-    about = about.astype(jnp.float32).astype(jnp.bfloat16)
+            row = tile * ORB_DEV * 8 + 8 * orbital
+            tall[row : row + 8, :] = box[:, tile * LANES : (tile + 1) * LANES]
+    about[...] = jnp.zeros_like(about)
+    about[0:1, :PAIR_DEV] = first[...].astype(jnp.float32)
+    about[1:3, :PAIR_DEV] = shift[...].astype(jnp.float32)
+    placed = pltpu.roll(about[...], lax.axis_index("orb") % 8 * PAIR_DEV, 1).astype(jnp.bfloat16)
     for tile in range(TILES):
-        pieces[tile, ORB_DEV * 8 :, :] = about
-
-
-def list_kernel(count, owner, local, listed):
-    def of_orb(e, base):
-        live = count[e]
-
-        def of_slot(k, carry):
-            slot = e * PAIR_DEV + k
-            listed[base + k] = e * LANES + k
-            listed[N_DEV + base + k] = owner[slot] * ORB_DEV + local[slot]
-            return carry
-
-        lax.fori_loop(0, live, of_slot, 0)
-        return base + live
-
-    lax.fori_loop(0, N_ORB, of_orb, 0)
-
-
-def pick_kernel(me, listed, pieces, picked, firsts, mine, held, whole, about, done):
-    whole[...] = pieces[:, ORB_DEV * 8, :].astype(jnp.float32).astype(jnp.int32)
-    copy = pltpu.make_async_copy(whole, about, done)
-    copy.start()
+        for z in range(8):
+            row = tile * ORB_DEV * 8 + z
+            pieces[tile, z] = tall[pl.ds(row, ORB_DEV, stride=8), :].astype(jnp.bfloat16)
+        pieces[tile, 8] = placed
+
+
+def dot_rows(one, two):
+    return lax.dot_general(one, two, (((1,), (1,)), ((), ())), preferred_element_type=jnp.float32)
+
+
+def chosen(column):
+    lane = lax.broadcasted_iota(jnp.int32, (N_DEV, LANES), 1).astype(jnp.float32)
+    hits = [jnp.where(column == lane + half * LANES, 1.0, 0.0) for half in range(2)]
+    return jnp.concatenate(hits, axis=1).astype(jnp.bfloat16)
+
+
+def place_kernel(count, owner, local, place, second, choose):
+    shape = (4, LANES)
+    slot = lax.broadcasted_iota(jnp.int32, shape, 0) * LANES + lax.broadcasted_iota(jnp.int32, shape, 1)
+    orb, rank = slot // PAIR_DEV, slot % PAIR_DEV
+    before, live = jnp.zeros(shape, jnp.int32), jnp.zeros(shape, jnp.int32)
     for e in range(N_ORB):
-        block = pieces[e, : ORB_DEV * 8, :].astype(jnp.float32)
-        held[e * ORB_DEV : (e + 1) * ORB_DEV] = block.reshape(ORB_DEV, 8, LANES)
-    copy.wait()
-
-    def step(at, carry):
-        for k in range(8):
-            d = at * 8 + k
-            e, lane = listed[d] // LANES, listed[d] % LANES
-            first = e * ORB_DEV + about[e, lane]
-            firsts[d] = first
-            both = jnp.concatenate([held[first], held[listed[N_DEV + d]]], axis=0)
-            picked[d] = both.astype(jnp.bfloat16)
-        return carry
-
-    lax.fori_loop(0, N_DEV // 8, step, 0)
-    e, lane = listed[me[0]] // LANES, listed[me[0]] % LANES
-    mine[0] = about[e, lane + PAIR_DEV]
-    mine[1] = about[e, lane + 2 * PAIR_DEV]
+        before = before + jnp.where(orb > e, count[e], 0)
+        live = jnp.where(orb == e, count[e], live)
+    rank = jnp.where(rank < live, before + rank, -1).astype(jnp.float32)
+    pair = lax.broadcasted_iota(jnp.int32, (N_DEV, LANES), 0).astype(jnp.float32)
+    second[...] = (owner[...] * ORB_DEV + local[...]).astype(jnp.float32)
+    for k in range(4):
+        at = slice(k * LANES, (k + 1) * LANES)
+        place[:, at] = jnp.where(pair == rank[k : k + 1], 1.0, 0.0).astype(jnp.bfloat16)
+    rows = jnp.concatenate([second[k : k + 1, :] for k in range(4)], axis=1)
+    rows = jnp.broadcast_to(rows, (LANES, 4 * LANES)).astype(jnp.bfloat16)
+    choose[...] = chosen(dot_rows(place[...], rows))
+
+
+def pick_kernel(me, place, second, choose, pieces, picked, index, mine, tall):
+    blocks = []
+    for k in range(4):
+        block = jnp.sum(pieces[8 * k : 8 * k + 8, 8].astype(jnp.float32), axis=0)
+        row = lax.broadcasted_iota(jnp.int32, (8, LANES), 0)
+        lane = lax.broadcasted_iota(jnp.int32, (8, LANES), 1)
+        orbital = (8 * (8 * k + lane // PAIR_DEV)).astype(jnp.float32)
+        block = jnp.where(row == 0, block + orbital, block)
+        blocks.append(jnp.where(row == 3, jnp.broadcast_to(second[k : k + 1, :], (8, LANES)), block))
+    facts = jnp.concatenate(blocks, axis=1)
+    first = jnp.broadcast_to(facts[0:1], (LANES, 4 * LANES)).astype(jnp.bfloat16)
+    choose_first = chosen(dot_rows(place[...], first))
+    known = dot_rows(facts.astype(jnp.bfloat16), place[...])
+    index[0:1, :] = known[0:1].astype(jnp.int32)
+    index[1:2, :] = known[3:4].astype(jnp.int32)
+    lane = lax.broadcasted_iota(jnp.int32, (8, N_DEV), 1)
+    here = jnp.sum(jnp.where(lane == me[0], known, 0.0), axis=1, keepdims=True)
+    lane = lax.broadcasted_iota(jnp.int32, (1, LANES), 1)
+    mine[...] = jnp.where(lane == 0, here[1:2], here[2:3]).astype(jnp.int32)
+    for z in range(0, 8, 2):
+        field = [
+            pieces[:, z + k].astype(jnp.float32).reshape(N_DEV, LANES).astype(jnp.bfloat16) for k in range(2)
+        ]
+        field = jnp.concatenate(field, axis=1)
+        for side, picker in enumerate((choose_first, choose[...])):
+            out = jnp.dot(picker, field, preferred_element_type=jnp.float32)
+            tall[pl.ds(8 * side + z, N_DEV, stride=16), :] = out[:, :LANES]
+            tall[pl.ds(8 * side + z + 1, N_DEV, stride=16), :] = out[:, LANES:]
+    for k in range(0, N_DEV, 8):
+        picked[k : k + 8] = tall[16 * k : 16 * k + 128, :].reshape(8, 16, LANES).astype(jnp.bfloat16)
 
 
 def shifted(tiles, start, count, flat, shift_x, shift_y):
@@ -178,7 +195,7 @@
 
 
 def solve_kernel(shift, right, left, screen, boxes, terms, moved, field, other):
-    shift_x, shift_y = shift[0], shift[1]
+    shift_x, shift_y = shift[0, 0], shift[0, 1]
     full = BOX * BOX
     ahead = (shift_x * BOX + shift_y + full) % full
     back = (full - ahead) % full
@@ -271,17 +288,17 @@
     lax.fori_loop(0, TILES // 4, pack, 0)
 
 
-def sum_kernel(firsts, listed, terms, pieces, own, carried):
+def sum_kernel(index, terms, pieces, own, carried):
     own[...] = jnp.zeros_like(own)
     carried[...] = jnp.zeros_like(carried)
 
     def step(at, carry):
+        both = terms[pl.ds(at * 8, 8)].astype(jnp.float32)
+        first = [index[0, at * 8 + k] for k in range(8)]
+        second = [index[1, at * 8 + k] for k in range(8)]
         for k in range(8):
-            d = at * 8 + k
-            both = terms[d].astype(jnp.float32)
-            first, second = firsts[d], listed[N_DEV + d]
-            own[first] = own[first] + both[:8]
-            carried[second] = carried[second] + both[8:]
+            own[first[k]] = own[first[k]] + both[k, :8]
+            carried[second[k]] = carried[second[k]] + both[k, 8:]
         return carry
 
     lax.fori_loop(0, N_DEV // 8, step, 0)
@@ -305,29 +322,26 @@
     rows = ORB_DEV * 8
     pair_shape = shape((N_DEV, 16, LANES), bf16)
     pieces = pl.pallas_call(
-        spread_kernel, out_shape=shape((N_ORB, rows + 8, LANES), bf16),
-        in_specs=[WHOLE_S, WHOLE_S, WHOLE_V], out_specs=WHOLE_V,
+        spread_kernel, out_shape=shape((N_ORB, 9, ORB_DEV, LANES), bf16),
+        in_specs=[WHOLE_V] * 3, out_specs=WHOLE_V,
+        scratch_shapes=[pltpu.VMEM((TILES * rows, LANES), f32), pltpu.VMEM((8, LANES), f32)],
         compiler_params=PARAMS, name="spread",
-    )(pair_first, pair_shift, orbitals)
+    )(pair_first.reshape(1, PAIR_DEV), pair_shift.T, orbitals)
     pieces = lax.all_to_all(pieces, "orb", split_axis=0, concat_axis=0, tiled=True)
-    listed = pl.pallas_call(
-        list_kernel, out_shape=shape((2 * N_DEV,), i32),
-        in_specs=[WHOLE_S] * 3, out_specs=WHOLE_S,
-        compiler_params=PARAMS, name="list",
-    )(pair_count, second_owner[:, 0], second_local)
-    picked, firsts, mine = pl.pallas_call(
+    place, second, choose = pl.pallas_call(
+        place_kernel,
+        out_shape=(shape((N_DEV, 4 * LANES), bf16), shape((4, LANES), f32), shape((N_DEV, N_DEV), bf16)),
+        in_specs=[WHOLE_S, WHOLE_V, WHOLE_V], out_specs=(WHOLE_V,) * 3,
+        compiler_params=PARAMS, name="place",
+    )(pair_count, second_owner.reshape(4, LANES), second_local.reshape(4, LANES))
+    picked, index, mine = pl.pallas_call(
         pick_kernel,
-        out_shape=(pair_shape, shape((N_DEV,), i32), shape((2,), i32)),
-        in_specs=[WHOLE_S, WHOLE_S, WHOLE_V],
-        out_specs=(WHOLE_V, WHOLE_S, WHOLE_S),
-        scratch_shapes=[
-            pltpu.VMEM((N_DEV, 8, LANES), f32),
-            pltpu.VMEM((N_ORB, LANES), i32),
-            pltpu.SMEM((N_ORB, LANES), i32),
-            pltpu.SemaphoreType.DMA,
-        ],
+        out_shape=(pair_shape, shape((2, N_DEV), i32), shape((1, LANES), i32)),
+        in_specs=[WHOLE_S] + [WHOLE_V] * 4,
+        out_specs=(WHOLE_V,) * 3,
+        scratch_shapes=[pltpu.VMEM((N_DEV * 16, LANES), f32)],
         compiler_params=PARAMS, name="pick",
-    )(me, listed, pieces)
+    )(me, place, second, choose, pieces)
     boxes = lax.all_to_all(picked, ("orb", "slab"), split_axis=0, concat_axis=0, tiled=True)
     right, left, screen = (jnp.asarray(table) for table in tables())
     terms = pl.pallas_call(
@@ -344,10 +358,10 @@
     terms = lax.all_to_all(terms, ("orb", "slab"), split_axis=0, concat_axis=0, tiled=True)
     pieces = pl.pallas_call(
         sum_kernel, out_shape=shape((N_ORB, rows, LANES), bf16),
-        in_specs=[WHOLE_S, WHOLE_S, WHOLE_V], out_specs=WHOLE_V,
+        in_specs=[WHOLE_S, WHOLE_V], out_specs=WHOLE_V,
         scratch_shapes=[pltpu.VMEM((N_DEV, 8, LANES), f32)] * 2,
         compiler_params=PARAMS, name="sum",
-    )(firsts, listed, terms)
+    )(index, terms)
     pieces = lax.all_to_all(pieces, "orb", split_axis=0, concat_axis=0, tiled=True)
     return pl.pallas_call(
         join_kernel, out_shape=shape((ORB_DEV, 8, BOX * BOX), bf16),

time: 149 us -> 145 us (0.973)
  Pallas kernels: 21.5 us -> 14.8 us
  waiting for transfers between devices: 14.2 us -> 16.9 us
    pallas_call x3, Pallas kernels: 9.83 us -> 2.97 us  [the longest x1 1.15 us: body(): pl.pallas_call(spread_kernel, out_shape=shape((N_ORB, 9, ORB_DEV, LANES),...]
    all_to_all x1, waiting for transfers between devices: 14.2 us -> 16.9 us  [body(): lax.all_to_all(pieces, 'orb', split_axis=0, concat_axis=0, tiled=True)]
  transfers between devices with their start and end apart: 1 -> 1, of which waited for: 1 -> 1; matrix products, arithmetic and copies ran while one was open for 0% -> 0% of each run, Pallas kernels for 2% -> 1%
where the time goes in v3:
time: 145 us; the launch traced here: 143 us
  blocking collectives  97.6 us (67%)
  waiting for transfers between devices  16.9 us (12%)
  Pallas kernels  14.8 us (10%)
  starting transfers between devices  11.5 us (8%)
  local copies, waits for them, and re-layouts  2.42 us (2%)
    all_to_all x1, blocking collectives, body(): lax.all_to_all(picked, ('orb', 'slab'), split_axis=0, concat_axis=0, tile...  39.7 us
    all_to_all x1, blocking collectives, body(): lax.all_to_all(terms, ('orb', 'slab'), split_axis=0, concat_axis=0, tiled...  37.2 us
    all_to_all x1, blocking collectives, body(): lax.all_to_all(pieces, 'orb', split_axis=0, concat_axis=0, tiled=True)  20.7 us
    all_to_all x1, waiting for transfers between devices, body(): lax.all_to_all(pieces, 'orb', split_axis=0, concat_axis=0, tiled=True)  16.9 us
    all_to_all x1, starting transfers between devices, body(): lax.all_to_all(pieces, 'orb', split_axis=0, concat_axis=0, tiled=True)  11.5 us
    pallas_call x1, Pallas kernels, body(): pl.pallas_call(solve_kernel, out_shape=pair_shape, in_specs=[WHOLE_S] + [...  8.87 us
  transfers between devices with their start and end apart: 1, of which 1 were waited for; matrix products, arithmetic and copies ran while one was open for 0% of the time, Pallas kernels for 1%

profile of v3, /device:TPU:2, one launch (start us, length us, event | category | flops | bytes accessed | tf_op | source)
XLA Modules:
  0.0 143.3 jit_solution(5172518834892054603)
XLA Ops:
  0.0 0.0 copy-start.6
  0.0 0.0 copy-start.7
  0.0 0.7 copy-done.6
  0.7 0.0 copy-done.7
  0.7 0.0 copy-start.1
  0.7 1.0 copy-done.1
  1.7 1.1 spread.1
  2.9 11.5 %all-to-all-start = ((bf16[32,9,8,128]{3,2,1,0:T(8,128)(2,1)}), bf16[32,9,8,128]{3,2,1,0:T(8,128)(2,1)S(1)}, u32[]{:S(2)}, u32[]{:S(2)}) async-start(bf16[32,9,8,128]{3,2,1,0:T(8,128)(2,1)} %spread.1), calls=%async_computation | async-start | bytes 1179648 | tf_op jit(solution)/shard_map/all_to_all | solution.py:330
  14.4 0.0 copy-start.5
  14.4 0.0 copy-start.4
  14.4 0.0 copy-start.8
  14.4 0.6 copy-done.5
  15.1 0.0 copy-done.4
  15.1 0.0 copy-done.8
  15.1 0.8 place.1
  15.9 16.9 %all-to-all-done.pieces = bf16[32,9,8,128]{3,2,1,0:T(8,128)(2,1)S(1)} async-done(((bf16[32,9,8,128]{3,2,1,0:T(8,128)(2,1)}), bf16[32,9,8,128]{3,2,1,0:T(8,128)(2,1)S(1)}, u32[]{:S(2)}, u32[]{:S(2)}) %all-to-all-start) | async-done | bytes 589856 | tf_op jit(solution)/shard_map/all_to_all | solution.py:330
  32.8 1.0 pick.1
  33.9 0.0 copy-start
  33.9 0.0 copy-start.2
  33.9 0.0 copy-start.3
  33.9 39.7 %all_to_all.20.boxes = bf16[256,16,128]{2,1,0:T(8,128)(2,1)S(1)} all-to-all(bf16[256,16,128]{2,1,0:T(8,128)(2,1)S(1)} %get-tuple-element.16), channel_id=1, replica_groups=mesh['orb'=32,'slab'=8] {'orb','slab'}, dimensions={0} | all-to-all | bytes 2097152 | tf_op jit(solution)/shard_map/all_to_all | solution.py:345
  73.5 0.0 copy-done
  73.6 0.0 copy-done.2
  73.6 0.0 copy-done.3
  73.6 8.9 %solve.1 = bf16[256,16,128]{2,1,0:T(8,128)(2,1)S(1)} custom-call(s32[1,128]{1,0:T(1,128)S(1)} %get-tuple-element.15.shift, bf16[256,256]{1,0:T(8,128)(2,1)S(1)} %copy-done.2, bf16[64,192]{1,0:T(8,128)(2,1)S(1)} %copy-done.3, f32[32,64,128]{2,1,0:T(8,128)S(1)} %copy-done, bf16[256,16,128]{2,1,0:T(8,128)(2,1)S(1)} %all_to_all.20.boxes), custom_call_target="tpu_custom_call" | custom-call | tf_op jit(solution)/shard_map/solve/pallas_call | solution.py:347
  82.4 37.2 %all_to_all.21.terms = bf16[256,16,128]{2,1,0:T(8,128)(2,1)S(1)} all-to-all(bf16[256,16,128]{2,1,0:T(8,128)(2,1)S(1)} %solve.1), channel_id=1, replica_groups=mesh['orb'=32,'slab'=8] {'orb','slab'}, dimensions={0} | all-to-all | bytes 2097152 | tf_op jit(solution)/shard_map/all_to_all | solution.py:358
  119.6 2.1 %sum.1 = bf16[32,64,128]{2,1,0:T(8,128)(2,1)S(1)} custom-call(s32[2,256]{1,0:T(2,128)S(1)} %get-tuple-element.14.index, bf16[256,16,128]{2,1,0:T(8,128)(2,1)S(1)} %all_to_all.21.terms), custom_call_target="tpu_custom_call" | custom-call | tf_op jit(solution)/shard_map/sum/pallas_call | solution.py:359
  121.7 20.7 %all_to_all.22.pieces = bf16[32,64,128]{2,1,0:T(8,128)(2,1)S(1)} all-to-all(bf16[32,64,128]{2,1,0:T(8,128)(2,1)S(1)} %sum.1), channel_id=1, replica_groups=mesh['orb'=32,'slab'=8] {'orb'}, dimensions={0} | all-to-all | bytes 1048576 | tf_op jit(solution)/shard_map/all_to_all | solution.py:365
  142.4 0.9 join.1
Async XLA Ops:
  0.0 0.7 copy-start.6
  0.0 0.7 copy-start.7
  0.7 1.0 copy-start.1
  2.9 30.0 %all-to-all-start = ((bf16[32,9,8,128]{3,2,1,0:T(8,128)(2,1)}), bf16[32,9,8,128]{3,2,1,0:T(8,128)(2,1)S(1)}, u32[]{:S(2)}, u32[]{:S(2)}) async-start(bf16[32,9,8,128]{3,2,1,0:T(8,128)(2,1)} %spread.1), calls=%async_computation | async-start | bytes 1179648 | tf_op jit(solution)/shard_map/all_to_all | solution.py:330
  14.4 0.7 copy-start.5
  14.4 0.7 copy-start.4
  14.4 0.7 copy-start.8
  33.9 39.7 %copy-start = (f32[32,64,128]{2,1,0:T(8,128)S(1)}, f32[32,64,128]{2,1,0:T(8,128)}, u32[]{:S(2)}) copy-start(f32[32,64,128]{2,1,0:T(8,128)} %constant.19.clone.screen) | copy-start | bytes 3145732
  33.9 39.7 %copy-start.2 = (bf16[256,256]{1,0:T(8,128)(2,1)S(1)}, bf16[256,256]{1,0:T(8,128)(2,1)}, u32[]{:S(2)}) copy-start(bf16[256,256]{1,0:T(8,128)(2,1)} %constant.17.clone.right) | copy-start | bytes 393220
  33.9 39.7 %copy-start.3 = (bf16[64,192]{1,0:T(8,128)(2,1)S(1)}, bf16[64,192]{1,0:T(8,128)(2,1)}, u32[]{:S(2)}) copy-start(bf16[64,192]{1,0:T(8,128)(2,1)} %constant.18.clone.left) | copy-start | bytes 73732

commit v4 on v3

--- a/solution.py
+++ b/solution.py
@@ -215,25 +215,19 @@
         )
         return product[:, :LANES] + product[:, LANES:]
 
-    def forward_y(step, carry):
-        for k, box in enumerate(shifted(second_tile, step * 4, 4, ahead, shift_x, shift_y)):
-            tile = step * 4 + k
-            moved[tile] = box
-            other[tile] = first_tile(tile) * box
-        tiles = pl.ds(step * 4, 4)
-        field[tiles] = along_y(other[tiles].reshape(4 * BOX, LANES)).reshape(4, BOX, LANES)
-        return carry
-
-    lax.fori_loop(0, TILES // 4, forward_y, 0)
-
-    def forward_x(step, carry):
-        rows = pl.ds(pl.multiple_of(step * 8, 8), 8)
-        parts = twist(fast_hartley([field[k, rows, :] for k in range(TILES)]), early)
+    for start in range(0, TILES, 4):
+        products = []
+        for k, box in enumerate(shifted(second_tile, start, 4, ahead, shift_x, shift_y)):
+            moved[start + k] = box
+            products.append(first_tile(start + k) * box)
+        block = along_y(jnp.stack(products).reshape(4 * BOX, LANES)).reshape(4, BOX, LANES)
+        for k in range(4):
+            field[start + k] = block[k]
+
+    for row in range(0, BOX, 8):
+        parts = twist(fast_hartley([field[k, row : row + 8, :] for k in range(TILES)]), early)
         for k in range(TILES):
-            field[k, rows, :] = sign * parts[k] + pltpu.roll(parts[k], BOX, 1)
-        return carry
-
-    lax.fori_loop(0, 8, forward_x, 0)
+            field[k, row : row + 8, :] = sign * parts[k] + pltpu.roll(parts[k], BOX, 1)
 
     def along_z(block):
         high, low = split(block)
@@ -241,51 +235,32 @@
             left[...], jnp.concatenate([high, low, high], axis=0), preferred_element_type=jnp.float32
         )
 
-    def screened_z(step, carry):
-        tiles = [step * 8 + k for k in range(8)]
-        blocks = [jnp.concatenate([field[tiles[k]], field[tiles[k + 1]]], axis=1) for k in range(0, 8, 2)]
-        blocks = [along_z(block) for block in blocks]
-        for k in range(8):
-            half = slice(k % 2 * LANES, (k % 2 + 1) * LANES)
-            field[tiles[k]] = blocks[k // 2][:, half] * screen[tiles[k]]
-        blocks = [jnp.concatenate([field[tiles[k]], field[tiles[k + 1]]], axis=1) for k in range(0, 8, 2)]
-        blocks = [along_z(block) for block in blocks]
-        for k in range(8):
-            half = slice(k % 2 * LANES, (k % 2 + 1) * LANES)
-            field[tiles[k]] = blocks[k // 2][:, half]
-        return carry
-
-    lax.fori_loop(0, TILES // 8, screened_z, 0)
-
-    def inverse_x(step, carry):
-        rows = pl.ds(pl.multiple_of(step * 8, 8), 8)
-        parts = [field[k, rows, :] for k in range(TILES)]
+    for tile in range(0, TILES, 2):
+        block = along_z(jnp.concatenate([field[tile], field[tile + 1]], axis=1))
+        block = block * jnp.concatenate([screen[tile], screen[tile + 1]], axis=1)
+        block = along_z(block)
+        field[tile] = block[:, :LANES]
+        field[tile + 1] = block[:, LANES:]
+
+    for row in range(0, BOX, 8):
+        parts = [field[k, row : row + 8, :] for k in range(TILES)]
         parts = [sign * part + pltpu.roll(part, BOX, 1) for part in parts]
         parts = fast_hartley(untwist(parts, early))
         for k in range(TILES):
-            field[k, rows, :] = parts[k]
-        return carry
-
-    lax.fori_loop(0, 8, inverse_x, 0)
-
-    def inverse_y(step, carry):
-        tiles = pl.ds(step * 4, 4)
-        potential = along_y(field[tiles].reshape(4 * BOX, LANES)).reshape(4, 8, 8, LANES)
+            field[k, row : row + 8, :] = parts[k]
+
+    for start in range(0, TILES, 4):
+        block = field[start : start + 4].reshape(4 * BOX, LANES)
+        potential = along_y(block).reshape(4, 8, 8, LANES)
         for k in range(4):
-            other[step * 4 + k] = potential[k] * first_tile(step * 4 + k)
-            moved[step * 4 + k] = potential[k] * moved[step * 4 + k]
-        return carry
-
-    lax.fori_loop(0, TILES // 4, inverse_y, 0)
-
-    def pack(step, carry):
-        carried = shifted(lambda tile: other[tile], step * 4, 4, back, -shift_x, -shift_y)
+            other[start + k] = potential[k] * first_tile(start + k)
+            moved[start + k] = potential[k] * moved[start + k]
+
+    for start in range(0, TILES, 4):
+        carried = shifted(lambda tile: other[tile], start, 4, back, -shift_x, -shift_y)
         for k in range(4):
-            both = jnp.concatenate([moved[step * 4 + k], carried[k]], axis=1)
-            terms[pl.ds((step * 4 + k) * 8, 8)] = both.astype(jnp.bfloat16)
-        return carry
-
-    lax.fori_loop(0, TILES // 4, pack, 0)
+            both = jnp.concatenate([moved[start + k], carried[k]], axis=1)
+            terms[(start + k) * 8 : (start + k + 1) * 8] = both.astype(jnp.bfloat16)
 
 
 def sum_kernel(index, terms, pieces, own, carried):

time: 145 us -> 139 us (0.959)
  Pallas kernels: 14.8 us -> 9.3 us
    pallas_call x1, Pallas kernels: 8.87 us -> 3.41 us  [body(): pl.pallas_call(solve_kernel, out_shape=pair_shape, in_specs=[WHOLE_S] + [...]
where the time goes in v4:
time: 139 us; the launch traced here: 138 us
  blocking collectives  97.6 us (70%)
  waiting for transfers between devices  16.9 us (12%)
  starting transfers between devices  11.5 us (8%)
  Pallas kernels  9.3 us (7%)
  local copies, waits for them, and re-layouts  2.42 us (2%)
    all_to_all x1, blocking collectives, body(): lax.all_to_all(picked, ('orb', 'slab'), split_axis=0, concat_axis=0, tile...  39.7 us
    all_to_all x1, blocking collectives, body(): lax.all_to_all(terms, ('orb', 'slab'), split_axis=0, concat_axis=0, tiled...  37.2 us
    all_to_all x1, blocking collectives, body(): lax.all_to_all(pieces, 'orb', split_axis=0, concat_axis=0, tiled=True)  20.7 us
    all_to_all x1, waiting for transfers between devices, body(): lax.all_to_all(pieces, 'orb', split_axis=0, concat_axis=0, tiled=True)  16.9 us
    all_to_all x1, starting transfers between devices, body(): lax.all_to_all(pieces, 'orb', split_axis=0, concat_axis=0, tiled=True)  11.5 us
    pallas_call x1, Pallas kernels, body(): pl.pallas_call(solve_kernel, out_shape=pair_shape, in_specs=[WHOLE_S] + [...  3.41 us
  transfers between devices with their start and end apart: 1, of which 1 were waited for; matrix products, arithmetic and copies ran while one was open for 0% of the time, Pallas kernels for 1%

profile of v4, /device:TPU:2, one launch (start us, length us, event | category | flops | bytes accessed | tf_op | source)
XLA Modules:
  0.0 137.8 jit_solution(15833392495738488743)
XLA Ops:
  0.0 0.0 copy-start.6
  0.0 0.0 copy-start.7
  0.0 0.7 copy-done.6
  0.7 0.0 copy-done.7
  0.7 0.0 copy-start.1
  0.7 1.0 copy-done.1
  1.7 1.1 spread.1
  2.9 11.5 %all-to-all-start = ((bf16[32,9,8,128]{3,2,1,0:T(8,128)(2,1)}), bf16[32,9,8,128]{3,2,1,0:T(8,128)(2,1)S(1)}, u32[]{:S(2)}, u32[]{:S(2)}) async-start(bf16[32,9,8,128]{3,2,1,0:T(8,128)(2,1)} %spread.1), calls=%async_computation | async-start | bytes 1179648 | tf_op jit(solution)/shard_map/all_to_all | solution.py:305
  14.4 0.0 copy-start.5
  14.4 0.0 copy-start.4
  14.4 0.0 copy-start.8
  14.4 0.6 copy-done.5
  15.1 0.0 copy-done.4
  15.1 0.0 copy-done.8
  15.1 0.8 place.1
  15.9 16.9 %all-to-all-done.pieces = bf16[32,9,8,128]{3,2,1,0:T(8,128)(2,1)S(1)} async-done(((bf16[32,9,8,128]{3,2,1,0:T(8,128)(2,1)}), bf16[32,9,8,128]{3,2,1,0:T(8,128)(2,1)S(1)}, u32[]{:S(2)}, u32[]{:S(2)}) %all-to-all-start) | async-done | bytes 589856 | tf_op jit(solution)/shard_map/all_to_all | solution.py:305
  32.8 1.0 pick.1
  33.9 0.0 copy-start
  33.9 0.0 copy-start.2
  33.9 0.0 copy-start.3
  33.9 39.7 %all_to_all.20.boxes = bf16[256,16,128]{2,1,0:T(8,128)(2,1)S(1)} all-to-all(bf16[256,16,128]{2,1,0:T(8,128)(2,1)S(1)} %get-tuple-element.16), channel_id=1, replica_groups=mesh['orb'=32,'slab'=8] {'orb','slab'}, dimensions={0} | all-to-all | bytes 2097152 | tf_op jit(solution)/shard_map/all_to_all | solution.py:320
  73.5 0.0 copy-done
  73.6 0.0 copy-done.2
  73.6 0.0 copy-done.3
  73.6 3.4 %solve.1 = bf16[256,16,128]{2,1,0:T(8,128)(2,1)S(1)} custom-call(s32[1,128]{1,0:T(1,128)S(1)} %get-tuple-element.15.shift, bf16[256,256]{1,0:T(8,128)(2,1)S(1)} %copy-done.2, bf16[64,192]{1,0:T(8,128)(2,1)S(1)} %copy-done.3, f32[32,64,128]{2,1,0:T(8,128)S(1)} %copy-done, bf16[256,16,128]{2,1,0:T(8,128)(2,1)S(1)} %all_to_all.20.boxes), custom_call_target="tpu_custom_call" | custom-call | tf_op jit(solution)/shard_map/solve/pallas_call | solution.py:322
  77.0 37.2 %all_to_all.21.terms = bf16[256,16,128]{2,1,0:T(8,128)(2,1)S(1)} all-to-all(bf16[256,16,128]{2,1,0:T(8,128)(2,1)S(1)} %solve.1), channel_id=1, replica_groups=mesh['orb'=32,'slab'=8] {'orb','slab'}, dimensions={0} | all-to-all | bytes 2097152 | tf_op jit(solution)/shard_map/all_to_all | solution.py:333
  114.2 2.1 %sum.1 = bf16[32,64,128]{2,1,0:T(8,128)(2,1)S(1)} custom-call(s32[2,256]{1,0:T(2,128)S(1)} %get-tuple-element.14.index, bf16[256,16,128]{2,1,0:T(8,128)(2,1)S(1)} %all_to_all.21.terms), custom_call_target="tpu_custom_call" | custom-call | tf_op jit(solution)/shard_map/sum/pallas_call | solution.py:334
  116.2 20.7 %all_to_all.22.pieces = bf16[32,64,128]{2,1,0:T(8,128)(2,1)S(1)} all-to-all(bf16[32,64,128]{2,1,0:T(8,128)(2,1)S(1)} %sum.1), channel_id=1, replica_groups=mesh['orb'=32,'slab'=8] {'orb'}, dimensions={0} | all-to-all | bytes 1048576 | tf_op jit(solution)/shard_map/all_to_all | solution.py:340
  136.9 0.9 join.1
Async XLA Ops:
  0.0 0.7 copy-start.6
  0.0 0.7 copy-start.7
  0.7 1.0 copy-start.1
  2.9 30.0 %all-to-all-start = ((bf16[32,9,8,128]{3,2,1,0:T(8,128)(2,1)}), bf16[32,9,8,128]{3,2,1,0:T(8,128)(2,1)S(1)}, u32[]{:S(2)}, u32[]{:S(2)}) async-start(bf16[32,9,8,128]{3,2,1,0:T(8,128)(2,1)} %spread.1), calls=%async_computation | async-start | bytes 1179648 | tf_op jit(solution)/shard_map/all_to_all | solution.py:305
  14.4 0.7 copy-start.5
  14.4 0.7 copy-start.4
  14.4 0.7 copy-start.8
  33.9 39.7 %copy-start = (f32[32,64,128]{2,1,0:T(8,128)S(1)}, f32[32,64,128]{2,1,0:T(8,128)}, u32[]{:S(2)}) copy-start(f32[32,64,128]{2,1,0:T(8,128)} %constant.19.clone.screen) | copy-start | bytes 3145732
  33.9 39.7 %copy-start.2 = (bf16[256,256]{1,0:T(8,128)(2,1)S(1)}, bf16[256,256]{1,0:T(8,128)(2,1)}, u32[]{:S(2)}) copy-start(bf16[256,256]{1,0:T(8,128)(2,1)} %constant.17.clone.right) | copy-start | bytes 393220
  33.9 39.7 %copy-start.3 = (bf16[64,192]{1,0:T(8,128)(2,1)S(1)}, bf16[64,192]{1,0:T(8,128)(2,1)}, u32[]{:S(2)}) copy-start(bf16[64,192]{1,0:T(8,128)(2,1)} %constant.18.clone.left) | copy-start | bytes 73732

commit v5 on v4

--- a/solution.py
+++ b/solution.py
@@ -16,8 +16,10 @@
 TILES = 32
 LANES = 128
 SCREENING = 0.02
+GROUPS = 4
 PARAMS = pltpu.CompilerParams(vmem_limit_bytes=48 * 1024 * 1024)
 WHOLE_V = pl.BlockSpec(memory_space=pltpu.VMEM)
+WHOLE_H = pl.BlockSpec(memory_space=pltpu.HBM)
 WHOLE_S = pl.BlockSpec(memory_space=pltpu.SMEM)
 
 
@@ -99,21 +101,43 @@
     return out
 
 
-def spread_kernel(first, shift, orbitals, pieces, tall, about):
-    for orbital in range(ORB_DEV):
-        box = orbitals[orbital].astype(jnp.float32)
-        for tile in range(TILES):
-            row = tile * ORB_DEV * 8 + 8 * orbital
-            tall[row : row + 8, :] = box[:, tile * LANES : (tile + 1) * LANES]
+def spread_kernel(first, shift, orbitals, pieces, taken, tall, small, about, packed, arrived, sent):
+    few = [
+        pltpu.make_async_copy(first, small.at[0:1], arrived.at[GROUPS]),
+        pltpu.make_async_copy(shift, small.at[8:10], arrived.at[GROUPS + 1]),
+    ]
+    width = BOX * BOX // GROUPS
+    many = [
+        pltpu.make_async_copy(orbitals.at[:, :, pl.ds(k * width, width)], taken.at[k], arrived.at[k])
+        for k in range(GROUPS)
+    ]
+    for copy in few + many:
+        copy.start()
     about[...] = jnp.zeros_like(about)
-    about[0:1, :PAIR_DEV] = first[...].astype(jnp.float32)
-    about[1:3, :PAIR_DEV] = shift[...].astype(jnp.float32)
+    for copy in few:
+        copy.wait()
+    about[0:1, :PAIR_DEV] = small[0:1, :].astype(jnp.float32)
+    about[1:3, :PAIR_DEV] = small[8:10, :].astype(jnp.float32)
     placed = pltpu.roll(about[...], lax.axis_index("orb") % 8 * PAIR_DEV, 1).astype(jnp.bfloat16)
-    for tile in range(TILES):
-        for z in range(8):
-            row = tile * ORB_DEV * 8 + z
-            pieces[tile, z] = tall[pl.ds(row, ORB_DEV, stride=8), :].astype(jnp.bfloat16)
-        pieces[tile, 8] = placed
+    inside = TILES // GROUPS
+    out = []
+    for k in range(GROUPS):
+        many[k].wait()
+        for orbital in range(ORB_DEV):
+            box = taken[k, orbital].astype(jnp.float32)
+            for tile in range(inside):
+                row = (k * inside + tile) * ORB_DEV * 8 + 8 * orbital
+                tall[row : row + 8, :] = box[:, tile * LANES : (tile + 1) * LANES]
+        for tile in range(k * inside, (k + 1) * inside):
+            for z in range(8):
+                row = tile * ORB_DEV * 8 + z
+                packed[tile, z] = tall[pl.ds(row, ORB_DEV, stride=8), :].astype(jnp.bfloat16)
+            packed[tile, 8] = placed
+        at = pl.ds(k * inside, inside)
+        out.append(pltpu.make_async_copy(packed.at[at], pieces.at[at], sent.at[k]))
+        out[k].start()
+    for copy in out:
+        copy.wait()
 
 
 def dot_rows(one, two):
@@ -263,23 +287,24 @@
             terms[(start + k) * 8 : (start + k + 1) * 8] = both.astype(jnp.bfloat16)
 
 
-def sum_kernel(index, terms, pieces, own, carried):
-    own[...] = jnp.zeros_like(own)
-    carried[...] = jnp.zeros_like(carried)
-
-    def step(at, carry):
-        both = terms[pl.ds(at * 8, 8)].astype(jnp.float32)
-        first = [index[0, at * 8 + k] for k in range(8)]
-        second = [index[1, at * 8 + k] for k in range(8)]
-        for k in range(8):
-            own[first[k]] = own[first[k]] + both[k, :8]
-            carried[second[k]] = carried[second[k]] + both[k, 8:]
-        return carry
-
-    lax.fori_loop(0, N_DEV // 8, step, 0)
+def sum_kernel(index, terms, pieces, tall, summed):
+    for k in range(0, N_DEV, 8):
+        tall[16 * k : 16 * k + 128, :] = terms[k : k + 8].astype(jnp.float32).reshape(128, LANES)
+    orbital = lax.broadcasted_iota(jnp.int32, (N_DEV, N_DEV), 0)
+    hits = [jnp.where(orbital == index[side : side + 1, :], 1.0, 0.0) for side in range(2)]
+    hits = jnp.concatenate(hits, axis=1).astype(jnp.bfloat16)
+    for z in range(0, 8, 2):
+        field = [
+            jnp.concatenate(
+                [tall[pl.ds(8 * side + z + k, N_DEV, stride=16), :] for side in range(2)], axis=0
+            ).astype(jnp.bfloat16)
+            for k in range(2)
+        ]
+        out = jnp.dot(hits, jnp.concatenate(field, axis=1), preferred_element_type=jnp.float32)
+        summed[pl.ds(z, N_DEV, stride=8), :] = out[:, :LANES]
+        summed[pl.ds(z + 1, N_DEV, stride=8), :] = out[:, LANES:]
     for e in range(N_ORB):
-        at = slice(e * ORB_DEV, (e + 1) * ORB_DEV)
-        pieces[e] = (own[at] + carried[at]).reshape(ORB_DEV * 8, LANES).astype(jnp.bfloat16)
+        pieces[e] = summed[e * ORB_DEV * 8 : (e + 1) * ORB_DEV * 8, :].astype(jnp.bfloat16)
 
 
 def join_kernel(pieces, result):
@@ -298,9 +323,17 @@
     pair_shape = shape((N_DEV, 16, LANES), bf16)
     pieces = pl.pallas_call(
         spread_kernel, out_shape=shape((N_ORB, 9, ORB_DEV, LANES), bf16),
-        in_specs=[WHOLE_V] * 3, out_specs=WHOLE_V,
-        scratch_shapes=[pltpu.VMEM((TILES * rows, LANES), f32), pltpu.VMEM((8, LANES), f32)],
-        compiler_params=PARAMS, name="spread",
+        in_specs=[WHOLE_H] * 3, out_specs=WHOLE_H,
+        scratch_shapes=[
+            pltpu.VMEM((GROUPS, ORB_DEV, 8, BOX * BOX // GROUPS), bf16),
+            pltpu.VMEM((TILES * rows, LANES), f32),
+            pltpu.VMEM((16, PAIR_DEV), i32),
+            pltpu.VMEM((8, LANES), f32),
+            pltpu.VMEM((N_ORB, 9, ORB_DEV, LANES), bf16),
+            pltpu.SemaphoreType.DMA((GROUPS + 2,)),
+            pltpu.SemaphoreType.DMA((GROUPS,)),
+        ],
+        compiler_params=pltpu.CompilerParams(vmem_limit_bytes=60 * 1024 * 1024), name="spread",
     )(pair_first.reshape(1, PAIR_DEV), pair_shift.T, orbitals)
     pieces = lax.all_to_all(pieces, "orb", split_axis=0, concat_axis=0, tiled=True)
     place, second, choose = pl.pallas_call(
@@ -333,8 +366,8 @@
     terms = lax.all_to_all(terms, ("orb", "slab"), split_axis=0, concat_axis=0, tiled=True)
     pieces = pl.pallas_call(
         sum_kernel, out_shape=shape((N_ORB, rows, LANES), bf16),
-        in_specs=[WHOLE_S, WHOLE_V], out_specs=WHOLE_V,
-        scratch_shapes=[pltpu.VMEM((N_DEV, 8, LANES), f32)] * 2,
+        in_specs=[WHOLE_V, WHOLE_V], out_specs=WHOLE_V,
+        scratch_shapes=[pltpu.VMEM((N_DEV * 16, LANES), f32), pltpu.VMEM((N_DEV * 8, LANES), f32)],
         compiler_params=PARAMS, name="sum",
     )(index, terms)
     pieces = lax.all_to_all(pieces, "orb", split_axis=0, concat_axis=0, tiled=True)

time: 139 us -> 137 us (0.986)
  local copies, waits for them, and re-layouts: 2.42 us -> 0.7 us
    unnamed x18 -> x12, local copies, waits for them, and re-layouts: 2.42 us -> 0.7 us
where the time goes in v5:
time: 137 us; the launch traced here: 136 us
  blocking collectives  97.6 us (71%)
  waiting for transfers between devices  16.9 us (12%)
  starting transfers between devices  11.5 us (8%)
  Pallas kernels  9.23 us (7%)
    all_to_all x1, blocking collectives, body(): lax.all_to_all(picked, ('orb', 'slab'), split_axis=0, concat_axis=0, tile...  39.7 us
    all_to_all x1, blocking collectives, body(): lax.all_to_all(terms, ('orb', 'slab'), split_axis=0, concat_axis=0, tiled...  37.2 us
    all_to_all x1, blocking collectives, body(): lax.all_to_all(pieces, 'orb', split_axis=0, concat_axis=0, tiled=True)  20.7 us
    all_to_all x1, waiting for transfers between devices, body(): lax.all_to_all(pieces, 'orb', split_axis=0, concat_axis=0, tiled=True)  16.9 us
    all_to_all x1, starting transfers between devices, body(): lax.all_to_all(pieces, 'orb', split_axis=0, concat_axis=0, tiled=True)  11.5 us
    pallas_call x1, Pallas kernels, body(): pl.pallas_call(solve_kernel, out_shape=pair_shape, in_specs=[WHOLE_S] + [...  3.45 us
  transfers between devices with their start and end apart: 1, of which 1 were waited for; matrix products, arithmetic and copies ran while one was open for 0% of the time, Pallas kernels for 1%

profile of v5, /device:TPU:2, one launch (start us, length us, event | category | flops | bytes accessed | tf_op | source)
XLA Modules:
  0.0 136.0 jit_solution(17119184689655505338)
XLA Ops:
  0.0 2.0 %spread.1 = bf16[32,9,8,128]{3,2,1,0:T(8,128)(2,1)} custom-call(s32[1,16]{1,0:T(1,128)} %bitcast.8, s32[2,16]{1,0:T(2,128)} %bitcast.7, bf16[8,8,4096]{2,1,0:T(8,128)(2,1)} %orbitals.1), custom_call_target="tpu_custom_call" | custom-call | tf_op jit(solution)/shard_map/spread/pallas_call | solution.py:324
  2.0 11.5 %all-to-all-start = ((bf16[32,9,8,128]{3,2,1,0:T(8,128)(2,1)}), bf16[32,9,8,128]{3,2,1,0:T(8,128)(2,1)S(1)}, u32[]{:S(2)}, u32[]{:S(2)}) async-start(bf16[32,9,8,128]{3,2,1,0:T(8,128)(2,1)} %spread.1), calls=%async_computation | async-start | bytes 1179648 | tf_op jit(solution)/shard_map/all_to_all | solution.py:338
  13.5 0.0 copy-start.4
  13.5 0.0 copy-start.3
  13.5 0.0 copy-start.5
  13.5 0.6 copy-done.4
  14.2 0.0 copy-done.3
  14.2 0.0 copy-done.5
  14.2 0.8 place.1
  15.0 16.9 %all-to-all-done.pieces = bf16[32,9,8,128]{3,2,1,0:T(8,128)(2,1)S(1)} async-done(((bf16[32,9,8,128]{3,2,1,0:T(8,128)(2,1)}), bf16[32,9,8,128]{3,2,1,0:T(8,128)(2,1)S(1)}, u32[]{:S(2)}, u32[]{:S(2)}) %all-to-all-start) | async-done | bytes 589856 | tf_op jit(solution)/shard_map/all_to_all | solution.py:338
  31.9 1.0 pick.1
  33.0 0.0 copy-start
  33.0 0.0 copy-start.1
  33.0 0.0 copy-start.2
  33.0 39.7 %all_to_all.20.boxes = bf16[256,16,128]{2,1,0:T(8,128)(2,1)S(1)} all-to-all(bf16[256,16,128]{2,1,0:T(8,128)(2,1)S(1)} %get-tuple-element.16), channel_id=1, replica_groups=mesh['orb'=32,'slab'=8] {'orb','slab'}, dimensions={0} | all-to-all | bytes 2097152 | tf_op jit(solution)/shard_map/all_to_all | solution.py:353
  72.7 0.0 copy-done
  72.7 0.0 copy-done.1
  72.7 0.0 copy-done.2
  72.7 3.4 %solve.1 = bf16[256,16,128]{2,1,0:T(8,128)(2,1)S(1)} custom-call(s32[1,128]{1,0:T(1,128)S(1)} %get-tuple-element.15.shift, bf16[256,256]{1,0:T(8,128)(2,1)S(1)} %copy-done.1, bf16[64,192]{1,0:T(8,128)(2,1)S(1)} %copy-done.2, f32[32,64,128]{2,1,0:T(8,128)S(1)} %copy-done, bf16[256,16,128]{2,1,0:T(8,128)(2,1)S(1)} %all_to_all.20.boxes), custom_call_target="tpu_custom_call" | custom-call | tf_op jit(solution)/shard_map/solve/pallas_call | solution.py:355
  76.1 37.2 %all_to_all.21.terms = bf16[256,16,128]{2,1,0:T(8,128)(2,1)S(1)} all-to-all(bf16[256,16,128]{2,1,0:T(8,128)(2,1)S(1)} %solve.1), channel_id=1, replica_groups=mesh['orb'=32,'slab'=8] {'orb','slab'}, dimensions={0} | all-to-all | bytes 2097152 | tf_op jit(solution)/shard_map/all_to_all | solution.py:366
  113.3 1.1 sum.1
  114.5 20.7 %all_to_all.22.pieces = bf16[32,64,128]{2,1,0:T(8,128)(2,1)S(1)} all-to-all(bf16[32,64,128]{2,1,0:T(8,128)(2,1)S(1)} %sum.1), channel_id=1, replica_groups=mesh['orb'=32,'slab'=8] {'orb'}, dimensions={0} | all-to-all | bytes 1048576 | tf_op jit(solution)/shard_map/all_to_all | solution.py:373
  135.2 0.9 join.1
Async XLA Ops:
  2.0 30.0 %all-to-all-start = ((bf16[32,9,8,128]{3,2,1,0:T(8,128)(2,1)}), bf16[32,9,8,128]{3,2,1,0:T(8,128)(2,1)S(1)}, u32[]{:S(2)}, u32[]{:S(2)}) async-start(bf16[32,9,8,128]{3,2,1,0:T(8,128)(2,1)} %spread.1), calls=%async_computation | async-start | bytes 1179648 | tf_op jit(solution)/shard_map/all_to_all | solution.py:338
  13.5 0.7 copy-start.4
  13.5 0.7 copy-start.3
  13.5 0.7 copy-start.5
  33.0 39.7 %copy-start = (f32[32,64,128]{2,1,0:T(8,128)S(1)}, f32[32,64,128]{2,1,0:T(8,128)}, u32[]{:S(2)}) copy-start(f32[32,64,128]{2,1,0:T(8,128)} %constant.19.clone.screen) | copy-start | bytes 3145732
  33.0 39.7 %copy-start.1 = (bf16[256,256]{1,0:T(8,128)(2,1)S(1)}, bf16[256,256]{1,0:T(8,128)(2,1)}, u32[]{:S(2)}) copy-start(bf16[256,256]{1,0:T(8,128)(2,1)} %constant.17.clone.right) | copy-start | bytes 393220
  33.0 39.7 %copy-start.2 = (bf16[64,192]{1,0:T(8,128)(2,1)S(1)}, bf16[64,192]{1,0:T(8,128)(2,1)}, u32[]{:S(2)}) copy-start(bf16[64,192]{1,0:T(8,128)(2,1)} %constant.18.clone.left) | copy-start | bytes 73732

commit v6 on v5

--- a/solution.py
+++ b/solution.py
@@ -227,10 +227,10 @@
     sign = jnp.where(early, 1.0, -1.0)
 
     def first_tile(tile):
-        return boxes[pl.ds(tile * 8, 8), :8, :].astype(jnp.float32)
+        return boxes[:, tile, :8, :].astype(jnp.float32)
 
     def second_tile(tile):
-        return boxes[pl.ds(tile * 8, 8), 8:, :].astype(jnp.float32)
+        return boxes[:, tile, 8:, :].astype(jnp.float32)
 
     def along_y(block):
         high, low = split(block)
@@ -284,7 +284,7 @@
         carried = shifted(lambda tile: other[tile], start, 4, back, -shift_x, -shift_y)
         for k in range(4):
             both = jnp.concatenate([moved[start + k], carried[k]], axis=1)
-            terms[(start + k) * 8 : (start + k + 1) * 8] = both.astype(jnp.bfloat16)
+            terms[:, start + k] = both.astype(jnp.bfloat16)
 
 
 def sum_kernel(index, terms, pieces, tall, summed):
@@ -318,7 +318,7 @@
 def body(orbitals, pair_first, second_owner, second_local, pair_shift, pair_count):
     f32, bf16, i32 = jnp.float32, jnp.bfloat16, jnp.int32
     shape = jax.ShapeDtypeStruct
-    me = (lax.axis_index("orb") * 8 + lax.axis_index("slab")).reshape(1)
+    me = (lax.axis_index("slab") * N_ORB + lax.axis_index("orb")).reshape(1)
     rows = ORB_DEV * 8
     pair_shape = shape((N_DEV, 16, LANES), bf16)
     pieces = pl.pallas_call(
@@ -350,10 +350,10 @@
         scratch_shapes=[pltpu.VMEM((N_DEV * 16, LANES), f32)],
         compiler_params=PARAMS, name="pick",
     )(me, place, second, choose, pieces)
-    boxes = lax.all_to_all(picked, ("orb", "slab"), split_axis=0, concat_axis=0, tiled=True)
+    boxes = lax.all_to_all(picked, ("slab", "orb"), split_axis=0, concat_axis=0, tiled=True)
     right, left, screen = (jnp.asarray(table) for table in tables())
     terms = pl.pallas_call(
-        solve_kernel, out_shape=pair_shape,
+        solve_kernel, out_shape=shape((8, TILES, 16, LANES), bf16),
         in_specs=[WHOLE_S] + [WHOLE_V] * 4,
         out_specs=WHOLE_V,
         scratch_shapes=[
@@ -362,8 +362,9 @@
             pltpu.VMEM((TILES, 8, 8, LANES), f32),
         ],
         compiler_params=PARAMS, name="solve",
-    )(mine, right, left, screen, boxes)
-    terms = lax.all_to_all(terms, ("orb", "slab"), split_axis=0, concat_axis=0, tiled=True)
+    )(mine, right, left, screen, boxes.reshape(8, TILES, 16, LANES))
+    terms = terms.reshape(N_DEV, 16, LANES)
+    terms = lax.all_to_all(terms, ("slab", "orb"), split_axis=0, concat_axis=0, tiled=True)
     pieces = pl.pallas_call(
         sum_kernel, out_shape=shape((N_ORB, rows, LANES), bf16),
         in_specs=[WHOLE_V, WHOLE_V], out_specs=WHOLE_V,

time: 137 us -> 138 us (level)
  no operation moved by 1% of the time
where the time goes in v6:
time: 138 us; the launch traced here: 136 us
  blocking collectives  97.8 us (71%)
  waiting for transfers between devices  16.9 us (12%)
  starting transfers between devices  11.5 us (8%)
  Pallas kernels  9.23 us (7%)
    all_to_all x1, blocking collectives, body(): lax.all_to_all(picked, ('slab', 'orb'), split_axis=0, concat_axis=0, tile...  39.3 us
    all_to_all x1, blocking collectives, body(): lax.all_to_all(terms, ('slab', 'orb'), split_axis=0, concat_axis=0, tiled...  37.5 us
    all_to_all x1, blocking collectives, body(): lax.all_to_all(pieces, 'orb', split_axis=0, concat_axis=0, tiled=True)  21 us
    all_to_all x1, waiting for transfers between devices, body(): lax.all_to_all(pieces, 'orb', split_axis=0, concat_axis=0, tiled=True)  16.9 us
    all_to_all x1, starting transfers between devices, body(): lax.all_to_all(pieces, 'orb', split_axis=0, concat_axis=0, tiled=True)  11.5 us
    pallas_call x1, Pallas kernels, body(): pl.pallas_call(solve_kernel, out_shape=shape((8, TILES, 16, LANES), bf16)...  3.45 us
  transfers between devices with their start and end apart: 1, of which 1 were waited for; matrix products, arithmetic and copies ran while one was open for 0% of the time, Pallas kernels for 1%

profile of v6, /device:TPU:2, one launch (start us, length us, event | category | flops | bytes accessed | tf_op | source)
XLA Modules:
  0.0 136.3 jit_solution(6392499369326034822)
XLA Ops:
  0.0 2.0 %spread.1 = bf16[32,9,8,128]{3,2,1,0:T(8,128)(2,1)} custom-call(s32[1,16]{1,0:T(1,128)} %bitcast.12, s32[2,16]{1,0:T(2,128)} %bitcast.11, bf16[8,8,4096]{2,1,0:T(8,128)(2,1)} %orbitals.1), custom_call_target="tpu_custom_call" | custom-call | tf_op jit(solution)/shard_map/spread/pallas_call | solution.py:324
  2.0 11.5 %all-to-all-start = ((bf16[32,9,8,128]{3,2,1,0:T(8,128)(2,1)}), bf16[32,9,8,128]{3,2,1,0:T(8,128)(2,1)S(1)}, u32[]{:S(2)}, u32[]{:S(2)}) async-start(bf16[32,9,8,128]{3,2,1,0:T(8,128)(2,1)} %spread.1), calls=%async_computation | async-start | bytes 1179648 | tf_op jit(solution)/shard_map/all_to_all | solution.py:338
  13.5 0.0 copy-start.4
  13.5 0.0 copy-start.3
  13.5 0.0 copy-start.5
  13.5 0.6 copy-done.4
  14.2 0.0 copy-done.3
  14.2 0.0 copy-done.5
  14.2 0.8 place.1
  15.0 16.9 %all-to-all-done.pieces = bf16[32,9,8,128]{3,2,1,0:T(8,128)(2,1)S(1)} async-done(((bf16[32,9,8,128]{3,2,1,0:T(8,128)(2,1)}), bf16[32,9,8,128]{3,2,1,0:T(8,128)(2,1)S(1)}, u32[]{:S(2)}, u32[]{:S(2)}) %all-to-all-start) | async-done | bytes 589856 | tf_op jit(solution)/shard_map/all_to_all | solution.py:338
  31.9 1.0 pick.1
  33.0 0.0 copy-start
  33.0 0.0 copy-start.1
  33.0 0.0 copy-start.2
  33.0 39.3 %all_to_all.20 = bf16[256,16,128]{2,1,0:T(8,128)(2,1)S(1)} all-to-all(bf16[256,16,128]{2,1,0:T(8,128)(2,1)S(1)} %get-tuple-element.16), channel_id=1, replica_groups=mesh['orb'=32,'slab'=8] {'slab','orb'}, dimensions={0} | all-to-all | bytes 2097152 | tf_op jit(solution)/shard_map/all_to_all | solution.py:353
  72.3 0.0 copy-done
  72.3 0.0 copy-done.1
  72.3 0.0 copy-done.2
  72.3 3.4 %solve.1 = bf16[8,32,16,128]{3,2,1,0:T(8,128)(2,1)S(1)} custom-call(s32[1,128]{1,0:T(1,128)S(1)} %get-tuple-element.15.shift, bf16[256,256]{1,0:T(8,128)(2,1)S(1)} %copy-done.1, bf16[64,192]{1,0:T(8,128)(2,1)S(1)} %copy-done.2, f32[32,64,128]{2,1,0:T(8,128)S(1)} %copy-done, bf16[8,32,16,128]{3,2,1,0:T(8,128)(2,1)S(1)} %bitcast.7), custom_call_target="tpu_custom_call" | custom-call | tf_op jit(solution)/shard_map/solve/pallas_call | solution.py:355
  75.8 37.5 %all_to_all.21.terms = bf16[256,16,128]{2,1,0:T(8,128)(2,1)S(1)} all-to-all(bf16[256,16,128]{2,1,0:T(8,128)(2,1)S(1)} %bitcast.8), channel_id=1, replica_groups=mesh['orb'=32,'slab'=8] {'slab','orb'}, dimensions={0} | all-to-all | bytes 2097152 | tf_op jit(solution)/shard_map/all_to_all | solution.py:367
  113.3 1.1 sum.1
  114.4 21.0 %all_to_all.22.pieces = bf16[32,64,128]{2,1,0:T(8,128)(2,1)S(1)} all-to-all(bf16[32,64,128]{2,1,0:T(8,128)(2,1)S(1)} %sum.1), channel_id=1, replica_groups=mesh['orb'=32,'slab'=8] {'orb'}, dimensions={0} | all-to-all | bytes 1048576 | tf_op jit(solution)/shard_map/all_to_all | solution.py:374
  135.4 0.9 join.1
Async XLA Ops:
  2.0 30.0 %all-to-all-start = ((bf16[32,9,8,128]{3,2,1,0:T(8,128)(2,1)}), bf16[32,9,8,128]{3,2,1,0:T(8,128)(2,1)S(1)}, u32[]{:S(2)}, u32[]{:S(2)}) async-start(bf16[32,9,8,128]{3,2,1,0:T(8,128)(2,1)} %spread.1), calls=%async_computation | async-start | bytes 1179648 | tf_op jit(solution)/shard_map/all_to_all | solution.py:338
  13.5 0.7 copy-start.4
  13.5 0.7 copy-start.3
  13.5 0.7 copy-start.5
  33.0 39.3 %copy-start = (f32[32,64,128]{2,1,0:T(8,128)S(1)}, f32[32,64,128]{2,1,0:T(8,128)}, u32[]{:S(2)}) copy-start(f32[32,64,128]{2,1,0:T(8,128)} %constant.19.clone.screen) | copy-start | bytes 3145732
  33.0 39.3 %copy-start.1 = (bf16[256,256]{1,0:T(8,128)(2,1)S(1)}, bf16[256,256]{1,0:T(8,128)(2,1)}, u32[]{:S(2)}) copy-start(bf16[256,256]{1,0:T(8,128)(2,1)} %constant.17.clone.right) | copy-start | bytes 393220
  33.0 39.3 %copy-start.2 = (bf16[64,192]{1,0:T(8,128)(2,1)S(1)}, bf16[64,192]{1,0:T(8,128)(2,1)}, u32[]{:S(2)}) copy-start(bf16[64,192]{1,0:T(8,128)(2,1)} %constant.18.clone.left) | copy-start | bytes 73732

commit v7 on v5

--- a/solution.py
+++ b/solution.py
@@ -16,7 +16,7 @@
 TILES = 32
 LANES = 128
 SCREENING = 0.02
-GROUPS = 4
+GROUPS = 8
 PARAMS = pltpu.CompilerParams(vmem_limit_bytes=48 * 1024 * 1024)
 WHOLE_V = pl.BlockSpec(memory_space=pltpu.VMEM)
 WHOLE_H = pl.BlockSpec(memory_space=pltpu.HBM)
@@ -201,21 +201,23 @@
         picked[k : k + 8] = tall[16 * k : 16 * k + 128, :].reshape(8, 16, LANES).astype(jnp.bfloat16)
 
 
-def shifted(tiles, start, count, flat, shift_x, shift_y):
+def shifted(tiles, start, count, flat, shift_x, shift_y, held):
     lane = lax.broadcasted_iota(jnp.int32, (8, LANES), 1)
     whole, rest = flat // LANES, flat % LANES
     later = (lane >= rest)[None]
     y = lane % BOX - shift_y
     keep_y = (y >= 0) & (y < BOX)
     turned = [
-        pltpu.roll(tiles((start + k - whole - 1 + 2 * TILES) % TILES), rest, 2) for k in range(count + 1)
+        pltpu.roll(tiles((start + k - whole - 1 + 2 * TILES) % TILES), rest, 2)
+        for k in range(0 if held is None else 1, count + 1)
     ]
+    turned = turned if held is None else [held] + turned
     out = []
     for k in range(count):
         x = 2 * (start + k) + lane // BOX - shift_x
         keep = jnp.where(keep_y & (x >= 0) & (x < BOX), 1.0, 0.0)
         out.append(jnp.where(later, turned[k + 1], turned[k]) * keep[None])
-    return out
+    return out, turned[count]
 
 
 def solve_kernel(shift, right, left, screen, boxes, terms, moved, field, other):
@@ -239,9 +241,11 @@
         )
         return product[:, :LANES] + product[:, LANES:]
 
+    held = None
     for start in range(0, TILES, 4):
         products = []
-        for k, box in enumerate(shifted(second_tile, start, 4, ahead, shift_x, shift_y)):
+        found, held = shifted(second_tile, start, 4, ahead, shift_x, shift_y, held)
+        for k, box in enumerate(found):
             moved[start + k] = box
             products.append(first_tile(start + k) * box)
         block = along_y(jnp.stack(products).reshape(4 * BOX, LANES)).reshape(4, BOX, LANES)
@@ -280,8 +284,9 @@
             other[start + k] = potential[k] * first_tile(start + k)
             moved[start + k] = potential[k] * moved[start + k]
 
+    held = None
     for start in range(0, TILES, 4):
-        carried = shifted(lambda tile: other[tile], start, 4, back, -shift_x, -shift_y)
+        carried, held = shifted(lambda tile: other[tile], start, 4, back, -shift_x, -shift_y, held)
         for k in range(4):
             both = jnp.concatenate([moved[start + k], carried[k]], axis=1)
             terms[(start + k) * 8 : (start + k + 1) * 8] = both.astype(jnp.bfloat16)
@@ -308,11 +313,11 @@
 
 
 def join_kernel(pieces, result):
-    for pair in range(ORB_DEV // 2):
-        tiles = [pieces[tile, 16 * pair : 16 * pair + 16, :].astype(jnp.float32) for tile in range(TILES)]
-        for side in range(2):
-            rows = [tile[8 * side : 8 * side + 8] for tile in tiles]
-            result[2 * pair + side] = jnp.concatenate(rows, axis=1).astype(jnp.bfloat16)
+    rows = pl.ds(pl.multiple_of(pl.program_id(0) * 16, 16), 16)
+    tiles = [pieces[tile, rows, :].astype(jnp.float32) for tile in range(TILES)]
+    for side in range(2):
+        box = [tile[8 * side : 8 * side + 8] for tile in tiles]
+        result[side] = jnp.concatenate(box, axis=1).astype(jnp.bfloat16)
 
 
 def body(orbitals, pair_first, second_owner, second_local, pair_shift, pair_count):
@@ -372,8 +377,9 @@
     )(index, terms)
     pieces = lax.all_to_all(pieces, "orb", split_axis=0, concat_axis=0, tiled=True)
     return pl.pallas_call(
-        join_kernel, out_shape=shape((ORB_DEV, 8, BOX * BOX), bf16),
-        in_specs=[WHOLE_V], out_specs=WHOLE_V,
+        join_kernel, out_shape=shape((ORB_DEV, 8, BOX * BOX), bf16), grid=(ORB_DEV // 2,),
+        in_specs=[pl.BlockSpec((N_ORB, rows, LANES), lambda pair: (0, 0, 0))],
+        out_specs=pl.BlockSpec((2, 8, BOX * BOX), lambda pair: (pair, 0, 0)),
         compiler_params=PARAMS, name="join",
     )(pieces)
 

time: 137 us -> 138 us (level)
  no operation moved by 1% of the time
where the time goes in v7:
time: 138 us; the launch traced here: 137 us
  blocking collectives  97.6 us (71%)
  waiting for transfers between devices  16.9 us (12%)
  starting transfers between devices  11.5 us (8%)
  Pallas kernels  9.7 us (7%)
    all_to_all x1, blocking collectives, body(): lax.all_to_all(picked, ('orb', 'slab'), split_axis=0, concat_axis=0, tile...  39.7 us
    all_to_all x1, blocking collectives, body(): lax.all_to_all(terms, ('orb', 'slab'), split_axis=0, concat_axis=0, tiled...  37.2 us
    all_to_all x1, blocking collectives, body(): lax.all_to_all(pieces, 'orb', split_axis=0, concat_axis=0, tiled=True)  20.7 us
    all_to_all x1, waiting for transfers between devices, body(): lax.all_to_all(pieces, 'orb', split_axis=0, concat_axis=0, tiled=True)  16.9 us
    all_to_all x1, starting transfers between devices, body(): lax.all_to_all(pieces, 'orb', split_axis=0, concat_axis=0, tiled=True)  11.5 us
    pallas_call x1, Pallas kernels, body(): pl.pallas_call(solve_kernel, out_shape=pair_shape, in_specs=[WHOLE_S] + [...  3.36 us
  transfers between devices with their start and end apart: 1, of which 1 were waited for; matrix products, arithmetic and copies ran while one was open for 0% of the time, Pallas kernels for 1%

profile of v7, /device:TPU:2, one launch (start us, length us, event | category | flops | bytes accessed | tf_op | source)
XLA Modules:
  0.0 136.5 jit_solution(1208070131013150534)
XLA Ops:
  0.0 2.0 %spread.1 = bf16[32,9,8,128]{3,2,1,0:T(8,128)(2,1)} custom-call(s32[1,16]{1,0:T(1,128)} %bitcast.8, s32[2,16]{1,0:T(2,128)} %bitcast.7, bf16[8,8,4096]{2,1,0:T(8,128)(2,1)} %orbitals.1), custom_call_target="tpu_custom_call" | custom-call | tf_op jit(solution)/shard_map/spread/pallas_call | solution.py:329
  2.0 11.5 %all-to-all-start = ((bf16[32,9,8,128]{3,2,1,0:T(8,128)(2,1)}), bf16[32,9,8,128]{3,2,1,0:T(8,128)(2,1)S(1)}, u32[]{:S(2)}, u32[]{:S(2)}) async-start(bf16[32,9,8,128]{3,2,1,0:T(8,128)(2,1)} %spread.1), calls=%async_computation | async-start | bytes 1179648 | tf_op jit(solution)/shard_map/all_to_all | solution.py:343
  13.5 0.0 copy-start.4
  13.5 0.0 copy-start.3
  13.5 0.0 copy-start.5
  13.5 0.6 copy-done.4
  14.2 0.0 copy-done.3
  14.2 0.0 copy-done.5
  14.2 0.8 place.1
  15.0 16.9 %all-to-all-done.pieces = bf16[32,9,8,128]{3,2,1,0:T(8,128)(2,1)S(1)} async-done(((bf16[32,9,8,128]{3,2,1,0:T(8,128)(2,1)}), bf16[32,9,8,128]{3,2,1,0:T(8,128)(2,1)S(1)}, u32[]{:S(2)}, u32[]{:S(2)}) %all-to-all-start) | async-done | bytes 589856 | tf_op jit(solution)/shard_map/all_to_all | solution.py:343
  32.0 1.0 pick.1
  33.0 0.0 copy-start
  33.0 0.0 copy-start.1
  33.0 0.0 copy-start.2
  33.0 39.7 %all_to_all.20.boxes = bf16[256,16,128]{2,1,0:T(8,128)(2,1)S(1)} all-to-all(bf16[256,16,128]{2,1,0:T(8,128)(2,1)S(1)} %get-tuple-element.16), channel_id=1, replica_groups=mesh['orb'=32,'slab'=8] {'orb','slab'}, dimensions={0} | all-to-all | bytes 2097152 | tf_op jit(solution)/shard_map/all_to_all | solution.py:358
  72.7 0.0 copy-done
  72.7 0.0 copy-done.1
  72.7 0.0 copy-done.2
  72.7 3.4 %solve.1 = bf16[256,16,128]{2,1,0:T(8,128)(2,1)S(1)} custom-call(s32[1,128]{1,0:T(1,128)S(1)} %get-tuple-element.15.shift, bf16[256,256]{1,0:T(8,128)(2,1)S(1)} %copy-done.1, bf16[64,192]{1,0:T(8,128)(2,1)S(1)} %copy-done.2, f32[32,64,128]{2,1,0:T(8,128)S(1)} %copy-done, bf16[256,16,128]{2,1,0:T(8,128)(2,1)S(1)} %all_to_all.20.boxes), custom_call_target="tpu_custom_call" | custom-call | tf_op jit(solution)/shard_map/solve/pallas_call | solution.py:360
  76.1 37.2 %all_to_all.21.terms = bf16[256,16,128]{2,1,0:T(8,128)(2,1)S(1)} all-to-all(bf16[256,16,128]{2,1,0:T(8,128)(2,1)S(1)} %solve.1), channel_id=1, replica_groups=mesh['orb'=32,'slab'=8] {'orb','slab'}, dimensions={0} | all-to-all | bytes 2097152 | tf_op jit(solution)/shard_map/all_to_all | solution.py:371
  113.3 1.1 sum.1
  114.4 20.7 %all_to_all.22.pieces = bf16[32,64,128]{2,1,0:T(8,128)(2,1)S(1)} all-to-all(bf16[32,64,128]{2,1,0:T(8,128)(2,1)S(1)} %sum.1), channel_id=1, replica_groups=mesh['orb'=32,'slab'=8] {'orb'}, dimensions={0} | all-to-all | bytes 1048576 | tf_op jit(solution)/shard_map/all_to_all | solution.py:378
  135.1 1.4 %join.1 = bf16[8,8,4096]{2,1,0:T(8,128)(2,1)} custom-call(bf16[32,64,128]{2,1,0:T(8,128)(2,1)S(1)} %all_to_all.22.pieces), custom_call_target="tpu_custom_call" | custom-call | tf_op jit(solution)/shard_map/join/pallas_call | solution.py:379
Async XLA Ops:
  2.0 30.0 %all-to-all-start = ((bf16[32,9,8,128]{3,2,1,0:T(8,128)(2,1)}), bf16[32,9,8,128]{3,2,1,0:T(8,128)(2,1)S(1)}, u32[]{:S(2)}, u32[]{:S(2)}) async-start(bf16[32,9,8,128]{3,2,1,0:T(8,128)(2,1)} %spread.1), calls=%async_computation | async-start | bytes 1179648 | tf_op jit(solution)/shard_map/all_to_all | solution.py:343
  13.5 0.7 copy-start.4
  13.5 0.7 copy-start.3
  13.5 0.7 copy-start.5
  33.0 39.7 %copy-start = (f32[32,64,128]{2,1,0:T(8,128)S(1)}, f32[32,64,128]{2,1,0:T(8,128)}, u32[]{:S(2)}) copy-start(f32[32,64,128]{2,1,0:T(8,128)} %constant.19.clone.screen) | copy-start | bytes 3145732
  33.0 39.7 %copy-start.1 = (bf16[256,256]{1,0:T(8,128)(2,1)S(1)}, bf16[256,256]{1,0:T(8,128)(2,1)}, u32[]{:S(2)}) copy-start(bf16[256,256]{1,0:T(8,128)(2,1)} %constant.17.clone.right) | copy-start | bytes 393220
  33.0 39.7 %copy-start.2 = (bf16[64,192]{1,0:T(8,128)(2,1)S(1)}, bf16[64,192]{1,0:T(8,128)(2,1)}, u32[]{:S(2)}) copy-start(bf16[64,192]{1,0:T(8,128)(2,1)} %constant.18.clone.left) | copy-start | bytes 73732

commit v8 on v5

--- a/solution.py
+++ b/solution.py
@@ -326,7 +326,7 @@
         in_specs=[WHOLE_H] * 3, out_specs=WHOLE_H,
         scratch_shapes=[
             pltpu.VMEM((GROUPS, ORB_DEV, 8, BOX * BOX // GROUPS), bf16),
-            pltpu.VMEM((TILES * rows, LANES), f32),
+            pltpu.VMEM((TILES * rows + 64, LANES), f32),
             pltpu.VMEM((16, PAIR_DEV), i32),
             pltpu.VMEM((8, LANES), f32),
             pltpu.VMEM((N_ORB, 9, ORB_DEV, LANES), bf16),
@@ -347,7 +347,7 @@
         out_shape=(pair_shape, shape((2, N_DEV), i32), shape((1, LANES), i32)),
         in_specs=[WHOLE_S] + [WHOLE_V] * 4,
         out_specs=(WHOLE_V,) * 3,
-        scratch_shapes=[pltpu.VMEM((N_DEV * 16, LANES), f32)],
+        scratch_shapes=[pltpu.VMEM((N_DEV * 16 + 16, LANES), f32)],
         compiler_params=PARAMS, name="pick",
     )(me, place, second, choose, pieces)
     boxes = lax.all_to_all(picked, ("orb", "slab"), split_axis=0, concat_axis=0, tiled=True)
@@ -367,7 +367,7 @@
     pieces = pl.pallas_call(
         sum_kernel, out_shape=shape((N_ORB, rows, LANES), bf16),
         in_specs=[WHOLE_V, WHOLE_V], out_specs=WHOLE_V,
-        scratch_shapes=[pltpu.VMEM((N_DEV * 16, LANES), f32), pltpu.VMEM((N_DEV * 8, LANES), f32)],
+        scratch_shapes=[pltpu.VMEM((N_DEV * 16 + 16, LANES), f32), pltpu.VMEM((N_DEV * 8 + 8, LANES), f32)],
         compiler_params=PARAMS, name="sum",
     )(index, terms)
     pieces = lax.all_to_all(pieces, "orb", split_axis=0, concat_axis=0, tiled=True)

time: 137 us -> 137 us (level)
  no operation moved by 1% of the time
where the time goes in v8:
time: 137 us; the launch traced here: 136 us
  blocking collectives  97.6 us (71%)
  waiting for transfers between devices  16.9 us (12%)
  starting transfers between devices  11.5 us (8%)
  Pallas kernels  9.23 us (7%)
    all_to_all x1, blocking collectives, body(): lax.all_to_all(picked, ('orb', 'slab'), split_axis=0, concat_axis=0, tile...  39.7 us
    all_to_all x1, blocking collectives, body(): lax.all_to_all(terms, ('orb', 'slab'), split_axis=0, concat_axis=0, tiled...  37.2 us
    all_to_all x1, blocking collectives, body(): lax.all_to_all(pieces, 'orb', split_axis=0, concat_axis=0, tiled=True)  20.7 us
    all_to_all x1, waiting for transfers between devices, body(): lax.all_to_all(pieces, 'orb', split_axis=0, concat_axis=0, tiled=True)  16.9 us
    all_to_all x1, starting transfers between devices, body(): lax.all_to_all(pieces, 'orb', split_axis=0, concat_axis=0, tiled=True)  11.5 us
    pallas_call x1, Pallas kernels, body(): pl.pallas_call(solve_kernel, out_shape=pair_shape, in_specs=[WHOLE_S] + [...  3.44 us
  transfers between devices with their start and end apart: 1, of which 1 were waited for; matrix products, arithmetic and copies ran while one was open for 0% of the time, Pallas kernels for 1%

profile of v8, /device:TPU:2, one launch (start us, length us, event | category | flops | bytes accessed | tf_op | source)
XLA Modules:
  0.0 136.0 jit_solution(17442315528407498074)
XLA Ops:
  0.0 2.0 %spread.1 = bf16[32,9,8,128]{3,2,1,0:T(8,128)(2,1)} custom-call(s32[1,16]{1,0:T(1,128)} %bitcast.8, s32[2,16]{1,0:T(2,128)} %bitcast.7, bf16[8,8,4096]{2,1,0:T(8,128)(2,1)} %orbitals.1), custom_call_target="tpu_custom_call" | custom-call | tf_op jit(solution)/shard_map/spread/pallas_call | solution.py:324
  2.0 11.5 %all-to-all-start = ((bf16[32,9,8,128]{3,2,1,0:T(8,128)(2,1)}), bf16[32,9,8,128]{3,2,1,0:T(8,128)(2,1)S(1)}, u32[]{:S(2)}, u32[]{:S(2)}) async-start(bf16[32,9,8,128]{3,2,1,0:T(8,128)(2,1)} %spread.1), calls=%async_computation | async-start | bytes 1179648 | tf_op jit(solution)/shard_map/all_to_all | solution.py:338
  13.5 0.0 copy-start.4
  13.5 0.0 copy-start.3
  13.5 0.0 copy-start.5
  13.5 0.6 copy-done.4
  14.2 0.0 copy-done.3
  14.2 0.0 copy-done.5
  14.2 0.8 place.1
  15.0 16.9 %all-to-all-done.pieces = bf16[32,9,8,128]{3,2,1,0:T(8,128)(2,1)S(1)} async-done(((bf16[32,9,8,128]{3,2,1,0:T(8,128)(2,1)}), bf16[32,9,8,128]{3,2,1,0:T(8,128)(2,1)S(1)}, u32[]{:S(2)}, u32[]{:S(2)}) %all-to-all-start) | async-done | bytes 589856 | tf_op jit(solution)/shard_map/all_to_all | solution.py:338
  31.9 1.0 pick.1
  33.0 0.0 copy-start
  33.0 0.0 copy-start.1
  33.0 0.0 copy-start.2
  33.0 39.7 %all_to_all.20.boxes = bf16[256,16,128]{2,1,0:T(8,128)(2,1)S(1)} all-to-all(bf16[256,16,128]{2,1,0:T(8,128)(2,1)S(1)} %get-tuple-element.16), channel_id=1, replica_groups=mesh['orb'=32,'slab'=8] {'orb','slab'}, dimensions={0} | all-to-all | bytes 2097152 | tf_op jit(solution)/shard_map/all_to_all | solution.py:353
  72.7 0.0 copy-done
  72.7 0.0 copy-done.1
  72.7 0.0 copy-done.2
  72.7 3.4 %solve.1 = bf16[256,16,128]{2,1,0:T(8,128)(2,1)S(1)} custom-call(s32[1,128]{1,0:T(1,128)S(1)} %get-tuple-element.15.shift, bf16[256,256]{1,0:T(8,128)(2,1)S(1)} %copy-done.1, bf16[64,192]{1,0:T(8,128)(2,1)S(1)} %copy-done.2, f32[32,64,128]{2,1,0:T(8,128)S(1)} %copy-done, bf16[256,16,128]{2,1,0:T(8,128)(2,1)S(1)} %all_to_all.20.boxes), custom_call_target="tpu_custom_call" | custom-call | tf_op jit(solution)/shard_map/solve/pallas_call | solution.py:355
  76.1 37.2 %all_to_all.21.terms = bf16[256,16,128]{2,1,0:T(8,128)(2,1)S(1)} all-to-all(bf16[256,16,128]{2,1,0:T(8,128)(2,1)S(1)} %solve.1), channel_id=1, replica_groups=mesh['orb'=32,'slab'=8] {'orb','slab'}, dimensions={0} | all-to-all | bytes 2097152 | tf_op jit(solution)/shard_map/all_to_all | solution.py:366
  113.3 1.1 sum.1
  114.5 20.7 %all_to_all.22.pieces = bf16[32,64,128]{2,1,0:T(8,128)(2,1)S(1)} all-to-all(bf16[32,64,128]{2,1,0:T(8,128)(2,1)S(1)} %sum.1), channel_id=1, replica_groups=mesh['orb'=32,'slab'=8] {'orb'}, dimensions={0} | all-to-all | bytes 1048576 | tf_op jit(solution)/shard_map/all_to_all | solution.py:373
  135.2 0.9 join.1
Async XLA Ops:
  2.0 30.0 %all-to-all-start = ((bf16[32,9,8,128]{3,2,1,0:T(8,128)(2,1)}), bf16[32,9,8,128]{3,2,1,0:T(8,128)(2,1)S(1)}, u32[]{:S(2)}, u32[]{:S(2)}) async-start(bf16[32,9,8,128]{3,2,1,0:T(8,128)(2,1)} %spread.1), calls=%async_computation | async-start | bytes 1179648 | tf_op jit(solution)/shard_map/all_to_all | solution.py:338
  13.5 0.7 copy-start.4
  13.5 0.7 copy-start.3
  13.5 0.7 copy-start.5
  33.0 39.7 %copy-start = (f32[32,64,128]{2,1,0:T(8,128)S(1)}, f32[32,64,128]{2,1,0:T(8,128)}, u32[]{:S(2)}) copy-start(f32[32,64,128]{2,1,0:T(8,128)} %constant.19.clone.screen) | copy-start | bytes 3145732
  33.0 39.7 %copy-start.1 = (bf16[256,256]{1,0:T(8,128)(2,1)S(1)}, bf16[256,256]{1,0:T(8,128)(2,1)}, u32[]{:S(2)}) copy-start(bf16[256,256]{1,0:T(8,128)(2,1)} %constant.17.clone.right) | copy-start | bytes 393220
  33.0 39.7 %copy-start.2 = (bf16[64,192]{1,0:T(8,128)(2,1)S(1)}, bf16[64,192]{1,0:T(8,128)(2,1)}, u32[]{:S(2)}) copy-start(bf16[64,192]{1,0:T(8,128)(2,1)} %constant.18.clone.left) | copy-start | bytes 73732

commit v9 on v8

--- a/solution.py
+++ b/solution.py
@@ -16,6 +16,7 @@
 TILES = 32
 LANES = 128
 SCREENING = 0.02
+STEPS = [(dy, dz) for dz in (4, 3, 5, 2, 6, 1, 7, 0) for dy in (2, 1, 3, 0)]
 GROUPS = 4
 PARAMS = pltpu.CompilerParams(vmem_limit_bytes=48 * 1024 * 1024)
 WHOLE_V = pl.BlockSpec(memory_space=pltpu.VMEM)
@@ -287,7 +288,14 @@
             terms[(start + k) * 8 : (start + k + 1) * 8] = both.astype(jnp.bfloat16)
 
 
-def sum_kernel(index, terms, pieces, tall, summed):
+def partner(step, sign):
+    orb = lax.axis_index("orb")
+    y, z = orb // 8 + sign * step[0] + 4, orb % 8 + sign * step[1] + 8
+    return y % 4 * 8 + z % 8
+
+
+def sum_kernel(index, terms, *rest):
+    pieces, (tall, summed) = rest[:N_ORB], rest[N_ORB:]
     for k in range(0, N_DEV, 8):
         tall[16 * k : 16 * k + 128, :] = terms[k : k + 8].astype(jnp.float32).reshape(128, LANES)
     orbital = lax.broadcasted_iota(jnp.int32, (N_DEV, N_DEV), 0)
@@ -303,16 +311,28 @@
         out = jnp.dot(hits, jnp.concatenate(field, axis=1), preferred_element_type=jnp.float32)
         summed[pl.ds(z, N_DEV, stride=8), :] = out[:, :LANES]
         summed[pl.ds(z + 1, N_DEV, stride=8), :] = out[:, LANES:]
-    for e in range(N_ORB):
-        pieces[e] = summed[e * ORB_DEV * 8 : (e + 1) * ORB_DEV * 8, :].astype(jnp.bfloat16)
-
-
-def join_kernel(pieces, result):
-    for pair in range(ORB_DEV // 2):
-        tiles = [pieces[tile, 16 * pair : 16 * pair + 16, :].astype(jnp.float32) for tile in range(TILES)]
-        for side in range(2):
-            rows = [tile[8 * side : 8 * side + 8] for tile in tiles]
-            result[2 * pair + side] = jnp.concatenate(rows, axis=1).astype(jnp.bfloat16)
+    for k, away in enumerate(STEPS):
+        rows = pl.ds(pl.multiple_of(partner(away, 1) * ORB_DEV * 8, ORB_DEV * 8), ORB_DEV * 8)
+        pieces[k][...] = summed[rows, :].astype(jnp.bfloat16)
+
+
+def join_kernel(*rest):
+    pieces, result = rest[:N_ORB], rest[N_ORB]
+    for k, away in enumerate(STEPS):
+        lanes = pl.ds(pl.multiple_of(partner(away, -1) * LANES, LANES), LANES)
+        rows = pieces[k][...].astype(jnp.float32)
+        for orbital in range(ORB_DEV):
+            result[orbital, :, lanes] = rows[8 * orbital : 8 * orbital + 8].astype(jnp.bfloat16)
+
+
+def permuted(pieces, away):
+    if away == (0, 0):
+        return pieces
+    pairs = []
+    for orb in range(N_ORB):
+        y, z = (orb // 8 + away[0]) % 4, (orb % 8 + away[1]) % 8
+        pairs.append((orb, y * 8 + z))
+    return lax.ppermute(pieces, "orb", pairs)
 
 
 def body(orbitals, pair_first, second_owner, second_local, pair_shift, pair_count):
@@ -365,17 +385,17 @@
     )(mine, right, left, screen, boxes)
     terms = lax.all_to_all(terms, ("orb", "slab"), split_axis=0, concat_axis=0, tiled=True)
     pieces = pl.pallas_call(
-        sum_kernel, out_shape=shape((N_ORB, rows, LANES), bf16),
-        in_specs=[WHOLE_V, WHOLE_V], out_specs=WHOLE_V,
+        sum_kernel, out_shape=(shape((rows, LANES), bf16),) * N_ORB,
+        in_specs=[WHOLE_V, WHOLE_V], out_specs=(WHOLE_V,) * N_ORB,
         scratch_shapes=[pltpu.VMEM((N_DEV * 16 + 16, LANES), f32), pltpu.VMEM((N_DEV * 8 + 8, LANES), f32)],
         compiler_params=PARAMS, name="sum",
     )(index, terms)
-    pieces = lax.all_to_all(pieces, "orb", split_axis=0, concat_axis=0, tiled=True)
+    pieces = [permuted(piece, away) for piece, away in zip(pieces, STEPS)]
     return pl.pallas_call(
         join_kernel, out_shape=shape((ORB_DEV, 8, BOX * BOX), bf16),
-        in_specs=[WHOLE_V], out_specs=WHOLE_V,
+        in_specs=[WHOLE_V] * N_ORB, out_specs=WHOLE_V,
         compiler_params=PARAMS, name="join",
-    )(pieces)
+    )(*pieces)
 
 
 def solution(mesh):

time: 137 us -> 195 us (1.42)
  starting transfers between devices: 11.5 us -> 89.2 us
  blocking collectives: 97.6 us -> 76.9 us
    ppermute x0 -> x31, starting transfers between devices: none -> 77.7 us  [permuted(): return lax.ppermute(pieces, 'orb', pairs)]
    all_to_all x1 -> x0, blocking collectives: 20.7 us -> none  [body(): lax.all_to_all(pieces, 'orb', split_axis=0, concat_axis=0, tiled=True)]
  transfers between devices with their start and end apart: 1 -> 32, of which waited for: 1 -> 3; matrix products, arithmetic and copies ran while one was open for 0% -> 0% of each run, Pallas kernels for 1% -> 0%
where the time goes in v9:
time: 195 us
  starting transfers between devices  89.2 us (46%)
  blocking collectives  76.9 us (39%)
  waiting for transfers between devices  18.7 us (10%)
  Pallas kernels  9.3 us (5%)
    ppermute x31, starting transfers between devices, permuted(): return lax.ppermute(pieces, 'orb', pairs)  77.7 us
    all_to_all x1, blocking collectives, body(): lax.all_to_all(picked, ('orb', 'slab'), split_axis=0, concat_axis=0, tile...  39.7 us
    all_to_all x1, blocking collectives, body(): lax.all_to_all(terms, ('orb', 'slab'), split_axis=0, concat_axis=0, tiled...  37.2 us
    all_to_all x1, waiting for transfers between devices, body(): lax.all_to_all(pieces, 'orb', split_axis=0, concat_axis=0, tiled=True)  16.9 us
    all_to_all x1, starting transfers between devices, body(): lax.all_to_all(pieces, 'orb', split_axis=0, concat_axis=0, tiled=True)  11.5 us
  transfers between devices with their start and end apart: 32, of which 3 were waited for; matrix products, arithmetic and copies ran while one was open for 0% of the time, Pallas kernels for 0%

profile of v9, /device:TPU:2, one launch (start us, length us, event | category | flops | bytes accessed | tf_op | source)
XLA Modules:
  0.0 194.9 jit_solution(12502588969883108048)
XLA Ops:
  0.0 2.0 %spread.1 = bf16[32,9,8,128]{3,2,1,0:T(8,128)(2,1)} custom-call(s32[1,16]{1,0:T(1,128)} %bitcast.8, s32[2,16]{1,0:T(2,128)} %bitcast.7, bf16[8,8,4096]{2,1,0:T(8,128)(2,1)} %orbitals.1), custom_call_target="tpu_custom_call" | custom-call | tf_op jit(solution)/shard_map/spread/pallas_call | solution.py:344
  2.0 11.5 %all-to-all-start = ((bf16[32,9,8,128]{3,2,1,0:T(8,128)(2,1)}), bf16[32,9,8,128]{3,2,1,0:T(8,128)(2,1)S(1)}, u32[]{:S(2)}, u32[]{:S(2)}) async-start(bf16[32,9,8,128]{3,2,1,0:T(8,128)(2,1)} %spread.1), calls=%async_computation | async-start | bytes 1179648 | tf_op jit(solution)/shard_map/all_to_all | solution.py:358
  15.0 16.9 %all-to-all-done.pieces = bf16[32,9,8,128]{3,2,1,0:T(8,128)(2,1)S(1)} async-done(((bf16[32,9,8,128]{3,2,1,0:T(8,128)(2,1)}), bf16[32,9,8,128]{3,2,1,0:T(8,128)(2,1)S(1)}, u32[]{:S(2)}, u32[]{:S(2)}) %all-to-all-start) | async-done | bytes 589856 | tf_op jit(solution)/shard_map/all_to_all | solution.py:358
  33.0 39.7 %all_to_all.15.boxes = bf16[256,16,128]{2,1,0:T(8,128)(2,1)S(1)} all-to-all(bf16[256,16,128]{2,1,0:T(8,128)(2,1)S(1)} %get-tuple-element.48), channel_id=1, replica_groups=mesh['orb'=32,'slab'=8] {'orb','slab'}, dimensions={0} | all-to-all | bytes 2097152 | tf_op jit(solution)/shard_map/all_to_all | solution.py:373
  72.7 3.4 %solve.1 = bf16[256,16,128]{2,1,0:T(8,128)(2,1)S(1)} custom-call(s32[1,128]{1,0:T(1,128)S(1)} %get-tuple-element.47.shift, bf16[256,256]{1,0:T(8,128)(2,1)S(1)} %copy-done.1, bf16[64,192]{1,0:T(8,128)(2,1)S(1)} %copy-done.2, f32[32,64,128]{2,1,0:T(8,128)S(1)} %copy-done, bf16[256,16,128]{2,1,0:T(8,128)(2,1)S(1)} %all_to_all.15.boxes), custom_call_target="tpu_custom_call" | custom-call | tf_op jit(solution)/shard_map/solve/pallas_call | solution.py:375
  76.1 37.2 %all_to_all.16.terms = bf16[256,16,128]{2,1,0:T(8,128)(2,1)S(1)} all-to-all(bf16[256,16,128]{2,1,0:T(8,128)(2,1)S(1)} %solve.1), channel_id=1, replica_groups=mesh['orb'=32,'slab'=8] {'orb','slab'}, dimensions={0} | all-to-all | bytes 2097152 | tf_op jit(solution)/shard_map/all_to_all | solution.py:386
  113.2 1.1 sum.1
  114.4 1.7 collective-permute-start
  116.1 4.9 %collective-permute-start.1 = (bf16[64,128]{1,0:T(8,128)(2,1)S(1)}, bf16[64,128]{1,0:T(8,128)(2,1)S(1)}, u32[]{:S(2)}, u32[]{:S(2)}) collective-permute-start(bf16[64,128]{1,0:T(8,128)(2,1)S(1)} %get-tuple-element.50), channel_id=1, source_target_pairs={{0,96},{8,104},{16,112},{24,120},{32,64},{40,72},{48,80},{56,88},{... | collective-permute-start | bytes 49160 | tf_op jit(solution)/shard_map/ppermute | solution.py:335
  120.9 3.2 %collective-permute-start.2 = (bf16[64,128]{1,0:T(8,128)(2,1)S(1)}, bf16[64,128]{1,0:T(8,128)(2,1)S(1)}, u32[]{:S(2)}, u32[]{:S(2)}) collective-permute-start(bf16[64,128]{1,0:T(8,128)(2,1)S(1)} %get-tuple-element.51), channel_id=1, source_target_pairs={{0,224},{8,232},{16,240},{24,248},{32,192},{40,200},{48,208},{56,2... | collective-permute-start | bytes 49160 | tf_op jit(solution)/shard_map/ppermute | solution.py:335
  124.1 4.5 %collective-permute-start.3 = (bf16[64,128]{1,0:T(8,128)(2,1)S(1)}, bf16[64,128]{1,0:T(8,128)(2,1)S(1)}, u32[]{:S(2)}, u32[]{:S(2)}) collective-permute-start(bf16[64,128]{1,0:T(8,128)(2,1)S(1)} %get-tuple-element.52), channel_id=1, source_target_pairs={{0,32},{8,40},{16,48},{24,56},{32,0},{40,8},{48,16},{56,24},{64,96... | collective-permute-start | bytes 49160 | tf_op jit(solution)/shard_map/ppermute | solution.py:335
  128.6 2.0 %collective-permute-start.4 = (bf16[64,128]{1,0:T(8,128)(2,1)S(1)}, bf16[64,128]{1,0:T(8,128)(2,1)S(1)}, u32[]{:S(2)}, u32[]{:S(2)}) collective-permute-start(bf16[64,128]{1,0:T(8,128)(2,1)S(1)} %get-tuple-element.53), channel_id=1, source_target_pairs={{0,152},{8,160},{16,168},{24,176},{32,184},{40,128},{48,136},{56,1... | collective-permute-start | bytes 49160 | tf_op jit(solution)/shard_map/ppermute | solution.py:335
  131.6 7.0 %collective-permute-start.6 = (bf16[64,128]{1,0:T(8,128)(2,1)S(1)}, bf16[64,128]{1,0:T(8,128)(2,1)S(1)}, u32[]{:S(2)}, u32[]{:S(2)}) collective-permute-start(bf16[64,128]{1,0:T(8,128)(2,1)S(1)} %get-tuple-element.55), channel_id=1, source_target_pairs={{0,216},{8,224},{16,232},{24,240},{32,248},{40,192},{48,200},{56,2... | collective-permute-start | bytes 49160 | tf_op jit(solution)/shard_map/ppermute | solution.py:335
  138.6 1.4 collective-permute-start.7
  140.0 3.8 %collective-permute-start.8 = (bf16[64,128]{1,0:T(8,128)(2,1)S(1)}, bf16[64,128]{1,0:T(8,128)(2,1)S(1)}, u32[]{:S(2)}, u32[]{:S(2)}) collective-permute-start(bf16[64,128]{1,0:T(8,128)(2,1)S(1)} %get-tuple-element.57), channel_id=1, source_target_pairs={{0,168},{8,176},{16,184},{24,128},{32,136},{40,144},{48,152},{56,1... | collective-permute-start | bytes 49160 | tf_op jit(solution)/shard_map/ppermute | solution.py:335
  144.5 5.6 %collective-permute-start.10 = (bf16[64,128]{1,0:T(8,128)(2,1)S(1)}, bf16[64,128]{1,0:T(8,128)(2,1)S(1)}, u32[]{:S(2)}, u32[]{:S(2)}) collective-permute-start(bf16[64,128]{1,0:T(8,128)(2,1)S(1)} %get-tuple-element.59), channel_id=1, source_target_pairs={{0,232},{8,240},{16,248},{24,192},{32,200},{40,208},{48,216},{56,2... | collective-permute-start | bytes 49160 | tf_op jit(solution)/shard_map/ppermute | solution.py:335
  150.1 2.8 %collective-permute-start.11 = (bf16[64,128]{1,0:T(8,128)(2,1)S(1)}, bf16[64,128]{1,0:T(8,128)(2,1)S(1)}, u32[]{:S(2)}, u32[]{:S(2)}) collective-permute-start(bf16[64,128]{1,0:T(8,128)(2,1)S(1)} %get-tuple-element.60), channel_id=1, source_target_pairs={{0,40},{8,48},{16,56},{24,0},{32,8},{40,16},{48,24},{56,32},{64,10... | collective-permute-start | bytes 49160 | tf_op jit(solution)/shard_map/ppermute | solution.py:335
  153.0 2.2 %collective-permute-start.12 = (bf16[64,128]{1,0:T(8,128)(2,1)S(1)}, bf16[64,128]{1,0:T(8,128)(2,1)S(1)}, u32[]{:S(2)}, u32[]{:S(2)}) collective-permute-start(bf16[64,128]{1,0:T(8,128)(2,1)S(1)} %get-tuple-element.61), channel_id=1, source_target_pairs={{0,144},{8,152},{16,160},{24,168},{32,176},{40,184},{48,128},{56,1... | collective-permute-start | bytes 49160 | tf_op jit(solution)/shard_map/ppermute | solution.py:335
  155.2 4.9 %collective-permute-start.14 = (bf16[64,128]{1,0:T(8,128)(2,1)S(1)}, bf16[64,128]{1,0:T(8,128)(2,1)S(1)}, u32[]{:S(2)}, u32[]{:S(2)}) collective-permute-start(bf16[64,128]{1,0:T(8,128)(2,1)S(1)} %get-tuple-element.63), channel_id=1, source_target_pairs={{0,208},{8,216},{16,224},{24,232},{32,240},{40,248},{48,192},{56,2... | collective-permute-start | bytes 49160 | tf_op jit(solution)/shard_map/ppermute | solution.py:335
  160.0 3.2 %collective-permute-start.15 = (bf16[64,128]{1,0:T(8,128)(2,1)S(1)}, bf16[64,128]{1,0:T(8,128)(2,1)S(1)}, u32[]{:S(2)}, u32[]{:S(2)}) collective-permute-start(bf16[64,128]{1,0:T(8,128)(2,1)S(1)} %get-tuple-element.64), channel_id=1, source_target_pairs={{0,16},{8,24},{16,32},{24,40},{32,48},{40,56},{48,0},{56,8},{64,80... | collective-permute-start | bytes 49160 | tf_op jit(solution)/shard_map/ppermute | solution.py:335
  163.2 1.1 collective-permute-start.16
  164.7 6.0 %collective-permute-start.18 = (bf16[64,128]{1,0:T(8,128)(2,1)S(1)}, bf16[64,128]{1,0:T(8,128)(2,1)S(1)}, u32[]{:S(2)}, u32[]{:S(2)}) collective-permute-start(bf16[64,128]{1,0:T(8,128)(2,1)S(1)} %get-tuple-element.67), channel_id=1, source_target_pairs={{0,240},{8,248},{16,192},{24,200},{32,208},{40,216},{48,224},{56,2... | collective-permute-start | bytes 49160 | tf_op jit(solution)/shard_map/ppermute | solution.py:335
  170.8 1.8 collective-permute-start.19
  172.5 2.0 %collective-permute-start.20 = (bf16[64,128]{1,0:T(8,128)(2,1)S(1)}, bf16[64,128]{1,0:T(8,128)(2,1)S(1)}, u32[]{:S(2)}, u32[]{:S(2)}) collective-permute-start(bf16[64,128]{1,0:T(8,128)(2,1)S(1)} %get-tuple-element.69), channel_id=1, source_target_pairs={{0,136},{8,144},{16,152},{24,160},{32,168},{40,176},{48,184},{56,1... | collective-permute-start | bytes 49160 | tf_op jit(solution)/shard_map/ppermute | solution.py:335
  174.5 3.3 %collective-permute-start.22 = (bf16[64,128]{1,0:T(8,128)(2,1)S(1)}, bf16[64,128]{1,0:T(8,128)(2,1)S(1)}, u32[]{:S(2)}, u32[]{:S(2)}) collective-permute-start(bf16[64,128]{1,0:T(8,128)(2,1)S(1)} %get-tuple-element.71), channel_id=1, source_target_pairs={{0,200},{8,208},{16,216},{24,224},{32,232},{40,240},{48,248},{56,1... | collective-permute-start | bytes 49160 | tf_op jit(solution)/shard_map/ppermute | solution.py:335
  177.8 1.3 collective-permute-start.23
  179.1 2.1 %collective-permute-start.24 = (bf16[64,128]{1,0:T(8,128)(2,1)S(1)}, bf16[64,128]{1,0:T(8,128)(2,1)S(1)}, u32[]{:S(2)}, u32[]{:S(2)}) collective-permute-start(bf16[64,128]{1,0:T(8,128)(2,1)S(1)} %get-tuple-element.73), channel_id=1, source_target_pairs={{0,184},{8,128},{16,136},{24,144},{32,152},{40,160},{48,168},{56,1... | collective-permute-start | bytes 49160 | tf_op jit(solution)/shard_map/ppermute | solution.py:335
  182.3 3.9 %collective-permute-start.26 = (bf16[64,128]{1,0:T(8,128)(2,1)S(1)}, bf16[64,128]{1,0:T(8,128)(2,1)S(1)}, u32[]{:S(2)}, u32[]{:S(2)}) collective-permute-start(bf16[64,128]{1,0:T(8,128)(2,1)S(1)} %get-tuple-element.75), channel_id=1, source_target_pairs={{0,248},{8,192},{16,200},{24,208},{32,216},{40,224},{48,232},{56,2... | collective-permute-start | bytes 49160 | tf_op jit(solution)/shard_map/ppermute | solution.py:335
  186.2 1.1 collective-permute-start.27
  187.3 1.6 collective-permute-start.28
  188.9 3.2 %collective-permute-start.30 = (bf16[64,128]{1,0:T(8,128)(2,1)S(1)}, bf16[64,128]{1,0:T(8,128)(2,1)S(1)}, u32[]{:S(2)}, u32[]{:S(2)}) collective-permute-start(bf16[64,128]{1,0:T(8,128)(2,1)S(1)} %get-tuple-element.79), channel_id=1, source_target_pairs={{0,192},{8,200},{16,208},{24,216},{32,224},{40,232},{48,240},{56,2... | collective-permute-start | bytes 49160 | tf_op jit(solution)/shard_map/ppermute | solution.py:335
  192.5 1.3 collective-permute-done.29.rest_29_
  (52 shorter events, 7.1 us)
Async XLA Ops:
  2.0 30.0 %all-to-all-start = ((bf16[32,9,8,128]{3,2,1,0:T(8,128)(2,1)}), bf16[32,9,8,128]{3,2,1,0:T(8,128)(2,1)S(1)}, u32[]{:S(2)}, u32[]{:S(2)}) async-start(bf16[32,9,8,128]{3,2,1,0:T(8,128)(2,1)} %spread.1), calls=%async_computation | async-start | bytes 1179648 | tf_op jit(solution)/shard_map/all_to_all | solution.py:358
  114.4 16.2 %collective-permute-start = (bf16[64,128]{1,0:T(8,128)(2,1)S(1)}, bf16[64,128]{1,0:T(8,128)(2,1)S(1)}, u32[]{:S(2)}, u32[]{:S(2)}) collective-permute-start(bf16[64,128]{1,0:T(8,128)(2,1)S(1)} %get-tuple-element.49), channel_id=1, source_target_pairs={{0,160},{8,168},{16,176},{24,184},{32,128},{40,136},{48,144},{56,1... | collective-permute-start | bytes 49160 | tf_op jit(solution)/shard_map/ppermute | solution.py:335
  116.1 15.5 %collective-permute-start.1 = (bf16[64,128]{1,0:T(8,128)(2,1)S(1)}, bf16[64,128]{1,0:T(8,128)(2,1)S(1)}, u32[]{:S(2)}, u32[]{:S(2)}) collective-permute-start(bf16[64,128]{1,0:T(8,128)(2,1)S(1)} %get-tuple-element.50), channel_id=1, source_target_pairs={{0,96},{8,104},{16,112},{24,120},{32,64},{40,72},{48,80},{56,88},{... | collective-permute-start | bytes 49160 | tf_op jit(solution)/shard_map/ppermute | solution.py:335
  120.9 17.7 %collective-permute-start.2 = (bf16[64,128]{1,0:T(8,128)(2,1)S(1)}, bf16[64,128]{1,0:T(8,128)(2,1)S(1)}, u32[]{:S(2)}, u32[]{:S(2)}) collective-permute-start(bf16[64,128]{1,0:T(8,128)(2,1)S(1)} %get-tuple-element.51), channel_id=1, source_target_pairs={{0,224},{8,232},{16,240},{24,248},{32,192},{40,200},{48,208},{56,2... | collective-permute-start | bytes 49160 | tf_op jit(solution)/shard_map/ppermute | solution.py:335
  124.1 15.9 %collective-permute-start.3 = (bf16[64,128]{1,0:T(8,128)(2,1)S(1)}, bf16[64,128]{1,0:T(8,128)(2,1)S(1)}, u32[]{:S(2)}, u32[]{:S(2)}) collective-permute-start(bf16[64,128]{1,0:T(8,128)(2,1)S(1)} %get-tuple-element.52), channel_id=1, source_target_pairs={{0,32},{8,40},{16,48},{24,56},{32,0},{40,8},{48,16},{56,24},{64,96... | collective-permute-start | bytes 49160 | tf_op jit(solution)/shard_map/ppermute | solution.py:335
  128.6 15.2 %collective-permute-start.4 = (bf16[64,128]{1,0:T(8,128)(2,1)S(1)}, bf16[64,128]{1,0:T(8,128)(2,1)S(1)}, u32[]{:S(2)}, u32[]{:S(2)}) collective-permute-start(bf16[64,128]{1,0:T(8,128)(2,1)S(1)} %get-tuple-element.53), channel_id=1, source_target_pairs={{0,152},{8,160},{16,168},{24,176},{32,184},{40,128},{48,136},{56,1... | collective-permute-start | bytes 49160 | tf_op jit(solution)/shard_map/ppermute | solution.py:335
  130.6 13.9 %collective-permute-start.5 = (bf16[64,128]{1,0:T(8,128)(2,1)S(1)}, bf16[64,128]{1,0:T(8,128)(2,1)S(1)}, u32[]{:S(2)}, u32[]{:S(2)}) collective-permute-start(bf16[64,128]{1,0:T(8,128)(2,1)S(1)} %get-tuple-element.54), channel_id=1, source_target_pairs={{0,88},{8,96},{16,104},{24,112},{32,120},{40,64},{48,72},{56,80},{... | collective-permute-start | bytes 49160 | tf_op jit(solution)/shard_map/ppermute | solution.py:335
  131.6 18.5 %collective-permute-start.6 = (bf16[64,128]{1,0:T(8,128)(2,1)S(1)}, bf16[64,128]{1,0:T(8,128)(2,1)S(1)}, u32[]{:S(2)}, u32[]{:S(2)}) collective-permute-start(bf16[64,128]{1,0:T(8,128)(2,1)S(1)} %get-tuple-element.55), channel_id=1, source_target_pairs={{0,216},{8,224},{16,232},{24,240},{32,248},{40,192},{48,200},{56,2... | collective-permute-start | bytes 49160 | tf_op jit(solution)/shard_map/ppermute | solution.py:335
  138.6 14.3 %collective-permute-start.7 = (bf16[64,128]{1,0:T(8,128)(2,1)S(1)}, bf16[64,128]{1,0:T(8,128)(2,1)S(1)}, u32[]{:S(2)}, u32[]{:S(2)}) collective-permute-start(bf16[64,128]{1,0:T(8,128)(2,1)S(1)} %get-tuple-element.56), channel_id=1, source_target_pairs={{0,24},{8,32},{16,40},{24,48},{32,56},{40,0},{48,8},{56,16},{64,88... | collective-permute-start | bytes 49160 | tf_op jit(solution)/shard_map/ppermute | solution.py:335
  140.0 15.2 %collective-permute-start.8 = (bf16[64,128]{1,0:T(8,128)(2,1)S(1)}, bf16[64,128]{1,0:T(8,128)(2,1)S(1)}, u32[]{:S(2)}, u32[]{:S(2)}) collective-permute-start(bf16[64,128]{1,0:T(8,128)(2,1)S(1)} %get-tuple-element.57), channel_id=1, source_target_pairs={{0,168},{8,176},{16,184},{24,128},{32,136},{40,144},{48,152},{56,1... | collective-permute-start | bytes 49160 | tf_op jit(solution)/shard_map/ppermute | solution.py:335
  143.8 11.3 %collective-permute-start.9 = (bf16[64,128]{1,0:T(8,128)(2,1)S(1)}, bf16[64,128]{1,0:T(8,128)(2,1)S(1)}, u32[]{:S(2)}, u32[]{:S(2)}) collective-permute-start(bf16[64,128]{1,0:T(8,128)(2,1)S(1)} %get-tuple-element.58), channel_id=1, source_target_pairs={{0,104},{8,112},{16,120},{24,64},{32,72},{40,80},{48,88},{56,96},{... | collective-permute-start | bytes 49160 | tf_op jit(solution)/shard_map/ppermute | solution.py:335
  144.5 15.5 %collective-permute-start.10 = (bf16[64,128]{1,0:T(8,128)(2,1)S(1)}, bf16[64,128]{1,0:T(8,128)(2,1)S(1)}, u32[]{:S(2)}, u32[]{:S(2)}) collective-permute-start(bf16[64,128]{1,0:T(8,128)(2,1)S(1)} %get-tuple-element.59), channel_id=1, source_target_pairs={{0,232},{8,240},{16,248},{24,192},{32,200},{40,208},{48,216},{56,2... | collective-permute-start | bytes 49160 | tf_op jit(solution)/shard_map/ppermute | solution.py:335
  150.1 13.1 %collective-permute-start.11 = (bf16[64,128]{1,0:T(8,128)(2,1)S(1)}, bf16[64,128]{1,0:T(8,128)(2,1)S(1)}, u32[]{:S(2)}, u32[]{:S(2)}) collective-permute-start(bf16[64,128]{1,0:T(8,128)(2,1)S(1)} %get-tuple-element.60), channel_id=1, source_target_pairs={{0,40},{8,48},{16,56},{24,0},{32,8},{40,16},{48,24},{56,32},{64,10... | collective-permute-start | bytes 49160 | tf_op jit(solution)/shard_map/ppermute | solution.py:335
  153.0 11.4 %collective-permute-start.12 = (bf16[64,128]{1,0:T(8,128)(2,1)S(1)}, bf16[64,128]{1,0:T(8,128)(2,1)S(1)}, u32[]{:S(2)}, u32[]{:S(2)}) collective-permute-start(bf16[64,128]{1,0:T(8,128)(2,1)S(1)} %get-tuple-element.61), channel_id=1, source_target_pairs={{0,144},{8,152},{16,160},{24,168},{32,176},{40,184},{48,128},{56,1... | collective-permute-start | bytes 49160 | tf_op jit(solution)/shard_map/ppermute | solution.py:335
  155.2 9.6 %collective-permute-start.13 = (bf16[64,128]{1,0:T(8,128)(2,1)S(1)}, bf16[64,128]{1,0:T(8,128)(2,1)S(1)}, u32[]{:S(2)}, u32[]{:S(2)}) collective-permute-start(bf16[64,128]{1,0:T(8,128)(2,1)S(1)} %get-tuple-element.62), channel_id=1, source_target_pairs={{0,80},{8,88},{16,96},{24,104},{32,112},{40,120},{48,64},{56,72},{... | collective-permute-start | bytes 49160 | tf_op jit(solution)/shard_map/ppermute | solution.py:335
  155.2 15.6 %collective-permute-start.14 = (bf16[64,128]{1,0:T(8,128)(2,1)S(1)}, bf16[64,128]{1,0:T(8,128)(2,1)S(1)}, u32[]{:S(2)}, u32[]{:S(2)}) collective-permute-start(bf16[64,128]{1,0:T(8,128)(2,1)S(1)} %get-tuple-element.63), channel_id=1, source_target_pairs={{0,208},{8,216},{16,224},{24,232},{32,240},{40,248},{48,192},{56,2... | collective-permute-start | bytes 49160 | tf_op jit(solution)/shard_map/ppermute | solution.py:335
  160.0 12.5 %collective-permute-start.15 = (bf16[64,128]{1,0:T(8,128)(2,1)S(1)}, bf16[64,128]{1,0:T(8,128)(2,1)S(1)}, u32[]{:S(2)}, u32[]{:S(2)}) collective-permute-start(bf16[64,128]{1,0:T(8,128)(2,1)S(1)} %get-tuple-element.64), channel_id=1, source_target_pairs={{0,16},{8,24},{16,32},{24,40},{32,48},{40,56},{48,0},{56,8},{64,80... | collective-permute-start | bytes 49160 | tf_op jit(solution)/shard_map/ppermute | solution.py:335
  163.2 11.3 %collective-permute-start.16 = (bf16[64,128]{1,0:T(8,128)(2,1)S(1)}, bf16[64,128]{1,0:T(8,128)(2,1)S(1)}, u32[]{:S(2)}, u32[]{:S(2)}) collective-permute-start(bf16[64,128]{1,0:T(8,128)(2,1)S(1)} %get-tuple-element.65), channel_id=1, source_target_pairs={{0,176},{8,184},{16,128},{24,136},{32,144},{40,152},{48,160},{56,1... | collective-permute-start | bytes 49160 | tf_op jit(solution)/shard_map/ppermute | solution.py:335
  164.3 10.2 %collective-permute-start.17 = (bf16[64,128]{1,0:T(8,128)(2,1)S(1)}, bf16[64,128]{1,0:T(8,128)(2,1)S(1)}, u32[]{:S(2)}, u32[]{:S(2)}) collective-permute-start(bf16[64,128]{1,0:T(8,128)(2,1)S(1)} %get-tuple-element.66), channel_id=1, source_target_pairs={{0,112},{8,120},{16,64},{24,72},{32,80},{40,88},{48,96},{56,104},{... | collective-permute-start | bytes 49160 | tf_op jit(solution)/shard_map/ppermute | solution.py:335
  164.7 13.0 %collective-permute-start.18 = (bf16[64,128]{1,0:T(8,128)(2,1)S(1)}, bf16[64,128]{1,0:T(8,128)(2,1)S(1)}, u32[]{:S(2)}, u32[]{:S(2)}) collective-permute-start(bf16[64,128]{1,0:T(8,128)(2,1)S(1)} %get-tuple-element.67), channel_id=1, source_target_pairs={{0,240},{8,248},{16,192},{24,200},{32,208},{40,216},{48,224},{56,2... | collective-permute-start | bytes 49160 | tf_op jit(solution)/shard_map/ppermute | solution.py:335
  170.8 8.4 %collective-permute-start.19 = (bf16[64,128]{1,0:T(8,128)(2,1)S(1)}, bf16[64,128]{1,0:T(8,128)(2,1)S(1)}, u32[]{:S(2)}, u32[]{:S(2)}) collective-permute-start(bf16[64,128]{1,0:T(8,128)(2,1)S(1)} %get-tuple-element.68), channel_id=1, source_target_pairs={{0,48},{8,56},{16,0},{24,8},{32,16},{40,24},{48,32},{56,40},{64,11... | collective-permute-start | bytes 49160 | tf_op jit(solution)/shard_map/ppermute | solution.py:335
  172.5 8.7 %collective-permute-start.20 = (bf16[64,128]{1,0:T(8,128)(2,1)S(1)}, bf16[64,128]{1,0:T(8,128)(2,1)S(1)}, u32[]{:S(2)}, u32[]{:S(2)}) collective-permute-start(bf16[64,128]{1,0:T(8,128)(2,1)S(1)} %get-tuple-element.69), channel_id=1, source_target_pairs={{0,136},{8,144},{16,152},{24,160},{32,168},{40,176},{48,184},{56,1... | collective-permute-start | bytes 49160 | tf_op jit(solution)/shard_map/ppermute | solution.py:335
  174.5 7.8 %collective-permute-start.21 = (bf16[64,128]{1,0:T(8,128)(2,1)S(1)}, bf16[64,128]{1,0:T(8,128)(2,1)S(1)}, u32[]{:S(2)}, u32[]{:S(2)}) collective-permute-start(bf16[64,128]{1,0:T(8,128)(2,1)S(1)} %get-tuple-element.70), channel_id=1, source_target_pairs={{0,72},{8,80},{16,88},{24,96},{32,104},{40,112},{48,120},{56,64},{... | collective-permute-start | bytes 49160 | tf_op jit(solution)/shard_map/ppermute | solution.py:335
  174.5 11.7 %collective-permute-start.22 = (bf16[64,128]{1,0:T(8,128)(2,1)S(1)}, bf16[64,128]{1,0:T(8,128)(2,1)S(1)}, u32[]{:S(2)}, u32[]{:S(2)}) collective-permute-start(bf16[64,128]{1,0:T(8,128)(2,1)S(1)} %get-tuple-element.71), channel_id=1, source_target_pairs={{0,200},{8,208},{16,216},{24,224},{32,232},{40,240},{48,248},{56,1... | collective-permute-start | bytes 49160 | tf_op jit(solution)/shard_map/ppermute | solution.py:335
  177.8 9.5 %collective-permute-start.23 = (bf16[64,128]{1,0:T(8,128)(2,1)S(1)}, bf16[64,128]{1,0:T(8,128)(2,1)S(1)}, u32[]{:S(2)}, u32[]{:S(2)}) collective-permute-start(bf16[64,128]{1,0:T(8,128)(2,1)S(1)} %get-tuple-element.72), channel_id=1, source_target_pairs={{0,8},{8,16},{16,24},{24,32},{32,40},{40,48},{48,56},{56,0},{64,72... | collective-permute-start | bytes 49160 | tf_op jit(solution)/shard_map/ppermute | solution.py:335
  179.1 9.8 %collective-permute-start.24 = (bf16[64,128]{1,0:T(8,128)(2,1)S(1)}, bf16[64,128]{1,0:T(8,128)(2,1)S(1)}, u32[]{:S(2)}, u32[]{:S(2)}) collective-permute-start(bf16[64,128]{1,0:T(8,128)(2,1)S(1)} %get-tuple-element.73), channel_id=1, source_target_pairs={{0,184},{8,128},{16,136},{24,144},{32,152},{40,160},{48,168},{56,1... | collective-permute-start | bytes 49160 | tf_op jit(solution)/shard_map/ppermute | solution.py:335
  181.2 7.7 %collective-permute-start.25 = (bf16[64,128]{1,0:T(8,128)(2,1)S(1)}, bf16[64,128]{1,0:T(8,128)(2,1)S(1)}, u32[]{:S(2)}, u32[]{:S(2)}) collective-permute-start(bf16[64,128]{1,0:T(8,128)(2,1)S(1)} %get-tuple-element.74), channel_id=1, source_target_pairs={{0,120},{8,64},{16,72},{24,80},{32,88},{40,96},{48,104},{56,112},{... | collective-permute-start | bytes 49160 | tf_op jit(solution)/shard_map/ppermute | solution.py:335
  182.3 9.9 %collective-permute-start.26 = (bf16[64,128]{1,0:T(8,128)(2,1)S(1)}, bf16[64,128]{1,0:T(8,128)(2,1)S(1)}, u32[]{:S(2)}, u32[]{:S(2)}) collective-permute-start(bf16[64,128]{1,0:T(8,128)(2,1)S(1)} %get-tuple-element.75), channel_id=1, source_target_pairs={{0,248},{8,192},{16,200},{24,208},{32,216},{40,224},{48,232},{56,2... | collective-permute-start | bytes 49160 | tf_op jit(solution)/shard_map/ppermute | solution.py:335
  186.2 6.0 %collective-permute-start.27 = (bf16[64,128]{1,0:T(8,128)(2,1)S(1)}, bf16[64,128]{1,0:T(8,128)(2,1)S(1)}, u32[]{:S(2)}, u32[]{:S(2)}) collective-permute-start(bf16[64,128]{1,0:T(8,128)(2,1)S(1)} %get-tuple-element.76), channel_id=1, source_target_pairs={{0,56},{8,0},{16,8},{24,16},{32,24},{40,32},{48,40},{56,48},{64,12... | collective-permute-start | bytes 49160 | tf_op jit(solution)/shard_map/ppermute | solution.py:335
  187.3 5.2 %collective-permute-start.28 = (bf16[64,128]{1,0:T(8,128)(2,1)S(1)}, bf16[64,128]{1,0:T(8,128)(2,1)S(1)}, u32[]{:S(2)}, u32[]{:S(2)}) collective-permute-start(bf16[64,128]{1,0:T(8,128)(2,1)S(1)} %get-tuple-element.77), channel_id=1, source_target_pairs={{0,128},{8,136},{16,144},{24,152},{32,160},{40,168},{48,176},{56,1... | collective-permute-start | bytes 49160 | tf_op jit(solution)/shard_map/ppermute | solution.py:335
  188.9 5.0 %collective-permute-start.29 = (bf16[64,128]{1,0:T(8,128)(2,1)S(1)}, bf16[64,128]{1,0:T(8,128)(2,1)S(1)}, u32[]{:S(2)}, u32[]{:S(2)}) collective-permute-start(bf16[64,128]{1,0:T(8,128)(2,1)S(1)} %get-tuple-element.78), channel_id=1, source_target_pairs={{0,64},{8,72},{16,80},{24,88},{32,96},{40,104},{48,112},{56,120},{... | collective-permute-start | bytes 49160 | tf_op jit(solution)/shard_map/ppermute | solution.py:335
  188.9 4.9 %collective-permute-start.30 = (bf16[64,128]{1,0:T(8,128)(2,1)S(1)}, bf16[64,128]{1,0:T(8,128)(2,1)S(1)}, u32[]{:S(2)}, u32[]{:S(2)}) collective-permute-start(bf16[64,128]{1,0:T(8,128)(2,1)S(1)} %get-tuple-element.79), channel_id=1, source_target_pairs={{0,192},{8,200},{16,208},{24,216},{32,224},{40,232},{48,240},{56,2... | collective-permute-start | bytes 49160 | tf_op jit(solution)/shard_map/ppermute | solution.py:335
  (6 other events, 121.1 us)

commit v10 on v8

--- a/solution.py
+++ b/solution.py
@@ -43,7 +43,7 @@
         return np.block([[table, zero], [zero, table]])
 
     right = np.block([[twice(high), twice(low)], [twice(high), np.zeros((128, 128), high.dtype)]])
-    left = np.concatenate([high, high, low], axis=1)
+    left = np.block([[high, high], [low, np.zeros((BOX, BOX), high.dtype)]])
     lam = 2.0 - 2.0 * np.cos(np.arange(BOX) * (2.0 * math.pi / BOX))
     lam_a = np.repeat(lam.reshape(2, TILES).T, BOX, axis=1)
     under = lam_a[:, None, :] + lam[None, :, None] + np.tile(lam, 2)[None, None, :] + SCREENING
@@ -255,9 +255,10 @@
 
     def along_z(block):
         high, low = split(block)
-        return jnp.dot(
-            left[...], jnp.concatenate([high, low, high], axis=0), preferred_element_type=jnp.float32
+        product = jnp.dot(
+            left[...], jnp.concatenate([high, low], axis=0), preferred_element_type=jnp.float32
         )
+        return product[:BOX] + product[BOX:]
 
     for tile in range(0, TILES, 2):
         block = along_z(jnp.concatenate([field[tile], field[tile + 1]], axis=1))

time: 137 us -> 137 us (level)
  no operation moved by 1% of the time
where the time goes in v10:
time: 137 us; the launch traced here: 136 us
  blocking collectives  97.6 us (71%)
  waiting for transfers between devices  16.9 us (12%)
  starting transfers between devices  11.5 us (8%)
  Pallas kernels  9.21 us (7%)
    all_to_all x1, blocking collectives, body(): lax.all_to_all(picked, ('orb', 'slab'), split_axis=0, concat_axis=0, tile...  39.7 us
    all_to_all x1, blocking collectives, body(): lax.all_to_all(terms, ('orb', 'slab'), split_axis=0, concat_axis=0, tiled...  37.2 us
    all_to_all x1, blocking collectives, body(): lax.all_to_all(pieces, 'orb', split_axis=0, concat_axis=0, tiled=True)  20.7 us
    all_to_all x1, waiting for transfers between devices, body(): lax.all_to_all(pieces, 'orb', split_axis=0, concat_axis=0, tiled=True)  16.9 us
    all_to_all x1, starting transfers between devices, body(): lax.all_to_all(pieces, 'orb', split_axis=0, concat_axis=0, tiled=True)  11.5 us
    pallas_call x1, Pallas kernels, body(): pl.pallas_call(solve_kernel, out_shape=pair_shape, in_specs=[WHOLE_S] + [...  3.42 us
  transfers between devices with their start and end apart: 1, of which 1 were waited for; matrix products, arithmetic and copies ran while one was open for 0% of the time, Pallas kernels for 1%

profile of v10, /device:TPU:2, one launch (start us, length us, event | category | flops | bytes accessed | tf_op | source)
XLA Modules:
  0.0 136.0 jit_solution(3278256004695196753)
XLA Ops:
  0.0 2.0 %spread.1 = bf16[32,9,8,128]{3,2,1,0:T(8,128)(2,1)} custom-call(s32[1,16]{1,0:T(1,128)} %bitcast.8, s32[2,16]{1,0:T(2,128)} %bitcast.7, bf16[8,8,4096]{2,1,0:T(8,128)(2,1)} %orbitals.1), custom_call_target="tpu_custom_call" | custom-call | tf_op jit(solution)/shard_map/spread/pallas_call | solution.py:325
  2.0 11.5 %all-to-all-start = ((bf16[32,9,8,128]{3,2,1,0:T(8,128)(2,1)}), bf16[32,9,8,128]{3,2,1,0:T(8,128)(2,1)S(1)}, u32[]{:S(2)}, u32[]{:S(2)}) async-start(bf16[32,9,8,128]{3,2,1,0:T(8,128)(2,1)} %spread.1), calls=%async_computation | async-start | bytes 1179648 | tf_op jit(solution)/shard_map/all_to_all | solution.py:339
  13.5 0.0 copy-start.4
  13.5 0.0 copy-start.3
  13.5 0.0 copy-start.5
  13.5 0.6 copy-done.4
  14.2 0.0 copy-done.3
  14.2 0.0 copy-done.5
  14.2 0.8 place.1
  15.0 16.9 %all-to-all-done.pieces = bf16[32,9,8,128]{3,2,1,0:T(8,128)(2,1)S(1)} async-done(((bf16[32,9,8,128]{3,2,1,0:T(8,128)(2,1)}), bf16[32,9,8,128]{3,2,1,0:T(8,128)(2,1)S(1)}, u32[]{:S(2)}, u32[]{:S(2)}) %all-to-all-start) | async-done | bytes 589856 | tf_op jit(solution)/shard_map/all_to_all | solution.py:339
  31.9 1.0 pick.1
  33.0 0.0 copy-start
  33.0 0.0 copy-start.1
  33.0 0.0 copy-start.2
  33.0 39.7 %all_to_all.20.boxes = bf16[256,16,128]{2,1,0:T(8,128)(2,1)S(1)} all-to-all(bf16[256,16,128]{2,1,0:T(8,128)(2,1)S(1)} %get-tuple-element.16), channel_id=1, replica_groups=mesh['orb'=32,'slab'=8] {'orb','slab'}, dimensions={0} | all-to-all | bytes 2097152 | tf_op jit(solution)/shard_map/all_to_all | solution.py:354
  72.7 0.0 copy-done
  72.7 0.0 copy-done.1
  72.7 0.0 copy-done.2
  72.7 3.4 %solve.1 = bf16[256,16,128]{2,1,0:T(8,128)(2,1)S(1)} custom-call(s32[1,128]{1,0:T(1,128)S(1)} %get-tuple-element.15.shift, bf16[256,256]{1,0:T(8,128)(2,1)S(1)} %copy-done.1, bf16[128,128]{1,0:T(8,128)(2,1)S(1)} %copy-done.2, f32[32,64,128]{2,1,0:T(8,128)S(1)} %copy-done, bf16[256,16,128]{2,1,0:T(8,128)(2,1)S(1)} %all_to_all.20.boxes), custom_call_target="tpu_custom_call" | custom-call | tf_op jit(solution)/shard_map/solve/pallas_call | solution.py:356
  76.1 37.2 %all_to_all.21.terms = bf16[256,16,128]{2,1,0:T(8,128)(2,1)S(1)} all-to-all(bf16[256,16,128]{2,1,0:T(8,128)(2,1)S(1)} %solve.1), channel_id=1, replica_groups=mesh['orb'=32,'slab'=8] {'orb','slab'}, dimensions={0} | all-to-all | bytes 2097152 | tf_op jit(solution)/shard_map/all_to_all | solution.py:367
  113.3 1.1 sum.1
  114.4 20.7 %all_to_all.22.pieces = bf16[32,64,128]{2,1,0:T(8,128)(2,1)S(1)} all-to-all(bf16[32,64,128]{2,1,0:T(8,128)(2,1)S(1)} %sum.1), channel_id=1, replica_groups=mesh['orb'=32,'slab'=8] {'orb'}, dimensions={0} | all-to-all | bytes 1048576 | tf_op jit(solution)/shard_map/all_to_all | solution.py:374
  135.1 0.9 join.1
Async XLA Ops:
  2.0 30.0 %all-to-all-start = ((bf16[32,9,8,128]{3,2,1,0:T(8,128)(2,1)}), bf16[32,9,8,128]{3,2,1,0:T(8,128)(2,1)S(1)}, u32[]{:S(2)}, u32[]{:S(2)}) async-start(bf16[32,9,8,128]{3,2,1,0:T(8,128)(2,1)} %spread.1), calls=%async_computation | async-start | bytes 1179648 | tf_op jit(solution)/shard_map/all_to_all | solution.py:339
  13.5 0.7 copy-start.4
  13.5 0.7 copy-start.3
  13.5 0.7 copy-start.5
  33.0 39.7 %copy-start = (f32[32,64,128]{2,1,0:T(8,128)S(1)}, f32[32,64,128]{2,1,0:T(8,128)}, u32[]{:S(2)}) copy-start(f32[32,64,128]{2,1,0:T(8,128)} %constant.19.clone.screen) | copy-start | bytes 3145732
  33.0 39.7 %copy-start.1 = (bf16[256,256]{1,0:T(8,128)(2,1)S(1)}, bf16[256,256]{1,0:T(8,128)(2,1)}, u32[]{:S(2)}) copy-start(bf16[256,256]{1,0:T(8,128)(2,1)} %constant.17.clone.right) | copy-start | bytes 393220
  33.0 39.7 %copy-start.2 = (bf16[128,128]{1,0:T(8,128)(2,1)S(1)}, bf16[128,128]{1,0:T(8,128)(2,1)}, u32[]{:S(2)}) copy-start(bf16[128,128]{1,0:T(8,128)(2,1)} %constant.18.clone.left) | copy-start | bytes 98308

commit v11 on v10

--- a/solution.py
+++ b/solution.py
@@ -169,7 +169,7 @@
     choose[...] = chosen(dot_rows(place[...], rows))
 
 
-def pick_kernel(me, place, second, choose, pieces, picked, index, mine, tall):
+def pick_kernel(place, second, choose, pieces, picked, index, mine, tall):
     blocks = []
     for k in range(4):
         block = jnp.sum(pieces[8 * k : 8 * k + 8, 8].astype(jnp.float32), axis=0)
@@ -185,9 +185,10 @@
     index[0:1, :] = known[0:1].astype(jnp.int32)
     index[1:2, :] = known[3:4].astype(jnp.int32)
     lane = lax.broadcasted_iota(jnp.int32, (8, N_DEV), 1)
-    here = jnp.sum(jnp.where(lane == me[0], known, 0.0), axis=1, keepdims=True)
+    me = lax.axis_index("orb") * 8 + lax.axis_index("slab")
+    here = jnp.sum(jnp.where(lane == me, known, 0.0), axis=1, keepdims=True)
     lane = lax.broadcasted_iota(jnp.int32, (1, LANES), 1)
-    mine[...] = jnp.where(lane == 0, here[1:2], here[2:3]).astype(jnp.int32)
+    mine[...] = jnp.where(lane == 0, here[1:2], here[2:3])
     for z in range(0, 8, 2):
         field = [
             pieces[:, z + k].astype(jnp.float32).reshape(N_DEV, LANES).astype(jnp.bfloat16) for k in range(2)
@@ -219,7 +220,8 @@
 
 
 def solve_kernel(shift, right, left, screen, boxes, terms, moved, field, other):
-    shift_x, shift_y = shift[0, 0], shift[0, 1]
+    lane = lax.broadcasted_iota(jnp.int32, (1, LANES), 1)
+    shift_x, shift_y = (jnp.sum(jnp.where(lane == k, shift[...], 0.0)).astype(jnp.int32) for k in range(2))
     full = BOX * BOX
     ahead = (shift_x * BOX + shift_y + full) % full
     back = (full - ahead) % full
@@ -319,7 +321,6 @@
 def body(orbitals, pair_first, second_owner, second_local, pair_shift, pair_count):
     f32, bf16, i32 = jnp.float32, jnp.bfloat16, jnp.int32
     shape = jax.ShapeDtypeStruct
-    me = (lax.axis_index("orb") * 8 + lax.axis_index("slab")).reshape(1)
     rows = ORB_DEV * 8
     pair_shape = shape((N_DEV, 16, LANES), bf16)
     pieces = pl.pallas_call(
@@ -345,17 +346,17 @@
     )(pair_count, second_owner.reshape(4, LANES), second_local.reshape(4, LANES))
     picked, index, mine = pl.pallas_call(
         pick_kernel,
-        out_shape=(pair_shape, shape((2, N_DEV), i32), shape((1, LANES), i32)),
-        in_specs=[WHOLE_S] + [WHOLE_V] * 4,
+        out_shape=(pair_shape, shape((2, N_DEV), i32), shape((1, LANES), f32)),
+        in_specs=[WHOLE_V] * 4,
         out_specs=(WHOLE_V,) * 3,
         scratch_shapes=[pltpu.VMEM((N_DEV * 16 + 16, LANES), f32)],
         compiler_params=PARAMS, name="pick",
-    )(me, place, second, choose, pieces)
+    )(place, second, choose, pieces)
     boxes = lax.all_to_all(picked, ("orb", "slab"), split_axis=0, concat_axis=0, tiled=True)
     right, left, screen = (jnp.asarray(table) for table in tables())
     terms = pl.pallas_call(
         solve_kernel, out_shape=pair_shape,
-        in_specs=[WHOLE_S] + [WHOLE_V] * 4,
+        in_specs=[WHOLE_V] * 5,
         out_specs=WHOLE_V,
         scratch_shapes=[
             pltpu.VMEM((TILES, 8, 8, LANES), f32),

time: 137 us -> 137 us (level)
  no operation moved by 1% of the time
where the time goes in v11:
time: 137 us; the launch traced here: 136 us
  blocking collectives  97.6 us (71%)
  waiting for transfers between devices  17 us (12%)
  starting transfers between devices  11.5 us (8%)
  Pallas kernels  8.76 us (6%)
    all_to_all x1, blocking collectives, body(): lax.all_to_all(picked, ('orb', 'slab'), split_axis=0, concat_axis=0, tile...  39.7 us
    all_to_all x1, blocking collectives, body(): lax.all_to_all(terms, ('orb', 'slab'), split_axis=0, concat_axis=0, tiled...  37.2 us
    all_to_all x1, blocking collectives, body(): lax.all_to_all(pieces, 'orb', split_axis=0, concat_axis=0, tiled=True)  20.7 us
    all_to_all x1, waiting for transfers between devices, body(): lax.all_to_all(pieces, 'orb', split_axis=0, concat_axis=0, tiled=True)  17 us
    all_to_all x1, starting transfers between devices, body(): lax.all_to_all(pieces, 'orb', split_axis=0, concat_axis=0, tiled=True)  11.5 us
    pallas_call x1, Pallas kernels, body(): pl.pallas_call(solve_kernel, out_shape=pair_shape, in_specs=[WHOLE_V] * 5...  2.98 us
  transfers between devices with their start and end apart: 1, of which 1 were waited for; matrix products, arithmetic and copies ran while one was open for 0% of the time, Pallas kernels for 1%

profile of v11, /device:TPU:2, one launch (start us, length us, event | category | flops | bytes accessed | tf_op | source)
XLA Modules:
  0.0 135.6 jit_solution(11817220583933899295)
XLA Ops:
  0.0 2.0 %spread.1 = bf16[32,9,8,128]{3,2,1,0:T(8,128)(2,1)} custom-call(s32[1,16]{1,0:T(1,128)} %bitcast.7, s32[2,16]{1,0:T(2,128)} %bitcast.6, bf16[8,8,4096]{2,1,0:T(8,128)(2,1)} %orbitals.1), custom_call_target="tpu_custom_call" | custom-call | tf_op jit(solution)/shard_map/spread/pallas_call | solution.py:326
  2.0 0.0 copy-start.4
  2.0 11.5 %all-to-all-start = ((bf16[32,9,8,128]{3,2,1,0:T(8,128)(2,1)}), bf16[32,9,8,128]{3,2,1,0:T(8,128)(2,1)S(1)}, u32[]{:S(2)}, u32[]{:S(2)}) async-start(bf16[32,9,8,128]{3,2,1,0:T(8,128)(2,1)} %spread.1), calls=%async_computation | async-start | bytes 1179648 | tf_op jit(solution)/shard_map/all_to_all | solution.py:340
  13.5 0.0 copy-start.3
  13.5 0.0 copy-start.5
  13.5 0.0 copy-done.4
  13.5 0.7 copy-done.3
  14.2 0.0 copy-done.5
  14.2 0.8 place.1
  15.0 17.0 %all-to-all-done.pieces = bf16[32,9,8,128]{3,2,1,0:T(8,128)(2,1)S(1)} async-done(((bf16[32,9,8,128]{3,2,1,0:T(8,128)(2,1)}), bf16[32,9,8,128]{3,2,1,0:T(8,128)(2,1)S(1)}, u32[]{:S(2)}, u32[]{:S(2)}) %all-to-all-start) | async-done | bytes 589856 | tf_op jit(solution)/shard_map/all_to_all | solution.py:340
  32.0 1.0 pick.1
  33.0 0.0 copy-start
  33.0 0.0 copy-start.1
  33.0 0.0 copy-start.2
  33.0 39.7 %all_to_all.20.boxes = bf16[256,16,128]{2,1,0:T(8,128)(2,1)S(1)} all-to-all(bf16[256,16,128]{2,1,0:T(8,128)(2,1)S(1)} %get-tuple-element.16), channel_id=1, replica_groups=mesh['orb'=32,'slab'=8] {'orb','slab'}, dimensions={0} | all-to-all | bytes 2097152 | tf_op jit(solution)/shard_map/all_to_all | solution.py:355
  72.7 0.0 copy-done
  72.7 0.0 copy-done.1
  72.7 0.0 copy-done.2
  72.7 3.0 %solve.1 = bf16[256,16,128]{2,1,0:T(8,128)(2,1)S(1)} custom-call(f32[1,128]{1,0:T(1,128)S(1)} %get-tuple-element.15.shift, bf16[256,256]{1,0:T(8,128)(2,1)S(1)} %copy-done.1, bf16[128,128]{1,0:T(8,128)(2,1)S(1)} %copy-done.2, f32[32,64,128]{2,1,0:T(8,128)S(1)} %copy-done, bf16[256,16,128]{2,1,0:T(8,128)(2,1)S(1)} %all_to_all.20.boxes), custom_call_target="tpu_custom_call" | custom-call | tf_op jit(solution)/shard_map/solve/pallas_call | solution.py:357
  75.7 37.2 %all_to_all.21.terms = bf16[256,16,128]{2,1,0:T(8,128)(2,1)S(1)} all-to-all(bf16[256,16,128]{2,1,0:T(8,128)(2,1)S(1)} %solve.1), channel_id=1, replica_groups=mesh['orb'=32,'slab'=8] {'orb','slab'}, dimensions={0} | all-to-all | bytes 2097152 | tf_op jit(solution)/shard_map/all_to_all | solution.py:368
  112.9 1.1 sum.1
  114.0 20.7 %all_to_all.22.pieces = bf16[32,64,128]{2,1,0:T(8,128)(2,1)S(1)} all-to-all(bf16[32,64,128]{2,1,0:T(8,128)(2,1)S(1)} %sum.1), channel_id=1, replica_groups=mesh['orb'=32,'slab'=8] {'orb'}, dimensions={0} | all-to-all | bytes 1048576 | tf_op jit(solution)/shard_map/all_to_all | solution.py:375
  134.7 0.9 join.1
Async XLA Ops:
  2.0 11.5 %copy-start.4 = (s32[512]{0:T(512)S(1)}, s32[512]{0:T(512)}, u32[]{:S(2)}) copy-start(s32[512]{0:T(512)} %param.12) | copy-start | bytes 6148
  2.0 30.0 %all-to-all-start = ((bf16[32,9,8,128]{3,2,1,0:T(8,128)(2,1)}), bf16[32,9,8,128]{3,2,1,0:T(8,128)(2,1)S(1)}, u32[]{:S(2)}, u32[]{:S(2)}) async-start(bf16[32,9,8,128]{3,2,1,0:T(8,128)(2,1)} %spread.1), calls=%async_computation | async-start | bytes 1179648 | tf_op jit(solution)/shard_map/all_to_all | solution.py:340
  13.5 0.7 copy-start.3
  13.5 0.7 copy-start.5
  33.0 39.7 %copy-start = (f32[32,64,128]{2,1,0:T(8,128)S(1)}, f32[32,64,128]{2,1,0:T(8,128)}, u32[]{:S(2)}) copy-start(f32[32,64,128]{2,1,0:T(8,128)} %constant.8.clone.screen) | copy-start | bytes 3145732
  33.0 39.7 %copy-start.1 = (bf16[256,256]{1,0:T(8,128)(2,1)S(1)}, bf16[256,256]{1,0:T(8,128)(2,1)}, u32[]{:S(2)}) copy-start(bf16[256,256]{1,0:T(8,128)(2,1)} %constant.6.clone.right) | copy-start | bytes 393220
  33.0 39.7 %copy-start.2 = (bf16[128,128]{1,0:T(8,128)(2,1)S(1)}, bf16[128,128]{1,0:T(8,128)(2,1)}, u32[]{:S(2)}) copy-start(bf16[128,128]{1,0:T(8,128)(2,1)} %constant.7.clone.left) | copy-start | bytes 98308

commit v12 on v11

--- a/solution.py
+++ b/solution.py
@@ -311,11 +311,10 @@
 
 
 def join_kernel(pieces, result):
-    for pair in range(ORB_DEV // 2):
-        tiles = [pieces[tile, 16 * pair : 16 * pair + 16, :].astype(jnp.float32) for tile in range(TILES)]
-        for side in range(2):
-            rows = [tile[8 * side : 8 * side + 8] for tile in tiles]
-            result[2 * pair + side] = jnp.concatenate(rows, axis=1).astype(jnp.bfloat16)
+    for orbital in range(ORB_DEV):
+        rows = slice(8 * orbital, 8 * orbital + 8)
+        for tile in range(TILES):
+            result[orbital, :, tile * LANES : (tile + 1) * LANES] = pieces[tile, rows, :]
 
 
 def body(orbitals, pair_first, second_owner, second_local, pair_shift, pair_count):

time: 137 us -> 137 us (level)
  no operation moved by 1% of the time
where the time goes in v12:
time: 137 us; the launch traced here: 136 us
  blocking collectives  97.6 us (71%)
  waiting for transfers between devices  17 us (12%)
  starting transfers between devices  11.5 us (8%)
  Pallas kernels  8.79 us (6%)
    all_to_all x1, blocking collectives, body(): lax.all_to_all(picked, ('orb', 'slab'), split_axis=0, concat_axis=0, tile...  39.7 us
    all_to_all x1, blocking collectives, body(): lax.all_to_all(terms, ('orb', 'slab'), split_axis=0, concat_axis=0, tiled...  37.2 us
    all_to_all x1, blocking collectives, body(): lax.all_to_all(pieces, 'orb', split_axis=0, concat_axis=0, tiled=True)  20.7 us
    all_to_all x1, waiting for transfers between devices, body(): lax.all_to_all(pieces, 'orb', split_axis=0, concat_axis=0, tiled=True)  17 us
    all_to_all x1, starting transfers between devices, body(): lax.all_to_all(pieces, 'orb', split_axis=0, concat_axis=0, tiled=True)  11.5 us
    pallas_call x1, Pallas kernels, body(): pl.pallas_call(solve_kernel, out_shape=pair_shape, in_specs=[WHOLE_V] * 5...  2.98 us
  transfers between devices with their start and end apart: 1, of which 1 were waited for; matrix products, arithmetic and copies ran while one was open for 0% of the time, Pallas kernels for 1%

profile of v12, /device:TPU:2, one launch (start us, length us, event | category | flops | bytes accessed | tf_op | source)
XLA Modules:
  0.0 135.6 jit_solution(3225399017131595510)
XLA Ops:
  0.0 2.0 %spread.1 = bf16[32,9,8,128]{3,2,1,0:T(8,128)(2,1)} custom-call(s32[1,16]{1,0:T(1,128)} %bitcast.7, s32[2,16]{1,0:T(2,128)} %bitcast.6, bf16[8,8,4096]{2,1,0:T(8,128)(2,1)} %orbitals.1), custom_call_target="tpu_custom_call" | custom-call | tf_op jit(solution)/shard_map/spread/pallas_call | solution.py:325
  2.0 0.0 copy-start.4
  2.0 11.5 %all-to-all-start = ((bf16[32,9,8,128]{3,2,1,0:T(8,128)(2,1)}), bf16[32,9,8,128]{3,2,1,0:T(8,128)(2,1)S(1)}, u32[]{:S(2)}, u32[]{:S(2)}) async-start(bf16[32,9,8,128]{3,2,1,0:T(8,128)(2,1)} %spread.1), calls=%async_computation | async-start | bytes 1179648 | tf_op jit(solution)/shard_map/all_to_all | solution.py:339
  13.5 0.0 copy-start.3
  13.5 0.0 copy-start.5
  13.5 0.0 copy-done.4
  13.5 0.7 copy-done.3
  14.2 0.0 copy-done.5
  14.2 0.8 place.1
  15.0 17.0 %all-to-all-done.pieces = bf16[32,9,8,128]{3,2,1,0:T(8,128)(2,1)S(1)} async-done(((bf16[32,9,8,128]{3,2,1,0:T(8,128)(2,1)}), bf16[32,9,8,128]{3,2,1,0:T(8,128)(2,1)S(1)}, u32[]{:S(2)}, u32[]{:S(2)}) %all-to-all-start) | async-done | bytes 589856 | tf_op jit(solution)/shard_map/all_to_all | solution.py:339
  32.0 1.0 pick.1
  33.0 0.0 copy-start
  33.0 0.0 copy-start.1
  33.0 0.0 copy-start.2
  33.0 39.7 %all_to_all.20.boxes = bf16[256,16,128]{2,1,0:T(8,128)(2,1)S(1)} all-to-all(bf16[256,16,128]{2,1,0:T(8,128)(2,1)S(1)} %get-tuple-element.16), channel_id=1, replica_groups=mesh['orb'=32,'slab'=8] {'orb','slab'}, dimensions={0} | all-to-all | bytes 2097152 | tf_op jit(solution)/shard_map/all_to_all | solution.py:354
  72.7 0.0 copy-done
  72.7 0.0 copy-done.1
  72.7 0.0 copy-done.2
  72.7 3.0 %solve.1 = bf16[256,16,128]{2,1,0:T(8,128)(2,1)S(1)} custom-call(f32[1,128]{1,0:T(1,128)S(1)} %get-tuple-element.15.shift, bf16[256,256]{1,0:T(8,128)(2,1)S(1)} %copy-done.1, bf16[128,128]{1,0:T(8,128)(2,1)S(1)} %copy-done.2, f32[32,64,128]{2,1,0:T(8,128)S(1)} %copy-done, bf16[256,16,128]{2,1,0:T(8,128)(2,1)S(1)} %all_to_all.20.boxes), custom_call_target="tpu_custom_call" | custom-call | tf_op jit(solution)/shard_map/solve/pallas_call | solution.py:356
  75.7 37.2 %all_to_all.21.terms = bf16[256,16,128]{2,1,0:T(8,128)(2,1)S(1)} all-to-all(bf16[256,16,128]{2,1,0:T(8,128)(2,1)S(1)} %solve.1), channel_id=1, replica_groups=mesh['orb'=32,'slab'=8] {'orb','slab'}, dimensions={0} | all-to-all | bytes 2097152 | tf_op jit(solution)/shard_map/all_to_all | solution.py:367
  112.9 1.1 sum.1
  114.0 20.7 %all_to_all.22.pieces = bf16[32,64,128]{2,1,0:T(8,128)(2,1)S(1)} all-to-all(bf16[32,64,128]{2,1,0:T(8,128)(2,1)S(1)} %sum.1), channel_id=1, replica_groups=mesh['orb'=32,'slab'=8] {'orb'}, dimensions={0} | all-to-all | bytes 1048576 | tf_op jit(solution)/shard_map/all_to_all | solution.py:374
  134.7 0.9 join.1
Async XLA Ops:
  2.0 11.5 %copy-start.4 = (s32[512]{0:T(512)S(1)}, s32[512]{0:T(512)}, u32[]{:S(2)}) copy-start(s32[512]{0:T(512)} %param.12) | copy-start | bytes 6148
  2.0 30.0 %all-to-all-start = ((bf16[32,9,8,128]{3,2,1,0:T(8,128)(2,1)}), bf16[32,9,8,128]{3,2,1,0:T(8,128)(2,1)S(1)}, u32[]{:S(2)}, u32[]{:S(2)}) async-start(bf16[32,9,8,128]{3,2,1,0:T(8,128)(2,1)} %spread.1), calls=%async_computation | async-start | bytes 1179648 | tf_op jit(solution)/shard_map/all_to_all | solution.py:339
  13.5 0.7 copy-start.3
  13.5 0.7 copy-start.5
  33.0 39.7 %copy-start = (f32[32,64,128]{2,1,0:T(8,128)S(1)}, f32[32,64,128]{2,1,0:T(8,128)}, u32[]{:S(2)}) copy-start(f32[32,64,128]{2,1,0:T(8,128)} %constant.8.clone.screen) | copy-start | bytes 3145732
  33.0 39.7 %copy-start.1 = (bf16[256,256]{1,0:T(8,128)(2,1)S(1)}, bf16[256,256]{1,0:T(8,128)(2,1)}, u32[]{:S(2)}) copy-start(bf16[256,256]{1,0:T(8,128)(2,1)} %constant.6.clone.right) | copy-start | bytes 393220
  33.0 39.7 %copy-start.2 = (bf16[128,128]{1,0:T(8,128)(2,1)S(1)}, bf16[128,128]{1,0:T(8,128)(2,1)}, u32[]{:S(2)}) copy-start(bf16[128,128]{1,0:T(8,128)(2,1)} %constant.7.clone.left) | copy-start | bytes 98308

commit v13 on v11

--- a/solution.py
+++ b/solution.py
@@ -68,6 +68,10 @@
     for k in range(m):
         if k == 0 or 4 * k == n:
             turned = odd[k]
+        elif 8 * k == n:
+            turned = (odd[k] + odd[m - k]) * math.sqrt(0.5)
+        elif 8 * k == 3 * n:
+            turned = (odd[m - k] - odd[k]) * math.sqrt(0.5)
         else:
             angle = 2.0 * math.pi * k / n
             turned = odd[k] * math.cos(angle) + odd[m - k] * math.sin(angle)
@@ -76,28 +80,18 @@
     return out
 
 
-def twist(parts, first):
-    out = []
-    for k in range(TILES):
-        mirror = parts[(TILES - k) % TILES]
-        angle = 2.0 * math.pi * k / BOX
-        if k == 0 or 2 * k == TILES:
-            out.append(parts[k])
-        else:
-            out.append(jnp.where(first, parts[k], parts[k] * math.cos(angle) + mirror * math.sin(angle)))
-    return out
-
-
-def untwist(parts, first):
-    out = []
-    for k in range(TILES):
-        mirror = parts[(TILES - k) % TILES]
-        angle = 2.0 * math.pi * k / BOX
-        back = 2.0 * math.pi * ((TILES - k) % TILES) / BOX
-        if k == 0 or 2 * k == TILES:
-            out.append(parts[k])
-        else:
-            out.append(jnp.where(first, parts[k], parts[k] * math.cos(angle) + mirror * math.sin(back)))
+def turns(first):
+    angles = [2.0 * math.pi * k / BOX for k in range(TILES // 2 + 1)]
+    return [(jnp.where(first, 1.0, math.cos(b)), jnp.where(first, 0.0, math.sin(b))) for b in angles], first
+
+
+def twist(parts, known):
+    turn, first = known
+    out = list(parts)
+    for k in range(1, TILES // 2):
+        one, two = parts[k], parts[TILES - k]
+        out[k] = one * turn[k][0] + two * turn[k][1]
+        out[TILES - k] = jnp.where(first, two, one * turn[k][1] - two * turn[k][0])
     return out
 
 
@@ -227,6 +221,7 @@
     back = (full - ahead) % full
     early = lax.broadcasted_iota(jnp.int32, (8, LANES), 1) < BOX
     sign = jnp.where(early, 1.0, -1.0)
+    known = turns(early)
 
     def first_tile(tile):
         return boxes[pl.ds(tile * 8, 8), :8, :].astype(jnp.float32)
@@ -251,7 +246,7 @@
             field[start + k] = block[k]
 
     for row in range(0, BOX, 8):
-        parts = twist(fast_hartley([field[k, row : row + 8, :] for k in range(TILES)]), early)
+        parts = twist(fast_hartley([field[k, row : row + 8, :] for k in range(TILES)]), known)
         for k in range(TILES):
             field[k, row : row + 8, :] = sign * parts[k] + pltpu.roll(parts[k], BOX, 1)
 
@@ -272,7 +267,7 @@
     for row in range(0, BOX, 8):
         parts = [field[k, row : row + 8, :] for k in range(TILES)]
         parts = [sign * part + pltpu.roll(part, BOX, 1) for part in parts]
-        parts = fast_hartley(untwist(parts, early))
+        parts = fast_hartley(twist(parts, known))
         for k in range(TILES):
             field[k, row : row + 8, :] = parts[k]
 

time: 137 us -> 137 us (level)
  no operation moved by 1% of the time
where the time goes in v13:
time: 137 us; the launch traced here: 136 us
  blocking collectives  97.6 us (71%)
  waiting for transfers between devices  17 us (12%)
  starting transfers between devices  11.5 us (8%)
  Pallas kernels  8.72 us (6%)
    all_to_all x1, blocking collectives, body(): lax.all_to_all(picked, ('orb', 'slab'), split_axis=0, concat_axis=0, tile...  39.7 us
    all_to_all x1, blocking collectives, body(): lax.all_to_all(terms, ('orb', 'slab'), split_axis=0, concat_axis=0, tiled...  37.2 us
    all_to_all x1, blocking collectives, body(): lax.all_to_all(pieces, 'orb', split_axis=0, concat_axis=0, tiled=True)  20.7 us
    all_to_all x1, waiting for transfers between devices, body(): lax.all_to_all(pieces, 'orb', split_axis=0, concat_axis=0, tiled=True)  17 us
    all_to_all x1, starting transfers between devices, body(): lax.all_to_all(pieces, 'orb', split_axis=0, concat_axis=0, tiled=True)  11.5 us
    pallas_call x1, Pallas kernels, body(): pl.pallas_call(solve_kernel, out_shape=pair_shape, in_specs=[WHOLE_V] * 5...  2.93 us
  transfers between devices with their start and end apart: 1, of which 1 were waited for; matrix products, arithmetic and copies ran while one was open for 0% of the time, Pallas kernels for 1%

profile of v13, /device:TPU:2, one launch (start us, length us, event | category | flops | bytes accessed | tf_op | source)
XLA Modules:
  0.0 135.5 jit_solution(4392544972857551181)
XLA Ops:
  0.0 2.0 %spread.1 = bf16[32,9,8,128]{3,2,1,0:T(8,128)(2,1)} custom-call(s32[1,16]{1,0:T(1,128)} %bitcast.7, s32[2,16]{1,0:T(2,128)} %bitcast.6, bf16[8,8,4096]{2,1,0:T(8,128)(2,1)} %orbitals.1), custom_call_target="tpu_custom_call" | custom-call | tf_op jit(solution)/shard_map/spread/pallas_call | solution.py:321
  2.0 0.0 copy-start.4
  2.0 11.5 %all-to-all-start = ((bf16[32,9,8,128]{3,2,1,0:T(8,128)(2,1)}), bf16[32,9,8,128]{3,2,1,0:T(8,128)(2,1)S(1)}, u32[]{:S(2)}, u32[]{:S(2)}) async-start(bf16[32,9,8,128]{3,2,1,0:T(8,128)(2,1)} %spread.1), calls=%async_computation | async-start | bytes 1179648 | tf_op jit(solution)/shard_map/all_to_all | solution.py:335
  13.5 0.0 copy-start.3
  13.5 0.0 copy-start.5
  13.5 0.0 copy-done.4
  13.5 0.7 copy-done.3
  14.2 0.0 copy-done.5
  14.2 0.8 place.1
  15.0 17.0 %all-to-all-done.pieces = bf16[32,9,8,128]{3,2,1,0:T(8,128)(2,1)S(1)} async-done(((bf16[32,9,8,128]{3,2,1,0:T(8,128)(2,1)}), bf16[32,9,8,128]{3,2,1,0:T(8,128)(2,1)S(1)}, u32[]{:S(2)}, u32[]{:S(2)}) %all-to-all-start) | async-done | bytes 589856 | tf_op jit(solution)/shard_map/all_to_all | solution.py:335
  32.0 1.0 pick.1
  33.0 0.0 copy-start
  33.0 0.0 copy-start.1
  33.0 0.0 copy-start.2
  33.0 39.7 %all_to_all.20.boxes = bf16[256,16,128]{2,1,0:T(8,128)(2,1)S(1)} all-to-all(bf16[256,16,128]{2,1,0:T(8,128)(2,1)S(1)} %get-tuple-element.16), channel_id=1, replica_groups=mesh['orb'=32,'slab'=8] {'orb','slab'}, dimensions={0} | all-to-all | bytes 2097152 | tf_op jit(solution)/shard_map/all_to_all | solution.py:350
  72.7 0.0 copy-done
  72.7 0.0 copy-done.1
  72.7 0.0 copy-done.2
  72.7 2.9 %solve.1 = bf16[256,16,128]{2,1,0:T(8,128)(2,1)S(1)} custom-call(f32[1,128]{1,0:T(1,128)S(1)} %get-tuple-element.15.shift, bf16[256,256]{1,0:T(8,128)(2,1)S(1)} %copy-done.1, bf16[128,128]{1,0:T(8,128)(2,1)S(1)} %copy-done.2, f32[32,64,128]{2,1,0:T(8,128)S(1)} %copy-done, bf16[256,16,128]{2,1,0:T(8,128)(2,1)S(1)} %all_to_all.20.boxes), custom_call_target="tpu_custom_call" | custom-call | tf_op jit(solution)/shard_map/solve/pallas_call | solution.py:352
  75.6 37.2 %all_to_all.21.terms = bf16[256,16,128]{2,1,0:T(8,128)(2,1)S(1)} all-to-all(bf16[256,16,128]{2,1,0:T(8,128)(2,1)S(1)} %solve.1), channel_id=1, replica_groups=mesh['orb'=32,'slab'=8] {'orb','slab'}, dimensions={0} | all-to-all | bytes 2097152 | tf_op jit(solution)/shard_map/all_to_all | solution.py:363
  112.8 1.1 sum.1
  114.0 20.7 %all_to_all.22.pieces = bf16[32,64,128]{2,1,0:T(8,128)(2,1)S(1)} all-to-all(bf16[32,64,128]{2,1,0:T(8,128)(2,1)S(1)} %sum.1), channel_id=1, replica_groups=mesh['orb'=32,'slab'=8] {'orb'}, dimensions={0} | all-to-all | bytes 1048576 | tf_op jit(solution)/shard_map/all_to_all | solution.py:370
  134.7 0.9 join.1
Async XLA Ops:
  2.0 11.5 %copy-start.4 = (s32[512]{0:T(512)S(1)}, s32[512]{0:T(512)}, u32[]{:S(2)}) copy-start(s32[512]{0:T(512)} %param.12) | copy-start | bytes 6148
  2.0 30.0 %all-to-all-start = ((bf16[32,9,8,128]{3,2,1,0:T(8,128)(2,1)}), bf16[32,9,8,128]{3,2,1,0:T(8,128)(2,1)S(1)}, u32[]{:S(2)}, u32[]{:S(2)}) async-start(bf16[32,9,8,128]{3,2,1,0:T(8,128)(2,1)} %spread.1), calls=%async_computation | async-start | bytes 1179648 | tf_op jit(solution)/shard_map/all_to_all | solution.py:335
  13.5 0.7 copy-start.3
  13.5 0.7 copy-start.5
  33.0 39.7 %copy-start = (f32[32,64,128]{2,1,0:T(8,128)S(1)}, f32[32,64,128]{2,1,0:T(8,128)}, u32[]{:S(2)}) copy-start(f32[32,64,128]{2,1,0:T(8,128)} %constant.8.clone.screen) | copy-start | bytes 3145732
  33.0 39.7 %copy-start.1 = (bf16[256,256]{1,0:T(8,128)(2,1)S(1)}, bf16[256,256]{1,0:T(8,128)(2,1)}, u32[]{:S(2)}) copy-start(bf16[256,256]{1,0:T(8,128)(2,1)} %constant.6.clone.right) | copy-start | bytes 393220
  33.0 39.7 %copy-start.2 = (bf16[128,128]{1,0:T(8,128)(2,1)S(1)}, bf16[128,128]{1,0:T(8,128)(2,1)}, u32[]{:S(2)}) copy-start(bf16[128,128]{1,0:T(8,128)(2,1)} %constant.7.clone.left) | copy-start | bytes 98308

commit v14 on v13

--- a/solution.py
+++ b/solution.py
@@ -276,13 +276,13 @@
         potential = along_y(block).reshape(4, 8, 8, LANES)
         for k in range(4):
             other[start + k] = potential[k] * first_tile(start + k)
-            moved[start + k] = potential[k] * moved[start + k]
+            own = potential[k] * moved[start + k]
+            terms[(start + k) * 8 : (start + k + 1) * 8, :8, :] = own.astype(jnp.bfloat16)
 
     for start in range(0, TILES, 4):
         carried = shifted(lambda tile: other[tile], start, 4, back, -shift_x, -shift_y)
         for k in range(4):
-            both = jnp.concatenate([moved[start + k], carried[k]], axis=1)
-            terms[(start + k) * 8 : (start + k + 1) * 8] = both.astype(jnp.bfloat16)
+            terms[(start + k) * 8 : (start + k + 1) * 8, 8:, :] = carried[k].astype(jnp.bfloat16)
 
 
 def sum_kernel(index, terms, pieces, tall, summed):

time: 137 us -> 137 us (level)
  no operation moved by 1% of the time
where the time goes in v14:
time: 137 us; the launch traced here: 136 us
  blocking collectives  97.6 us (71%)
  waiting for transfers between devices  17 us (12%)
  starting transfers between devices  11.5 us (8%)
  Pallas kernels  8.75 us (6%)
    all_to_all x1, blocking collectives, body(): lax.all_to_all(picked, ('orb', 'slab'), split_axis=0, concat_axis=0, tile...  39.7 us
    all_to_all x1, blocking collectives, body(): lax.all_to_all(terms, ('orb', 'slab'), split_axis=0, concat_axis=0, tiled...  37.2 us
    all_to_all x1, blocking collectives, body(): lax.all_to_all(pieces, 'orb', split_axis=0, concat_axis=0, tiled=True)  20.7 us
    all_to_all x1, waiting for transfers between devices, body(): lax.all_to_all(pieces, 'orb', split_axis=0, concat_axis=0, tiled=True)  17 us
    all_to_all x1, starting transfers between devices, body(): lax.all_to_all(pieces, 'orb', split_axis=0, concat_axis=0, tiled=True)  11.5 us
    pallas_call x1, Pallas kernels, body(): pl.pallas_call(solve_kernel, out_shape=pair_shape, in_specs=[WHOLE_V] * 5...  2.97 us
  transfers between devices with their start and end apart: 1, of which 1 were waited for; matrix products, arithmetic and copies ran while one was open for 0% of the time, Pallas kernels for 1%

profile of v14, /device:TPU:2, one launch (start us, length us, event | category | flops | bytes accessed | tf_op | source)
XLA Modules:
  0.0 135.6 jit_solution(10277686254311829268)
XLA Ops:
  0.0 2.0 %spread.1 = bf16[32,9,8,128]{3,2,1,0:T(8,128)(2,1)} custom-call(s32[1,16]{1,0:T(1,128)} %bitcast.7, s32[2,16]{1,0:T(2,128)} %bitcast.6, bf16[8,8,4096]{2,1,0:T(8,128)(2,1)} %orbitals.1), custom_call_target="tpu_custom_call" | custom-call | tf_op jit(solution)/shard_map/spread/pallas_call | solution.py:321
  2.0 0.0 copy-start.4
  2.0 11.5 %all-to-all-start = ((bf16[32,9,8,128]{3,2,1,0:T(8,128)(2,1)}), bf16[32,9,8,128]{3,2,1,0:T(8,128)(2,1)S(1)}, u32[]{:S(2)}, u32[]{:S(2)}) async-start(bf16[32,9,8,128]{3,2,1,0:T(8,128)(2,1)} %spread.1), calls=%async_computation | async-start | bytes 1179648 | tf_op jit(solution)/shard_map/all_to_all | solution.py:335
  13.5 0.0 copy-start.3
  13.5 0.0 copy-start.5
  13.5 0.0 copy-done.4
  13.5 0.7 copy-done.3
  14.2 0.0 copy-done.5
  14.2 0.8 place.1
  15.0 17.0 %all-to-all-done.pieces = bf16[32,9,8,128]{3,2,1,0:T(8,128)(2,1)S(1)} async-done(((bf16[32,9,8,128]{3,2,1,0:T(8,128)(2,1)}), bf16[32,9,8,128]{3,2,1,0:T(8,128)(2,1)S(1)}, u32[]{:S(2)}, u32[]{:S(2)}) %all-to-all-start) | async-done | bytes 589856 | tf_op jit(solution)/shard_map/all_to_all | solution.py:335
  32.0 1.0 pick.1
  33.0 0.0 copy-start
  33.0 0.0 copy-start.1
  33.0 0.0 copy-start.2
  33.0 39.7 %all_to_all.20.boxes = bf16[256,16,128]{2,1,0:T(8,128)(2,1)S(1)} all-to-all(bf16[256,16,128]{2,1,0:T(8,128)(2,1)S(1)} %get-tuple-element.16), channel_id=1, replica_groups=mesh['orb'=32,'slab'=8] {'orb','slab'}, dimensions={0} | all-to-all | bytes 2097152 | tf_op jit(solution)/shard_map/all_to_all | solution.py:350
  72.7 0.0 copy-done
  72.7 0.0 copy-done.1
  72.7 0.0 copy-done.2
  72.7 3.0 %solve.1 = bf16[256,16,128]{2,1,0:T(8,128)(2,1)S(1)} custom-call(f32[1,128]{1,0:T(1,128)S(1)} %get-tuple-element.15.shift, bf16[256,256]{1,0:T(8,128)(2,1)S(1)} %copy-done.1, bf16[128,128]{1,0:T(8,128)(2,1)S(1)} %copy-done.2, f32[32,64,128]{2,1,0:T(8,128)S(1)} %copy-done, bf16[256,16,128]{2,1,0:T(8,128)(2,1)S(1)} %all_to_all.20.boxes), custom_call_target="tpu_custom_call" | custom-call | tf_op jit(solution)/shard_map/solve/pallas_call | solution.py:352
  75.7 37.2 %all_to_all.21.terms = bf16[256,16,128]{2,1,0:T(8,128)(2,1)S(1)} all-to-all(bf16[256,16,128]{2,1,0:T(8,128)(2,1)S(1)} %solve.1), channel_id=1, replica_groups=mesh['orb'=32,'slab'=8] {'orb','slab'}, dimensions={0} | all-to-all | bytes 2097152 | tf_op jit(solution)/shard_map/all_to_all | solution.py:363
  112.8 1.1 sum.1
  114.0 20.7 %all_to_all.22.pieces = bf16[32,64,128]{2,1,0:T(8,128)(2,1)S(1)} all-to-all(bf16[32,64,128]{2,1,0:T(8,128)(2,1)S(1)} %sum.1), channel_id=1, replica_groups=mesh['orb'=32,'slab'=8] {'orb'}, dimensions={0} | all-to-all | bytes 1048576 | tf_op jit(solution)/shard_map/all_to_all | solution.py:370
  134.7 0.9 join.1
Async XLA Ops:
  2.0 11.5 %copy-start.4 = (s32[512]{0:T(512)S(1)}, s32[512]{0:T(512)}, u32[]{:S(2)}) copy-start(s32[512]{0:T(512)} %param.12) | copy-start | bytes 6148
  2.0 30.0 %all-to-all-start = ((bf16[32,9,8,128]{3,2,1,0:T(8,128)(2,1)}), bf16[32,9,8,128]{3,2,1,0:T(8,128)(2,1)S(1)}, u32[]{:S(2)}, u32[]{:S(2)}) async-start(bf16[32,9,8,128]{3,2,1,0:T(8,128)(2,1)} %spread.1), calls=%async_computation | async-start | bytes 1179648 | tf_op jit(solution)/shard_map/all_to_all | solution.py:335
  13.5 0.7 copy-start.3
  13.5 0.7 copy-start.5
  33.0 39.7 %copy-start = (f32[32,64,128]{2,1,0:T(8,128)S(1)}, f32[32,64,128]{2,1,0:T(8,128)}, u32[]{:S(2)}) copy-start(f32[32,64,128]{2,1,0:T(8,128)} %constant.8.clone.screen) | copy-start | bytes 3145732
  33.0 39.7 %copy-start.1 = (bf16[256,256]{1,0:T(8,128)(2,1)S(1)}, bf16[256,256]{1,0:T(8,128)(2,1)}, u32[]{:S(2)}) copy-start(bf16[256,256]{1,0:T(8,128)(2,1)} %constant.6.clone.right) | copy-start | bytes 393220
  33.0 39.7 %copy-start.2 = (bf16[128,128]{1,0:T(8,128)(2,1)S(1)}, bf16[128,128]{1,0:T(8,128)(2,1)}, u32[]{:S(2)}) copy-start(bf16[128,128]{1,0:T(8,128)(2,1)} %constant.7.clone.left) | copy-start | bytes 98308
